TPU v7x, 32 devices: a whole 2x2x4 slice. The times are simulated.
32 devices in a mesh: batch: 8 (over z, x), head: 4 (over y, core).
Axes of the slice: x: 2, y: 2, z: 4, core: 2. Of those that a mesh axis runs over, the one named last changes fastest.
Arguments:
- hidden_in: bfloat16 [8, 2048, 1024], P('batch', None, 'head'), may hold values from -6 to 6
- cotangent: bfloat16 [8, 2048, 1024], P('batch', None, 'head'), may hold values from -6 to 6
- doc_ids: int32 [8, 2048], P('batch'), may hold values from 0 to 5, never falling along the last dimension, each value on 1 to 1024 neighbouring positions
- lengths: int32 [8], P('batch'), may hold values from 1536 to 2048
- w_query: bfloat16 [1024, 1024], P(None, 'head'), may hold values from -0.1875 to 0.1875
- w_key: bfloat16 [1024, 1024], P(None, 'head'), may hold values from -0.1875 to 0.1875
- w_value: bfloat16 [1024, 1024], P(None, 'head'), may hold values from -0.1875 to 0.1875
- w_out: bfloat16 [1024, 1024], P('head'), may hold values from -0.1875 to 0.1875
- w_up: bfloat16 [1024, 4096], P(None, 'head'), may hold values from -0.1875 to 0.1875
- w_gate: bfloat16 [1024, 4096], P(None, 'head'), may hold values from -0.1875 to 0.1875
- w_down: bfloat16 [4096, 1024], P('head'), may hold values from -0.09375 to 0.09375
- scale_qk: float32 [1024], P('head'), may hold values from 0.7 to 1.5
- scale_up: float32 [4096], P('head'), may hold values from 0.25 to 1.75
- scale_gate: float32 [4096], P('head'), may hold values from 0.5 to 2
- alpha_attn: float32 [1024], replicated, may hold values from 0.05 to 0.6
- alpha_ffn: float32 [1024], replicated, may hold values from 0.15 to 0.6
Outputs:
- hidden_out: bfloat16 [8, 2048, 1024], P('batch', None, 'head')
- grad_hidden: float32 [8, 2048, 1024], P('batch', None, 'head')
- grad_query: float32 [1024, 1024], P(None, 'head')
- grad_key: float32 [1024, 1024], P(None, 'head')
- grad_value: float32 [1024, 1024], P(None, 'head')
- grad_out: float32 [1024, 1024], P('head')
- grad_up: float32 [1024, 4096], P(None, 'head')
- grad_gate: float32 [1024, 4096], P(None, 'head')
- grad_down: float32 [4096, 1024], P('head')
- grad_scale_qk: float32 [1024], P('head')
- grad_scale_up: float32 [4096], P('head')
- grad_scale_gate: float32 [4096], P('head')
- grad_alpha_attn: float32 [1024], P('head')
- grad_alpha_ffn: float32 [1024], P('head')
Inputs may be any that keep to these rules, and one draw needn't show every extreme that they name: `doc_ids`: document number of each slot: never falls along a row, each document holds 1 to 1024 slots, one exactly 1024, all 6 present. `lengths`: slots at or past the length are padding.
All inputs are finite; a program needn't handle non-finite values.
Results may differ from a plain program's by a relative error of at most 0.025.
Values may be sent and summed in bfloat16 or wider, within the bound.
No kernel may reach another device: no remote copies, remote signals or barrier semaphores. Data moves between devices by JAX's collectives and lax.ppermute only.
A program may use at most 256 MiB of HBM per device.

v0:
```python
import functools
import math

import jax
import jax.numpy as jnp
from jax import lax
from jax.experimental import pallas as pl
from jax.experimental.pallas import tpu as pltpu
from jax.sharding import PartitionSpec as P

HD = 64
HALF = HD // 2
VALUE_ROWS = 80
EPSILON = 1e-06
BLOCK = 256
QUERIES = 512
KEYS = 512
CHUNKS = 2
F32 = jnp.float32
BF16 = jnp.bfloat16
MIB = 1024 * 1024


def dot(left, right, left_dim=1, right_dim=0):
    return lax.dot_general(
        left, right, (((left_dim,), (right_dim,)), ((), ())), preferred_element_type=F32
    )


def shape(dims, dtype):
    return jax.ShapeDtypeStruct(dims, dtype)


def kept_shape(dims, dtype):
    return pltpu.HBM(dims, dtype)


def held(array):
    return pltpu.with_memory_space_constraint(array, pltpu.HBM)


def after(value, *others):
    others = [o for o in others if o is not None]
    return lax.optimization_barrier((value, *others))[0] if others else value


def whole(dims):
    return pl.BlockSpec(dims, lambda *_: (0,) * len(dims))


def term_spec(term):
    if term.ndim == 3:
        return pl.BlockSpec((None, *term.shape[1:]), lambda *_: (0, 0, 0))
    return whole(term.shape)


def params(mib):
    return pltpu.CompilerParams(vmem_limit_bytes=mib * MIB)


def cost(flops, moved):
    return pl.CostEstimate(flops=int(flops), bytes_accessed=int(moved), transcendentals=0)


class Order:
    def __init__(self):
        self.last = None

    def run(self, step, value, need=(), beside=()):
        out = step(after(value, self.last, *need))
        out, beside = lax.optimization_barrier((out, beside))
        self.last = jax.tree.leaves(out)[0]
        return out, beside


def swap(value, axis, mask, size):
    return lax.ppermute(value, axis, [(i, i ^ mask) for i in range(size)])


def gather_far(own, size):
    pieces = {0: own}
    bit = size // 2
    while bit > 1:
        pieces.update({e | bit: swap(p, "head", bit, size) for e, p in pieces.items()})
        bit //= 2
    return pieces


def gather_near(far, size):
    pieces = dict(far)
    pieces.update({e | 1: swap(p, "head", 1, size) for e, p in far.items()})
    return [pieces[e] for e in range(size)]


class Exchange:
    def __init__(self, near, far, size):
        self.size = size
        if size == 4:
            self.flying = [swap(near, "head", 1, size), swap(far, "head", 2, size)]
        else:
            blocks = [near, *far]
            self.flying = [swap(p, "head", e, size) for e, p in enumerate(blocks, 1)]

    def finish(self, flying):
        if self.size != 4:
            return flying
        near, far = flying
        return [near, far[0], swap(far[1], "head", 1, self.size)]


def total(terms):
    if len(terms) == 1:
        return terms[0]
    return sum(t.astype(F32) for t in terms).astype(BF16)


def reduce_near(odd, size):
    return jax.tree.map(lambda p: swap(p, "head", 1, size), odd)


def reduce_far(even, near, size):
    held = {2 * i: [p, near[i]] for i, p in enumerate(even)}
    bit, sent = 2, None
    while bit < size:
        for e in [e for e in held if e & bit]:
            sent = total(held.pop(e))
            got = swap(sent, "head", bit, size)
            held[e ^ bit].append(got)
        bit *= 2
    return held[0], sent


def term_sum(terms):
    return sum((t[0] if t.ndim == 3 else t).astype(F32) for t in terms)


def sum_small(value, axis, size):
    bit = 1
    while bit < size:
        value = value + swap(value, axis, bit, size)
        bit *= 2
    return value


def halve(values, bit, place):
    rows = values.shape[0] // 2
    own = (place & bit) // bit
    return tuple(
        lax.dynamic_slice_in_dim(values, part * rows, rows, 0) for part in (own, 1 - own)
    )


class BatchSum:
    def __init__(self, values, size, direct=False, before=()):
        self.size = size
        self.place = lax.axis_index("batch")
        self.bits = [1 << i for i in range(size.bit_length() - 1)]
        self.todo = [("halve", b) for b in self.bits] + [("join", b) for b in reversed(self.bits)]
        if direct and size <= 8:
            self.bits = self.bits[:1] + self.bits[:0:-1]
            self.todo = [("halve", 1), ("scatter", 0), ("gather", 0), ("join", 1)]
        self.values, self.mine, self.flying, self.sent = values, None, None, None
        self.before = list(before)
        self.start()

    def start(self):
        kind, bit = self.todo[0]
        self.sent = self.values
        if kind == "halve":
            self.mine, self.sent = halve(self.values, bit, self.place)
        others = range(1, self.size // 2)
        if kind == "scatter":
            rows = self.values.shape[0] * 2 // self.size
            own = self.place // 2
            blocks = [
                lax.dynamic_slice_in_dim(self.values, (own ^ d) * rows, rows, 0)
                for d in range(self.size // 2)
            ]
            self.mine, self.sent = blocks[0], blocks[-1]
            self.flying = [swap(blocks[d], "batch", 2 * d, self.size) for d in others]
        elif kind == "gather":
            self.flying = [swap(self.values, "batch", 2 * d, self.size) for d in others]
        else:
            self.flying = swap(self.sent, "batch", bit, self.size)

    def advance(self, got):
        kind, _ = self.todo.pop(0)
        if not self.todo:
            self.parts = [self.values, got]
        elif kind == "halve":
            self.values = total([self.mine, got])
        elif kind == "scatter":
            self.values = total([self.mine] + got)
        else:
            got = got if kind == "gather" else [got]
            self.values = jnp.concatenate([self.values] + got, axis=0)
        if self.before:
            self.values = jnp.concatenate(self.before + [self.values], axis=0)
            self.before = []
        if self.todo:
            self.start()

    def finish(self):
        while self.todo:
            self.advance(self.flying)
        return self.parts, self.bits


def store_blocks(place, summed, refs, out):
    (first, _), bits = summed
    count = 1 << len(bits)
    rows = 2 * first.shape[0] // count
    for p in range(count):
        at = 0
        for level, bit in enumerate(bits):
            other = p >> (len(bits) - 1 - level) & 1
            at = at + (((place // bit) % 2) ^ other) * ((count >> (level + 1)) * rows)
        ref, row = refs[p * 2 // count], (p % (count // 2)) * rows
        out[pl.ds(pl.multiple_of(at, rows), rows), :] = ref[row : row + rows, :].astype(out.dtype)


def segments(first, count, ranges):
    half, skip = sum(ranges) // 2, 0
    found = []
    for size in ranges:
        part = size // 2
        for side in range(2):
            low, high = max(first, 0), min(first + count, part)
            if low < high:
                found.append((side * half + skip + low, low - first, high - low))
            first -= part
        skip += part
    return found


def assemble(summed, place):
    parts, _ = summed
    rows, width = parts[0].shape

    def body(place, own_ref, other_ref, out):
        store_blocks(place[0], summed, (own_ref, other_ref), out)

    return pl.pallas_call(
        body,
        grid_spec=pltpu.PrefetchScalarGridSpec(
            num_scalar_prefetch=1,
            grid=(1,),
            in_specs=[whole((rows, width))] * 2,
            out_specs=whole((2 * rows, width)),
        ),
        out_shape=shape((2 * rows, width), F32),
        compiler_params=params(24),
        cost_estimate=cost(0, rows * width * 12),
        name="assemble",
    )(place, *parts)


def assemble_turned(summed, place, info, cols, n_head, pairs, ranges):
    parts, _ = summed
    width = cols // pairs
    rows, model = parts[0].shape
    share = model // n_head

    def body(place, info, own_ref, other_ref, q_out, k_out, v_out, o_out, small_out, room):
        store_blocks(place[0], summed, (own_ref, other_ref), room)
        for g in range(pairs):
            for i, out in enumerate((q_out, k_out, v_out)):
                for row, offset, count in segments((3 * g + i) * width, width, ranges):
                    lanes = slice(g * width + offset, g * width + offset + count)
                    for e in range(n_head):
                        at = pl.ds(pl.multiple_of((info[0] ^ e) * share, share), share)
                        out[at, lanes] = room[row : row + count, e * share : (e + 1) * share].T
        for out, first, rows in ((o_out, 3 * cols, cols), (small_out, 4 * cols, 8)):
            for row, offset, count in segments(first, rows, ranges):
                out[offset : offset + count, :] = room[row : row + count, :]

    return pl.pallas_call(
        body,
        grid_spec=pltpu.PrefetchScalarGridSpec(
            num_scalar_prefetch=2,
            grid=(1,),
            in_specs=[whole((rows, model))] * 2,
            out_specs=[whole((model, cols))] * 3 + [whole((cols, model)), whole((8, model))],
            scratch_shapes=[pltpu.VMEM((2 * rows, model), F32)],
        ),
        out_shape=[shape((model, cols), F32)] * 3 + [shape((n, model), F32) for n in (cols, 8)],
        compiler_params=params(32),
        cost_estimate=cost(0, cols * model * 24),
        name="assemble_turned",
    )(place, info, *parts)


def visible(first_key, first_query, starts, length, rows, cols):
    key = first_key + lax.broadcasted_iota(jnp.int32, (rows, cols), 0)
    query = first_query + lax.broadcasted_iota(jnp.int32, (rows, cols), 1)
    last = jnp.minimum(query, length - 1)
    return (key >= starts) & ((key <= last) | (key == query))


def prepare(w_query, w_key, w_value, w_out, cotangent, own, pair, n_head):
    model, cols = w_query.shape
    row_len, share = cotangent.shape
    rows = row_len // CHUNKS // n_head

    def body(own, q_ref, k_ref, v_ref, o_ref, c_ref, out, half, near, far_blocks):
        for g in range(cols // pair):
            for i, ref in enumerate((q_ref, k_ref, v_ref)):
                first = (3 * g + i) * pair
                out[first : first + pair, :] = ref[:, g * pair : (g + 1) * pair].T
        half[...] = o_ref[:, pl.ds(pl.multiple_of(own[1] * (model // 2), model // 2), model // 2)]
        for e in range(1, n_head):
            for c in range(CHUNKS):
                at = (c * n_head + (own[0] ^ e)) * rows
                block = c_ref[pl.ds(pl.multiple_of(at, rows), rows), :]
                if e == 1:
                    near[c * rows : (c + 1) * rows, :] = block
                else:
                    far_blocks[e - 2, c * rows : (c + 1) * rows, :] = block

    outs = pl.pallas_call(
        body,
        grid_spec=pltpu.PrefetchScalarGridSpec(
            num_scalar_prefetch=1,
            grid=(1,),
            in_specs=[whole((model, cols))] * 3 + [whole((cols, model)), whole((row_len, share))],
            out_specs=[
                whole((3 * cols, model)),
                whole((cols, model // 2)),
                whole((CHUNKS * rows, share)),
                whole((n_head - 2, CHUNKS * rows, share)),
            ],
        ),
        out_shape=[
            shape((3 * cols, model), BF16),
            shape((cols, model // 2), BF16),
            shape((CHUNKS * rows, share), BF16),
            shape((n_head - 2, CHUNKS * rows, share), BF16),
        ],
        compiler_params=params(24),
        cost_estimate=cost(0, 12 * cols * model),
        name="prepare",
    )(own, w_query, w_key, w_value, w_out, cotangent)
    return outs


def attend_kernel(
    chunk, n_head, heads, chunk_len, share, info, *refs
):
    refs = list(refs)
    x_refs = [refs.pop(0) for _ in range(n_head)]
    w_ref, cos_ref, sin_ref, gain_ref, start_ref = [refs.pop(0) for _ in range(5)]
    old_k, old_v = None, None
    if chunk:
        old_k, old_v = refs.pop(0), refs.pop(0)
        refs = refs[7:]
    k_ref, ve_ref, v_ref, kt_ref, qt_ref, ot_ref, inv_ref, qf_ref, kf_ref, o_ref = refs[:10]
    near_ref, far_ref, raw, acc = refs[10:]
    me, length = info[0], info[1]
    cols = heads * HD
    pair = min(2, heads)
    for e in range(n_head):
        first = pl.multiple_of((me ^ e) * share, share)
        for third in range(3):
            rows = slice(third * cols, (third + 1) * cols)
            term = dot(w_ref[rows, pl.ds(first, share)], x_refs[e][...], 1, 1)
            if e == 0:
                raw[rows, :] = term
            else:
                raw[rows, :] += term

    def raw_row(part, h):
        return ((h // pair * 3 + part) * pair + h % pair) * HD

    cosine, sine = cos_ref[...], sin_ref[...]
    for h in range(heads):
        own = slice(h * HD, (h + 1) * HD)
        for part, factor_ref in ((0, qf_ref), (1, kf_ref)):
            base = raw_row(part, h)
            a, b = raw[base : base + HALF, :], raw[base + HALF : base + HD, :]
            front, back = a * cosine - b * sine, b * cosine + a * sine
            mean = jnp.sum(front * front + back * back, axis=0, keepdims=True) / HD
            factor = lax.rsqrt(mean + EPSILON)
            factor_ref[h] = factor
            unit = jnp.concatenate([front, back], axis=0) * factor
            low = (unit * gain_ref[own, :]).astype(BF16)
            if part == 0:
                qt_ref[own, :] = low * BF16(1.0 / math.sqrt(HD))
            else:
                kt_ref[own, :] = low
                k_ref[h] = low.T
        value = raw[raw_row(2, h) : raw_row(2, h) + HD, :].astype(BF16)
        v_ref[h] = value.T
        ve_ref[h, :HD, :] = value
        ve_ref[h, HD:, :] = jnp.ones((VALUE_ROWS - HD, chunk_len), BF16)

    before = chunk * (chunk_len // KEYS)

    def step(local, key_first, k_of, v_of, starts):
        query = slice(local * QUERIES, (local + 1) * QUERIES)
        first = chunk * chunk_len + local * QUERIES
        mask = visible(key_first, first, starts, length, KEYS, QUERIES)
        for h in range(heads):
            scores = dot(k_of(h), qt_ref[h * HD : (h + 1) * HD, query])
            probs = jnp.where(mask, jnp.exp(scores), 0.0).astype(BF16)
            acc[h] += dot(v_of(h), probs)

    for local in range(chunk_len // QUERIES):
        query = slice(local * QUERIES, (local + 1) * QUERIES)
        starts = start_ref[:, query]
        lowest = info[2 + (chunk * chunk_len + local * QUERIES) // BLOCK] * BLOCK // KEYS
        acc[...] = jnp.zeros_like(acc)
        if chunk:

            @pl.loop(lowest, before)
            def _(kb):
                at = pl.ds(pl.multiple_of(kb * KEYS, KEYS), KEYS)
                step(
                    local, kb * KEYS, lambda h: old_k[h, at, :], lambda h: old_v[h, :, at], starts
                )

        @pl.loop(jnp.maximum(lowest - before, 0), (local + 1) * QUERIES // KEYS)
        def _(kb):
            at = pl.ds(pl.multiple_of(kb * KEYS, KEYS), KEYS)
            step(
                local,
                (before + kb) * KEYS,
                lambda h: k_ref[h, at, :],
                lambda h: ve_ref[h, :, at],
                starts,
            )

        for h in range(heads):
            inverse = 1.0 / acc[h, HD : HD + 1, :]
            inv_ref[h, :, query] = inverse
            out = acc[h, :HD, :] * inverse
            ot_ref[h * HD : (h + 1) * HD, query] = out.astype(BF16)
            o_ref[query, h * HD : (h + 1) * HD] = out.T.astype(BF16)
    rows = chunk_len // n_head
    for e in range(1, n_head):
        block = o_ref[pl.ds(pl.multiple_of((me ^ e) * rows, rows), rows), :]
        if e == 1:
            near_ref[...] = block
        else:
            far_ref[e - 2] = block


def attend_chunk(
    chunk, x_pieces, w_t, cosine, sine, gain, starts, info, buffers, row_len, chunk_len
):
    n_head = len(x_pieces)
    share = x_pieces[0].shape[1]
    cols = w_t.shape[0] // 3
    heads = cols // HD
    model = w_t.shape[1]
    body = functools.partial(attend_kernel, chunk, n_head, heads, chunk_len, share)
    by_lane = lambda rows: pl.BlockSpec((rows, chunk_len), lambda i, info: (0, chunk))
    specs = [whole((chunk_len, share))] * n_head + [
        whole((3 * cols, model)),
        by_lane(HALF),
        by_lane(HALF),
        whole((cols, 1)),
        by_lane(1),
    ]
    operands = [*x_pieces, w_t, cosine, sine, gain, starts]
    aliases = {}
    if chunk:
        aliases = {1 + len(operands) + i: i for i in range(9)}
        specs += [whole((heads, row_len, HD)), whole((heads, VALUE_ROWS, row_len))]
        specs += [pl.BlockSpec(memory_space=pl.ANY)] * 7
        operands += buffers
    lane3 = lambda rows: pl.BlockSpec((heads, rows, chunk_len), lambda i, info: (0, 0, chunk))
    row3 = pl.BlockSpec((heads, chunk_len, HD), lambda i, info: (0, chunk, 0))
    outs = pl.pallas_call(
        body,
        grid_spec=pltpu.PrefetchScalarGridSpec(
            num_scalar_prefetch=1,
            grid=(1,),
            in_specs=specs,
            out_specs=[
                row3,
                lane3(VALUE_ROWS),
                row3,
                by_lane(cols),
                by_lane(cols),
                by_lane(cols),
                lane3(1),
                lane3(1),
                lane3(1),
                whole((chunk_len, cols)),
            ]
            + [
                whole((chunk_len // n_head, cols)),
                whole((n_head - 2, chunk_len // n_head, cols)),
            ],
            scratch_shapes=[
                pltpu.VMEM((3 * cols, chunk_len), F32),
                pltpu.VMEM((heads, VALUE_ROWS, QUERIES), F32),
            ],
        ),
        out_shape=[
            kept_shape((heads, row_len, HD), BF16),
            kept_shape((heads, VALUE_ROWS, row_len), BF16),
            kept_shape((heads, row_len, HD), BF16),
            kept_shape((cols, row_len), BF16),
            kept_shape((cols, row_len), BF16),
            kept_shape((cols, row_len), BF16),
            kept_shape((heads, 1, row_len), F32),
            kept_shape((heads, 1, row_len), F32),
            kept_shape((heads, 1, row_len), F32),
            kept_shape((chunk_len, cols), BF16),
        ]
        + [
            kept_shape((chunk_len // n_head, cols), BF16),
            kept_shape((n_head - 2, chunk_len // n_head, cols), BF16),
        ],
        input_output_aliases=aliases,
        compiler_params=params(40),
        cost_estimate=cost(16e9 / CHUNKS, 8e6),
        name="attend",
    )(info, *operands)
    return outs[:9], list(outs[9:])


def unattend_kernel(n_head, chunks, row_len, piece, pair, info, *refs):
    refs = list(refs)
    d_refs = [refs.pop(0) for _ in range(chunks * n_head)]
    k_ref, v_ref, kt_ref, qt_ref, ot_ref, inv_ref, qf_ref, kf_ref = [refs.pop(0) for _ in range(8)]
    start_ref, cos_ref, sin_ref, gain_ref = [refs.pop(0) for _ in range(4)]
    out_ref, gain_out, do_s, inner_s, dq_s, dk_s, dv_s = refs
    me, length = info[0], info[1]
    for c in range(chunks):
        for e in range(n_head):
            first = c * n_head * piece + (me ^ e) * piece
            do_s[:, pl.ds(pl.multiple_of(first, piece), piece)] = d_refs[c * n_head + e][...]
    for h in range(pair):
        own = slice(h * HD, (h + 1) * HD)
        product = do_s[own, :].astype(F32) * ot_ref[own, :].astype(F32)
        inner_s[h] = jnp.sum(product, axis=0, keepdims=True)
    dq_s[...] = jnp.zeros_like(dq_s)
    dk_s[...] = jnp.zeros_like(dk_s)
    dv_s[...] = jnp.zeros_like(dv_s)

    ratio = QUERIES // BLOCK

    @pl.loop(0, row_len // QUERIES)
    def _(qb):
        query = pl.ds(pl.multiple_of(qb * QUERIES, QUERIES), QUERIES)
        starts = start_ref[:, query]

        @pl.loop(info[2 + qb * ratio], (qb + 1) * ratio)
        def _(kb):
            key = pl.ds(pl.multiple_of(kb * BLOCK, BLOCK), BLOCK)
            mask = visible(kb * BLOCK, qb * QUERIES, starts, length, BLOCK, QUERIES)
            for h in range(pair):
                own = slice(h * HD, (h + 1) * HD)
                q_block, do_block = qt_ref[own, query], do_s[own, query]
                scores = dot(k_ref[h, key, :], q_block)
                probs = jnp.where(mask, jnp.exp(scores), 0.0) * inv_ref[h, :, query]
                d_probs = dot(v_ref[h, key, :], do_block)
                d_scores = (probs * (d_probs - inner_s[h, :, query])).astype(BF16)
                dv_s[own, key] += dot(do_block, probs.astype(BF16), 1, 1)
                dk_s[own, key] += dot(q_block, d_scores, 1, 1)
                dq_s[own, query] += dot(kt_ref[own, key], d_scores)

    for h in range(pair):
        own = slice(h * HD, (h + 1) * HD)
        gain = gain_ref[own, :]
        summed = jnp.zeros((HD, 1), F32)
        for part, low_ref, grad_ref, factor_ref in (
            (0, qt_ref, dq_s, qf_ref),
            (1, kt_ref, dk_s, kf_ref),
        ):
            scale = math.sqrt(HD) if part == 0 else 1.0
            unit = low_ref[own, :].astype(F32) * (scale / gain)
            grad = grad_ref[own, :]
            if part == 0:
                grad = grad * (1.0 / math.sqrt(HD))
            summed += jnp.sum(grad * unit, axis=1, keepdims=True)
            grad = grad * gain
            mean = jnp.sum(grad * unit, axis=0, keepdims=True) / HD
            grad = (grad - unit * mean) * factor_ref[h]
            front, back = grad[:HALF], grad[HALF:]
            cosine, sine = cos_ref[...], sin_ref[...]
            out_ref[part, h * HD : h * HD + HALF, :] = (front * cosine + back * sine).astype(BF16)
            out_ref[part, h * HD + HALF : (h + 1) * HD, :] = (
                back * cosine - front * sine
            ).astype(BF16)
        out_ref[2, own, :] = dv_s[own, :].astype(BF16)
        gain_out[own, :] = summed


def unattend(index, do_pieces, buffers, starts, cosine, sine, gain, info, n_head):
    k, _, v, kt, qt, ot, inv, qf, kf = buffers
    chunks = len(do_pieces) // n_head
    cols, piece = do_pieces[0].shape
    heads, row_len, _ = k.shape
    pair = min(2, heads)
    rows = pair * HD
    by_rows = lambda width: pl.BlockSpec((rows, width), lambda g, info: (index, 0))
    by_head = lambda a, b: pl.BlockSpec((pair, a, b), lambda g, info: (index, 0, 0))
    return pl.pallas_call(
        functools.partial(unattend_kernel, n_head, chunks, row_len, piece, pair),
        grid_spec=pltpu.PrefetchScalarGridSpec(
            num_scalar_prefetch=1,
            grid=(1,),
            in_specs=[by_rows(piece)] * (chunks * n_head)
            + [by_head(row_len, HD)] * 2
            + [by_rows(row_len)] * 3
            + [by_head(1, row_len)] * 3
            + [whole((1, row_len)), whole((HALF, row_len)), whole((HALF, row_len)), by_rows(1)],
            out_specs=[whole((3, rows, row_len)), whole((rows, 1))],
            scratch_shapes=[
                pltpu.VMEM((rows, row_len), BF16),
                pltpu.VMEM((pair, 1, row_len), F32),
                pltpu.VMEM((rows, row_len), F32),
                pltpu.VMEM((rows, row_len), F32),
                pltpu.VMEM((rows, row_len), F32),
            ],
        ),
        out_shape=[kept_shape((3, rows, row_len), BF16), shape((rows, 1), F32)],
        compiler_params=params(32),
        cost_estimate=cost(22e9, 6e6),
        name="unattend",
    )(info, *do_pieces, k, v, kt, qt, ot, inv, qf, kf, starts, cosine, sine, gain)


def norm(values):
    factor = lax.rsqrt(jnp.mean(values * values, axis=-1, keepdims=True) + EPSILON)
    return values * factor, factor


def norm_back(grad, unit, factor):
    return factor * (grad - unit * jnp.mean(grad * unit, axis=-1, keepdims=True))


def project_kernel(n_head, share, kept, info, *refs):
    o_refs, w_refs = refs[:n_head], refs[n_head : 2 * n_head]
    x_refs = refs[2 * n_head : 3 * n_head]
    alpha_ref = refs[3 * n_head]
    cat_ref, y_ref, x_ref, h_ref, low_ref = refs[3 * n_head + 1 + kept :]
    me = info[0]
    cols = w_refs[0].shape[0]
    y = dot(o_refs[0][...], w_refs[0][...])
    for e in range(1, n_head):
        y += dot(o_refs[e][...], w_refs[e][...])
    for e in range(n_head):
        cat_ref[:, e * cols : (e + 1) * cols] = o_refs[e][...]
    for e in range(n_head):
        first = pl.multiple_of((me ^ e) * share, share)
        x_ref[:, pl.ds(first, share)] = x_refs[e][...]
    y_ref[...] = y
    h_zero = x_ref[...].astype(F32)
    h_one, _ = norm(h_zero + alpha_ref[...] * (norm(y)[0] - h_zero))
    h_ref[...] = h_one
    low_ref[...] = h_one.astype(BF16)


def project(chunk, kept, o_pieces, w_pieces, x_pieces, alpha, info, chunk_len):
    n_head = len(o_pieces)
    cols, model = w_pieces[0].shape
    share = x_pieces[0].shape[1]
    rows = chunk_len // n_head
    mine = lambda width: pl.BlockSpec((rows, width), lambda i, info: (info[0], 0))
    return pl.pallas_call(
        functools.partial(project_kernel, n_head, share, len(kept)),
        grid_spec=pltpu.PrefetchScalarGridSpec(
            num_scalar_prefetch=1,
            grid=(1,),
            in_specs=[mine(cols)]
            + [whole((rows, cols))] * (n_head - 1)
            + [whole((cols, model))] * n_head
            + [mine(share)] * n_head
            + [whole((1, model))]
            + [pl.BlockSpec(memory_space=pl.ANY)] * len(kept),
            out_specs=[pl.BlockSpec((rows, n_head * cols), lambda i, info: (chunk, 0))]
            + [whole((rows, model))] * 4,
        ),
        input_output_aliases={3 * n_head + 2 + i: i for i in range(len(kept))},
        out_shape=[
            kept_shape((CHUNKS * rows, n_head * cols), BF16),
            kept_shape((rows, model), F32),
            kept_shape((rows, model), BF16),
            kept_shape((rows, model), F32),
            shape((rows, model), BF16),
        ],
        compiler_params=params(32),
        cost_estimate=cost(2.0 * rows * model * model, 6e6),
        name="project",
    )(info, *o_pieces, *w_pieces, *x_pieces, alpha, *kept)


def feed_kernel(n_head, rows, *refs):
    h_refs = refs[:n_head]
    up_ref, gate_ref, down_hbm, su_ref, sg_ref = refs[n_head : n_head + 5]
    m_ref, cat_hbm, u_ref, g_ref = refs[n_head + 5 : n_head + 9]
    z_refs = refs[n_head + 9 : 2 * n_head + 9]
    cat, mixed_s, down, cat_sem, down_sem = refs[2 * n_head + 9 :]
    tile = pl.program_id(0)
    keep = pltpu.make_async_copy(cat, cat_hbm, cat_sem)
    fetch = pltpu.make_async_copy(down_hbm, down, down_sem)

    @pl.when(tile == 0)
    def _():
        fetch.start()
        for e in range(n_head):
            cat[e * rows : (e + 1) * rows, :] = h_refs[e][...]
        keep.start()

    up_raw = dot(cat[...], up_ref[...])
    gate_raw = dot(cat[...], gate_ref[...])
    u_ref[...] = up_raw.astype(BF16)
    g_ref[...] = gate_raw.astype(BF16)
    gate = gate_raw * sg_ref[...]
    mixed = (up_raw * su_ref[...] * (gate * jax.nn.sigmoid(gate))).astype(BF16)
    m_ref[...] = mixed
    width = m_ref.shape[1]
    mixed_s[:, pl.ds(pl.multiple_of(tile * width, width), width)] = mixed

    @pl.when(tile == pl.num_programs(0) - 1)
    def _():
        fetch.wait()
        z = dot(mixed_s[...], down[...])
        for e in range(n_head):
            z_refs[e][...] = z[e * rows : (e + 1) * rows, :].astype(BF16)
        keep.wait()


def feed(h_pieces, w_up, w_gate, w_down, scale_up, scale_gate):
    n_head = len(h_pieces)
    rows, model = h_pieces[0].shape
    hidden = w_up.shape[1]
    tile = min(256, hidden // 2)
    count = n_head * rows
    by_col = lambda height: pl.BlockSpec((height, tile), lambda n: (0, n))
    anywhere = pl.BlockSpec(memory_space=pl.ANY)
    outs = pl.pallas_call(
        functools.partial(feed_kernel, n_head, rows),
        grid=(hidden // tile,),
        in_specs=[whole((rows, model))] * n_head
        + [by_col(model), by_col(model), anywhere, by_col(1), by_col(1)],
        out_specs=[by_col(count), anywhere, by_col(count), by_col(count)]
        + [whole((rows, model))] * n_head,
        out_shape=[
            kept_shape((count, hidden), BF16),
            kept_shape((count, model), BF16),
            kept_shape((count, hidden), BF16),
            kept_shape((count, hidden), BF16),
        ]
        + [shape((rows, model), BF16)] * n_head,
        scratch_shapes=[
            pltpu.VMEM((count, model), BF16),
            pltpu.VMEM((count, hidden), BF16),
            pltpu.VMEM((hidden, model), BF16),
            pltpu.SemaphoreType.DMA,
            pltpu.SemaphoreType.DMA,
        ],
        compiler_params=params(48),
        cost_estimate=cost(6.0 * count * model * hidden, 20e6),
        name="feed",
    )(*h_pieces, w_up, w_gate, held(w_down), scale_up, scale_gate)
    return outs[:2], outs[2:4], list(outs[4::2]), list(outs[5::2])


def middle_kernel(n_head, n_terms, share, kept, info, *refs):
    z_refs, c_refs = refs[:n_terms], refs[n_terms : n_terms + n_head]
    h_ref, alpha_ref = refs[n_terms + n_head : n_terms + n_head + 2]
    refs = refs[n_terms + n_head + 2 + kept :]
    own_ref, near_ref, far_ref, dz_ref, direct_ref, grad_ref, two_s, cot_s = refs
    me = info[0]
    z = z_refs[0][...].astype(F32)
    for r in z_refs[1:]:
        z += r[...].astype(F32)
    h_one, alpha = h_ref[...], alpha_ref[...]
    h_ffn, z_factor = norm(z)
    h_two, factor = norm(h_one + alpha * (h_ffn - h_one))
    two_s[...] = h_two.astype(BF16)
    for e in range(n_head):
        at = pl.ds(pl.multiple_of((me ^ e) * share, share), share)
        if e < 2:
            (own_ref, near_ref)[e][...] = two_s[:, at]
        else:
            far_ref[e - 2] = two_s[:, at]
        cot_s[:, at] = c_refs[e][...]
    grad = norm_back(cot_s[...].astype(F32), h_two, factor)
    grad_ref[...] = jnp.sum(grad * (h_ffn - h_one), axis=0, keepdims=True)
    direct_ref[...] = grad * (1.0 - alpha)
    dz_ref[...] = norm_back(grad * alpha, h_ffn, z_factor).astype(BF16)


def middle(chunk, kept, z_terms, cot_pieces, h_one, alpha, info):
    n_head, n_terms = len(cot_pieces), len(z_terms)
    rows, model = h_one.shape
    share = cot_pieces[0].shape[1]
    mine = pl.BlockSpec((rows, share), lambda i, info: (chunk * n_head + info[0], 0))
    theirs = pl.BlockSpec((rows, share), lambda i, info: (chunk, 0))
    outs = pl.pallas_call(
        functools.partial(middle_kernel, n_head, n_terms, share, len(kept)),
        grid_spec=pltpu.PrefetchScalarGridSpec(
            num_scalar_prefetch=1,
            grid=(1,),
            in_specs=[term_spec(t) for t in z_terms]
            + [mine]
            + [theirs] * (n_head - 1)
            + [whole((rows, model)), whole((1, model))]
            + [pl.BlockSpec(memory_space=pl.ANY)] * len(kept),
            out_specs=[theirs] * 2
            + [pl.BlockSpec((n_head - 2, rows, share), lambda i, info: (0, chunk, 0))]
            + [whole((rows, model))] * 2
            + [whole((1, model))],
            scratch_shapes=[pltpu.VMEM((rows, model), BF16), pltpu.VMEM((rows, model), BF16)],
        ),
        input_output_aliases={n_terms + n_head + 3 + i: i for i in range(len(kept))},
        out_shape=[kept_shape((CHUNKS * rows, share), BF16)] * 2
        + [kept_shape((n_head - 2, CHUNKS * rows, share), BF16)]
        + [shape((rows, model), BF16), kept_shape((rows, model), F32), shape((1, model), F32)],
        compiler_params=params(32),
        cost_estimate=cost(rows * model * 60, rows * model * 24),
        name="middle",
    )(info, *z_terms, *cot_pieces, held(h_one), alpha, *kept)
    return list(outs[:3]), *outs[3:]


def join(pieces):
    rows, width = pieces[0].shape

    def body(*refs):
        for i, ref in enumerate(refs[:-1]):
            refs[-1][i * rows : (i + 1) * rows, :] = ref[...]

    return pl.pallas_call(
        body,
        in_specs=[whole((rows, width))] * len(pieces),
        out_specs=whole((rows * len(pieces), width)),
        grid=(1,),
        out_shape=shape((rows * len(pieces), width), pieces[0].dtype),
        compiler_params=params(16),
        cost_estimate=cost(0, rows * width * 4 * len(pieces)),
        name="join",
    )(*pieces)


def weigh_feed(mixed, joined, dz, du, dg):
    count, hidden = mixed.shape
    model = joined.shape[1]
    tile = min(256, hidden // 2)

    def body(m_ref, h_ref, z_ref, u_ref, g_ref, down, up, gate):
        down[...] = dot(m_ref[...], z_ref[...], 0, 0)
        up[...] = dot(h_ref[...], u_ref[...], 0, 0)
        gate[...] = dot(h_ref[...], g_ref[...], 0, 0)

    by_col = lambda height: pl.BlockSpec((height, tile), lambda n: (0, n))
    return pl.pallas_call(
        body,
        in_specs=[
            by_col(count),
            whole((count, model)),
            whole((count, model)),
            by_col(count),
            by_col(count),
        ],
        out_specs=[pl.BlockSpec((tile, model), lambda n: (n, 0)), by_col(model), by_col(model)],
        grid=(hidden // tile,),
        out_shape=[kept_shape((hidden, model), F32)] + [kept_shape((model, hidden), F32)] * 2,
        compiler_params=params(48),
        cost_estimate=cost(6.0 * count * hidden * model, 20e6),
        name="weigh_feed",
    )(mixed, joined, dz, du, dg)


def weigh(d_pair, x_pieces, chunk_len):
    rows, row_len = d_pair.shape
    n_head = len(x_pieces[0])
    share = x_pieces[0][0].shape[1]
    flat = [p for chunk in x_pieces for p in chunk]

    def body(d_ref, *refs):
        for e in range(n_head):
            term = None
            for c in range(len(x_pieces)):
                d_part = d_ref[:, c * chunk_len : (c + 1) * chunk_len]
                new = dot(d_part, refs[c * n_head + e][...])
                term = new if term is None else term + new
            refs[-1][:, e * share : (e + 1) * share] = term.astype(BF16)

    return pl.pallas_call(
        body,
        in_specs=[whole((rows, row_len))] + [whole((chunk_len, share))] * len(flat),
        out_specs=whole((rows, n_head * share)),
        grid=(1,),
        out_shape=shape((rows, n_head * share), BF16),
        compiler_params=params(32),
        cost_estimate=cost(0, 1),
        name="weigh",
    )(d_pair, *flat)


def unfeed_kernel(n_head, n_in, rows, *refs):
    d_refs, refs = refs[:n_in], refs[n_in:]
    u_ref, g_ref, up_hbm, gate_hbm, down_ref, su_ref, sg_ref = refs[:7]
    du_ref, dg_ref, gsu_ref, gsg_ref = refs[7:11]
    out_refs = refs[11 : 11 + n_head]
    cat_hbm = refs[11 + n_head] if n_in > 1 else None
    refs = refs[11 + n_head + (n_in > 1) :]
    du_s, dg_s, up, gate_w, sems = refs[:5]
    cat = refs[5] if n_in > 1 else d_refs[0]
    tile = pl.program_id(0)
    fetch_up = pltpu.make_async_copy(up_hbm, up, sems.at[0])
    fetch_gate = pltpu.make_async_copy(gate_hbm, gate_w, sems.at[1])
    keep = pltpu.make_async_copy(cat, cat_hbm, sems.at[2]) if n_in > 1 else None

    @pl.when(tile == 0)
    def _():
        fetch_up.start()
        fetch_gate.start()
        if n_in > 1:
            for e in range(n_in):
                cat[e * rows : (e + 1) * rows, :] = d_refs[e][...]
            keep.start()

    d_mixed = dot(cat[...], down_ref[...], 1, 1)
    up_raw, gate_raw = u_ref[...].astype(F32), g_ref[...].astype(F32)
    gate = gate_raw * sg_ref[...]
    sigmoid = jax.nn.sigmoid(gate)
    silu = gate * sigmoid
    d_up = d_mixed * silu
    d_gate = d_mixed * (up_raw * su_ref[...]) * (sigmoid + silu * (1.0 - sigmoid))
    gsu_ref[...] = jnp.sum(d_up * up_raw, axis=0, keepdims=True)
    gsg_ref[...] = jnp.sum(d_gate * gate_raw, axis=0, keepdims=True)
    up_low = (d_up * su_ref[...]).astype(BF16)
    gate_low = (d_gate * sg_ref[...]).astype(BF16)
    du_ref[...] = up_low
    dg_ref[...] = gate_low
    width = du_ref.shape[1]
    at = pl.ds(pl.multiple_of(tile * width, width), width)
    du_s[:, at] = up_low
    dg_s[:, at] = gate_low

    @pl.when(tile == pl.num_programs(0) - 1)
    def _():
        fetch_up.wait()
        fetch_gate.wait()
        dh = dot(du_s[...], up[...], 1, 1) + dot(dg_s[...], gate_w[...], 1, 1)
        for e in range(n_head):
            out_refs[e][...] = dh[e * rows : (e + 1) * rows, :].astype(BF16)
        if n_in > 1:
            keep.wait()


def unfeed(dz_pieces, u, g, w_up, w_gate, w_down, scale_up, scale_gate, n_head):
    n_in = len(dz_pieces)
    model = dz_pieces[0].shape[1]
    count, hidden = u.shape
    rows = count // n_head
    tile = min(256, hidden // 2)
    by_col = lambda height: pl.BlockSpec((height, tile), lambda n: (0, n))
    anywhere = pl.BlockSpec(memory_space=pl.ANY)
    outs = pl.pallas_call(
        functools.partial(unfeed_kernel, n_head, n_in, rows),
        grid=(hidden // tile,),
        in_specs=[whole(dz_pieces[0].shape)] * n_in
        + [
            by_col(count),
            by_col(count),
            anywhere,
            anywhere,
            pl.BlockSpec((tile, model), lambda n: (n, 0)),
            by_col(1),
            by_col(1),
        ],
        out_specs=[by_col(count)] * 2
        + [by_col(1), by_col(1)]
        + [whole((rows, model))] * n_head
        + [anywhere] * (n_in > 1),
        out_shape=[kept_shape((count, hidden), BF16)] * 2
        + [shape((1, hidden), F32), shape((1, hidden), F32)]
        + [shape((rows, model), BF16)] * n_head
        + [kept_shape((count, model), BF16)] * (n_in > 1),
        scratch_shapes=[
            pltpu.VMEM((count, hidden), BF16),
            pltpu.VMEM((count, hidden), BF16),
            pltpu.VMEM((model, hidden), BF16),
            pltpu.VMEM((model, hidden), BF16),
            pltpu.SemaphoreType.DMA((3,)),
        ]
        + [pltpu.VMEM((count, model), BF16)] * (n_in > 1),
        compiler_params=params(48),
        cost_estimate=cost(6.0 * count * model * hidden, 20e6),
        name="unfeed",
    )(*dz_pieces, u, g, held(w_up), held(w_gate), w_down, scale_up, scale_gate)
    pieces = outs[4 : 4 + n_head]
    return outs[:2], outs[2:4], list(pieces[::2]), list(pieces[1::2]), outs[-1]


def unproject_kernel(n_head, n_terms, kept, *refs):
    t_refs, w_refs = refs[:n_terms], refs[n_terms : n_terms + n_head]
    direct_ref, y_ref, x_ref, alpha_ref = refs[n_terms + n_head : n_terms + n_head + 4]
    refs = refs[n_terms + n_head + 4 + kept :]
    dy_ref, refs = refs[0], refs[1:]
    own_ref, near_ref, far_ref, zero_ref, grad_ref = refs
    grad = direct_ref[...]
    for r in t_refs:
        grad += r[...].astype(F32)
    alpha = alpha_ref[...]
    h_zero = x_ref[...].astype(F32)
    h_attn, y_factor = norm(y_ref[...])
    h_one, factor = norm(h_zero + alpha * (h_attn - h_zero))
    grad = norm_back(grad, h_one, factor)
    grad_ref[...] = jnp.sum(grad * (h_attn - h_zero), axis=0, keepdims=True)
    zero_ref[...] = grad * (1.0 - alpha)
    dy = norm_back(grad * alpha, h_attn, y_factor).astype(BF16)
    dy_ref[...] = dy
    for e in range(n_head):
        value = dot(w_refs[e][...], dy, 1, 1).astype(BF16)
        if e < 2:
            (own_ref, near_ref)[e][...] = value
        else:
            far_ref[e - 2] = value


def unproject(chunk, kept, terms, w_pieces, direct, y, x, alpha):
    n_head, n_terms = len(w_pieces), len(terms)
    rows, model = y.shape
    cols = w_pieces[0].shape[0]
    outs = pl.pallas_call(
        functools.partial(unproject_kernel, n_head, n_terms, len(kept)),
        grid=(1,),
        in_specs=[term_spec(t) for t in terms]
        + [whole((cols, model))] * n_head
        + [whole((rows, model))] * 3
        + [whole((1, model))]
        + [pl.BlockSpec(memory_space=pl.ANY)] * len(kept),
        out_specs=[pl.BlockSpec((rows, model), lambda i: (chunk, 0))]
        + [whole((cols, rows))] * 2
        + [whole((n_head - 2, cols, rows))]
        + [whole((rows, model)), whole((1, model))],
        input_output_aliases={n_terms + n_head + 4 + i: i for i in range(len(kept))},
        out_shape=[kept_shape((CHUNKS * rows, model), BF16)]
        + [shape((cols, rows), BF16)] * 2
        + [shape((n_head - 2, cols, rows), BF16)]
        + [kept_shape((rows, model), F32), shape((1, model), F32)],
        compiler_params=params(32),
        cost_estimate=cost(2.0 * rows * model * model, 8e6),
        name="unproject",
    )(*terms, *w_pieces, held(direct), held(y), held(x), alpha, *kept)
    return outs[0], list(outs[1:4]), outs[4], outs[5]


def spread_kernel(n_head, share, pairs, info, *refs):
    d_refs, (w_ref, direct_ref), out_refs = refs[:pairs], refs[pairs : pairs + 2], refs[pairs + 2 :]
    me = info[0]
    block = pl.program_id(0)
    d_all = jnp.concatenate([r[...] for r in d_refs], axis=0).T
    for e in range(n_head):
        at = pl.ds(pl.multiple_of((me ^ e) * share, share), share)
        term = dot(d_all, w_ref[:, at])

        ref = out_refs[n_head // 2].at[e // 2] if e % 2 else out_refs[e // 2]

        @pl.when(block == me)
        def _():
            ref[...] = (term + direct_ref[:, at]).astype(BF16)

        @pl.when(block != me)
        def _():
            ref[...] = term.astype(BF16)


def spread(chunk, chunk_len, d_all, w_t, direct, info, n_head):
    rows3, model = w_t.shape
    share = model // n_head
    rows = chunk_len // n_head
    return pl.pallas_call(
        functools.partial(spread_kernel, n_head, share, len(d_all)),
        grid_spec=pltpu.PrefetchScalarGridSpec(
            num_scalar_prefetch=1,
            grid=(n_head,),
            in_specs=[
                *[pl.BlockSpec((d.shape[0], rows), lambda i, info: (0, chunk * n_head + i)) for d in d_all],
                whole((rows3, model)),
                whole((rows, model)),
            ],
            out_specs=[pl.BlockSpec((rows, share), lambda i, info: (i, 0))] * (n_head // 2)
            + [pl.BlockSpec((n_head // 2, rows, share), lambda i, info: (0, i, 0))],
        ),
        out_shape=[shape((chunk_len, share), BF16)] * (n_head // 2)
        + [shape((n_head // 2, chunk_len, share), BF16)],
        compiler_params=params(32),
        cost_estimate=cost(2.0 * chunk_len * model * rows3, 8e6),
        name="spread",
    )(info, *d_all, w_t, direct)


def settle(own, pieces, info):
    pieces = [own] + pieces
    n_head = len(pieces)
    count, share = own.shape
    rows = count // CHUNKS

    def body(info, *refs):
        for e in range(n_head):
            for c in range(CHUNKS):
                at = (c * n_head + (info[0] ^ e)) * rows
                refs[-1][pl.ds(pl.multiple_of(at, rows), rows), :] = refs[e][
                    c * rows : (c + 1) * rows, :
                ]

    return pl.pallas_call(
        body,
        grid_spec=pltpu.PrefetchScalarGridSpec(
            num_scalar_prefetch=1,
            grid=(1,),
            in_specs=[whole((count, share))] * n_head,
            out_specs=whole((n_head * count, share)),
        ),
        out_shape=shape((n_head * count, share), BF16),
        compiler_params=params(16),
        cost_estimate=cost(0, n_head * count * share * 4),
        name="settle",
    )(info, *pieces)


def on_device(
    n_batch,
    n_head,
    hidden_in,
    cotangent,
    doc_ids,
    lengths,
    w_query,
    w_key,
    w_value,
    w_out,
    w_up,
    w_gate,
    w_down,
    scale_qk,
    scale_up,
    scale_gate,
    alpha_attn,
    alpha_ffn,
):
    _, row_len, share = hidden_in.shape
    model = share * n_head
    cols = w_query.shape[1]
    chunk_len = row_len // CHUNKS
    rows = chunk_len // n_head
    me = lax.axis_index("head")
    chunks = range(CHUNKS)
    x_own, cot_own = hidden_in[0], cotangent[0]

    docs = doc_ids[0]
    column = jnp.arange(row_len, dtype=jnp.int32)
    starts = sum(
        jnp.where(docs > d, jnp.sum((docs == d).astype(jnp.int32)), 0) for d in range(5)
    ).astype(jnp.int32)
    position = (column - starts).astype(F32)
    frequency = 10000.0 ** (-(jnp.arange(HALF, dtype=F32) * 2.0 / HD))
    angles = frequency[:, None] * position[None, :]
    cosine, sine = jnp.cos(angles), jnp.sin(angles)
    info = jnp.concatenate(
        [me[None].astype(jnp.int32), lengths.astype(jnp.int32), starts[::BLOCK] // BLOCK]
    )
    starts = starts[None, :]
    gain = scale_qk[:, None]
    up_scale, gate_scale = scale_up[None, :], scale_gate[None, :]
    attn_alpha, ffn_alpha = alpha_attn[None, :], alpha_ffn[None, :]

    def part(values, c):
        return lax.slice_in_dim(values, c * chunk_len, (c + 1) * chunk_len, axis=0)

    def block_of(values, e):
        return lax.dynamic_slice_in_dim(values, (me ^ e) * rows, rows, 0)

    order = Order()
    pair = min(2, cols // HD) * HD
    pairs = cols // pair
    far = n_head // 2
    place = lax.axis_index("batch")[None].astype(jnp.int32)

    bit = lax.axis_index("batch") % 2
    own = jnp.stack([me, bit]).astype(jnp.int32)

    x_far = gather_far(part(x_own, 0), n_head)
    (w_t, out_half, cot_near, cot_far), x_far = order.run(
        lambda w: prepare(w, w_key, w_value, w_out, cot_own, own, pair, n_head),
        w_query,
        beside=x_far,
    )
    buffers, x_pieces, o_own, o_moving = [], [], [], []
    for c in chunks:
        x_pieces.append(gather_near(x_far, n_head))
        beside = []
        if c == 0:
            halves = {
                e: swap(after(out_half, order.last), "head", e, n_head) for e in range(2, n_head, 2)
            }
            beside = [halves]
        else:
            cot_moving = Exchange(after(cot_near, order.last), after(cot_far, order.last), n_head)
            beside = [o_moving[0].flying, cot_moving.flying, out_far]
        if c < CHUNKS - 1:
            beside.append(gather_far(after(part(x_own, c + 1), order.last), n_head))
        (buffers, (o_chunk, near, far_blocks)), beside = order.run(
            lambda w: attend_chunk(
                c, x_pieces[c], w, cosine, sine, gain, starts, info, buffers, row_len, chunk_len
            ),
            w_t,
            need=x_pieces[c],
            beside=beside,
        )
        o_own.append(o_chunk)
        o_moving.append(Exchange(near, far_blocks, n_head))
        if c < CHUNKS - 1:
            x_far = beside[-1]
        if c == 0:
            out_far = {e: (v, swap(v, "batch", 1, n_batch)) for e, v in beside[0].items()}
        else:
            o_first = o_moving[0].finish(beside[0])
            cot_blocks = cot_moving.finish(beside[1])
            out_far = beside[2]

    out_far = {
        e: jnp.where(
            bit == 0, jnp.concatenate([v, w], axis=1), jnp.concatenate([w, v], axis=1)
        )
        for e, (v, w) in out_far.items()
    }
    out_far[0] = w_out
    out_pieces = gather_near(out_far, n_head)

    state, joined, h_far, h_fars = [], [], None, []
    o_came = o_first
    for c in chunks:
        o_pieces = [o_own[c]] + o_came
        beside = [h_far, o_moving[c + 1].flying if c < CHUNKS - 1 else None]
        (joined, y, x_rows, h_one, h_low), beside = order.run(
            lambda first: project(
                c,
                joined,
                [first] + o_pieces[1:],
                out_pieces,
                x_pieces[c],
                attn_alpha,
                info,
                chunk_len,
            ),
            o_pieces[0],
            need=o_pieces[1:] + out_pieces,
            beside=beside,
        )
        joined = [joined]
        if c < CHUNKS - 1:
            o_came = o_moving[c + 1].finish(beside[1])
        if c:
            h_fars = [beside[0]]
        state.append((y, x_rows, h_one))
        h_far = gather_far(h_low, n_head)
    cot_pieces = [cot_own] + cot_blocks

    fed, raws, z_terms, sent = [], [], None, None
    for c in chunks:
        h_pieces = gather_near(h_fars[c] if c < len(h_fars) else h_far, n_head)
        beside = [h_far if c < CHUNKS - 1 else None, z_terms]
        (kept, raw, z_even, z_odd), (h_next, z_done) = order.run(
            lambda first: feed(
                [first] + h_pieces[1:], w_up, w_gate, w_down, up_scale, gate_scale
            ),
            h_pieces[0],
            need=h_pieces[1:] + [sent],
            beside=beside,
        )
        if c < CHUNKS - 1:
            h_far = h_next
        fed.append(kept)
        raws.append(raw)
        z_near = reduce_near(z_odd, n_head)
        if c < CHUNKS - 1:
            z_terms, sent = reduce_far(z_even, z_near, n_head)

    two = []

    def mid_step(c, terms, beside, need=()):
        nonlocal two
        (two, dz, direct, alpha_sum), beside = order.run(
            lambda first: middle(
                c, two, [first] + terms[1:], cot_pieces, state[c][2], ffn_alpha, info
            ),
            terms[0],
            need=terms[1:] + list(need),
            beside=beside,
        )
        return dz, direct, alpha_sum, beside

    def unfeed_step(c, dz_pieces, beside, need=()):
        return order.run(
            lambda first: unfeed(
                [first] + dz_pieces[1:],
                *raws[c],
                w_up,
                w_gate,
                w_down,
                up_scale,
                gate_scale,
                n_head,
            ),
            dz_pieces[0],
            need=dz_pieces[1:] + list(need),
            beside=beside,
        )

    dz, direct, alpha_sum, z_near = mid_step(0, z_done, z_near)
    directs, ffn_alphas = [direct], [alpha_sum]
    dz_far = gather_far(dz, n_head)
    z_even = [z_even[0]] + [after(p, dz_far[far]) for p in z_even[1:]]
    z_terms, sent = reduce_far(z_even, z_near, n_head)
    dz_pieces = gather_near(dz_far, n_head)
    (low_first, scales_first, dh_even, dh_odd, dz_first), z_terms = unfeed_step(
        0, dz_pieces, z_terms, need=[sent]
    )
    dh_near = reduce_near(dh_odd, n_head)
    dz, direct, alpha_sum, dh_near = mid_step(1, z_terms, dh_near)
    directs.append(direct)
    ffn_alphas.append(alpha_sum)
    dz_far = gather_far(dz, n_head)
    firsts, dz_far = order.run(
        lambda v: weigh_feed(v, fed[0][1], dz_first, *low_first), fed[0][0], beside=dz_far
    )
    dz_pieces = gather_near(dz_far, n_head)
    dh_even = [dh_even[0]] + [after(p, dz_far[far]) for p in dh_even[1:]]
    dh_terms, sent = reduce_far(dh_even, dh_near, n_head)
    dz_last, _ = order.run(
        lambda first: join([first] + dz_pieces[1:]), dz_pieces[0], need=dz_pieces[1:] + [sent]
    )
    grad_down, _ = order.run(
        lambda v: (firsts[0] + dot(fed[1][0], v, 0, 0)).astype(BF16), dz_last
    )
    sum_down = BatchSum(grad_down, n_batch)
    (low_last, scales_last, dh_even, dh_odd, _), dh_terms = unfeed_step(
        1, [dz_last], dh_terms, need=[sum_down.sent]
    )
    scale_sums = [jnp.concatenate(s, axis=0) for s in (scales_first, scales_last)]
    dh_near = reduce_near(dh_odd, n_head)

    zeros, alphas, dys = [], [], []

    def back(c, terms, beside, need=()):
        y, x_rows, _ = state[c]
        (dy, d_pieces, zero, grad_alpha_attn), beside = order.run(
            lambda first: unproject(
                c, dys, [first] + terms[1:], out_pieces, directs[c], y, x_rows, attn_alpha
            ),
            terms[0],
            need=terms[1:] + list(need),
            beside=beside,
        )
        dys[:] = [dy]
        zeros.append(zero)
        alphas.append(grad_alpha_attn)
        return d_pieces[0], Exchange(d_pieces[1], d_pieces[2], n_head), beside

    def beside_sums(step, value, sums, beside=(), need=()):
        out, (got, beside) = order.run(
            step, value, need=need, beside=([b.flying for b in sums], beside)
        )
        for b, v in zip(sums, got, strict=True):
            b.advance(v)
        return out, beside

    grad_up, dh_near = beside_sums(
        lambda v: (firsts[1] + dot(fed[1][1], v, 0, 0)).astype(BF16),
        low_last[0],
        [sum_down],
        dh_near,
    )
    sum_up = BatchSum(grad_up, n_batch)
    dh_first, (dh_terms, sent) = dh_terms, reduce_far(dh_even, dh_near, n_head)
    grad_gate, _ = order.run(
        lambda v: (firsts[2] + dot(fed[1][1], v, 0, 0)).astype(BF16),
        low_last[1],
        need=[sent, sum_down.sent, sum_up.sent],
    )
    do_own, do_first, (dh_terms, got) = back(0, dh_first, (dh_terms, sum_down.flying))
    sum_down.advance(got)
    do_pieces = [do_own]
    do_own, do_last, do_came = back(1, dh_terms, do_first.flying, need=[sum_down.sent])
    do_pieces += do_first.finish(do_came)
    out_terms, do_came = beside_sums(
        lambda o: dot(o, dys[0], 0, 0).astype(BF16),
        joined[0],
        [sum_down, sum_up],
        do_last.flying,
    )
    sum_gate = BatchSum(after(grad_gate, order.last), n_batch)
    do_pieces += [do_own] + do_last.finish(do_came)
    alpha_sums = jnp.concatenate([sum(alphas), sum(ffn_alphas)], axis=0)
    alpha_rows = jnp.pad(alpha_sums.astype(BF16), ((0, 14), (0, 0)))
    out_blocks = [
        jnp.concatenate([out_terms[e * cols : (e + 1) * cols], alpha_rows], axis=0)
        for e in range(n_head)
    ]
    out_near = reduce_near(out_blocks[1::2], n_head)
    d_all, gains = [], []

    def attention_back(g, sums, beside, need=()):
        (d_pair, grad_gain), beside = beside_sums(
            lambda first: unattend(
                g, [first] + do_pieces[1:], buffers, starts, cosine, sine, gain, info, n_head
            ),
            do_pieces[0],
            sums,
            beside,
            need=do_pieces[1:] + list(need),
        )
        d_pair = d_pair.reshape(3 * pair, row_len)
        d_all.append(d_pair)
        gains.append(grad_gain[:, 0])
        return d_pair, beside

    big = [sum_down, sum_up, sum_gate]
    grads = []
    if pairs > 1:
        d_pair, out_near = attention_back(
            0, [sum_down, sum_up], out_near, need=[b.sent for b in big]
        )
        out_flying, out_sent = reduce_far(out_blocks[::2], out_near, n_head)
        grad_pair, _ = beside_sums(
            lambda d: weigh(d, x_pieces, chunk_len),
            d_pair,
            [sum_gate],
            need=[sum_down.sent, sum_up.sent, out_sent],
        )
        grads.append(grad_pair)
    else:
        out_flying, _ = reduce_far(out_blocks[::2], out_near, n_head)
    ahead = [BatchSum(g, n_batch) for g in grads] if n_batch == 8 else []
    d_pair, out_flying = attention_back(
        pairs - 1, big + ahead, out_flying, need=[sum_gate.sent] + [b.sent for b in ahead]
    )
    out_sum = term_sum(out_flying)
    grad_pair, _ = order.run(
        lambda d: weigh(d, x_pieces, chunk_len), d_pair, need=[sum_down.sent, sum_up.sent, sum_gate.sent]
    )
    small = jnp.concatenate(
        [out_sum[cols : cols + 2]]
        + [
            jnp.pad(v, ((0, 0), (0, model - v.shape[1])))
            for v in (sum(scale_sums), jnp.concatenate(gains)[None])
        ],
        axis=0,
    )
    small = jnp.pad(small, ((0, -(4 * cols + 5) % (16 * n_batch)), (0, 0)))
    if ahead:
        grads = []
    grads += [grad_pair, out_sum[:cols].astype(BF16), small.astype(BF16)]
    grads = jnp.concatenate(grads, axis=0)
    ranges = [2 * b.values.shape[0] for b in ahead] + [grads.shape[0]]
    sum_attn = BatchSum(grads, n_batch, direct=True, before=[b.values for b in ahead])

    def spread_step(c, sums, beside=(), need=()):
        return beside_sums(
            lambda w: spread(c, chunk_len, d_all, w, zeros[c], info, n_head),
            w_t,
            sums,
            beside,
            need=need,
        )

    def land(sums, beside=()):
        got, beside = lax.optimization_barrier(([b.flying for b in sums], beside))
        for i, (b, v) in enumerate(zip(sums, got, strict=True)):
            b.advance(after(v, sums[0].sent) if i else v)
        return jax.tree.map(lambda v: after(v, sums[0].sent), beside)

    two_moving = Exchange(after(two[1], order.last), after(two[2], order.last), n_head)
    d_first, two_came = spread_step(
        0, [sum_up, sum_gate, sum_down], two_moving.flying, need=[sum_attn.sent]
    )
    two_pieces = two_moving.finish(two_came)
    dx_near = reduce_near(d_first[-1], n_head)
    d_last, dx_near = spread_step(
        1, [sum_attn, sum_up, sum_gate], dx_near, need=[sum_up.sent, sum_gate.sent]
    )
    dx_first, _ = reduce_far(d_first[:-1], dx_near, n_head)
    down_done = assemble(sum_down.finish(), place)
    land([sum_attn, sum_up, sum_gate])
    dx_first = land([sum_attn, sum_gate], dx_first)
    dx_near = reduce_near(after(d_last[-1], sum_attn.sent), n_head)
    dx_last, _ = reduce_far(d_last[:-1], dx_near, n_head)
    while len(sum_attn.todo) > 1:
        land([sum_attn])
    hidden_out = settle(two[0], two_pieces, info)
    grad_down = down_done
    grad_up = assemble(sum_up.finish(), place)
    grad_gate = assemble(sum_gate.finish(), place)
    grad_query, grad_key, grad_value, grad_out, small = assemble_turned(
        sum_attn.finish(), place, info, cols, n_head, pairs, ranges
    )
    grad_hidden = jnp.concatenate([term_sum(dx_first), term_sum(dx_last)], axis=0)[None]
    alpha_own = lax.dynamic_slice_in_dim(small[:2], me * share, share, 1)
    hidden_units = w_up.shape[1]

    return (
        hidden_out[None],
        grad_hidden,
        grad_query,
        grad_key,
        grad_value,
        grad_out,
        grad_up,
        grad_gate,
        grad_down,
        small[4, :cols],
        small[2, :hidden_units],
        small[3, :hidden_units],
        alpha_own[0],
        alpha_own[1],
    )


def solution(mesh):
    split = P("batch", None, "head")
    by_col, by_row, by_head = P(None, "head"), P("head", None), P("head")
    return jax.shard_map(
        functools.partial(on_device, mesh.shape["batch"], mesh.shape["head"]),
        mesh=mesh,
        in_specs=(split, split, P("batch", None), P("batch"))
        + (by_col, by_col, by_col, by_row, by_col, by_col, by_row)
        + (by_head, by_head, by_head, P(), P()),
        out_specs=(split, split, by_col, by_col, by_col, by_row, by_col, by_col, by_row)
        + (by_head,) * 5,
        check_vma=False,
    )
```

profile of v0, /device:TPU:8, one launch (start us, length us, event | category | flops | bytes accessed | tf_op | source)
XLA Modules:
  0.0 462.3 jit_solution(3876408309561545403)
XLA Ops:
  4.4 3.9 subtract_convert_fusion
  13.5 2.4 collective-permute-done.refs_2_.refs_10_
  19.5 11.2 %attend.2 = (bf16[4,2048,64]{2,1,0:T(8,128)(2,1)}, bf16[4,80,2048]{2,1,0:T(8,128)(2,1)}, bf16[4,2048,64]{2,1,0:T(8,128)(2,1)}, bf16[256,2048]{1,0:T(8,128)(2,1)}...) custom-call(s32[10]{0:T(128)S(1)} %pad_add_fusion.info, ...), custom_call_target="tpu_custom_call" | custom-call | flops 8000000000 | bytes 8000000 | tf_op jit(solution)/shard_map/attend/pallas_call | solution.py:473
  30.8 6.2 %collective-permute-done.4.refs_2_.refs_10_.refs_6_ = bf16[1024,256]{1,0:T(8,128)(2,1)} collective-permute-done((bf16[1024,256]{1,0:T(8,128)(2,1)S(1)}, bf16[1024,256]{1,0:T(8,128)(2,1)}, u32[]{:S(2)}, u32[]{:S(2)}) %collective-permute-start.4) | collective-permute-done | bytes 524320 | tf_op jit(solution)/shard_map/ppermute | solution.py:77
  43.5 16.7 %attend.3 = (bf16[4,2048,64]{2,1,0:T(8,128)(2,1)}, bf16[4,80,2048]{2,1,0:T(8,128)(2,1)}, bf16[4,2048,64]{2,1,0:T(8,128)(2,1)}, bf16[256,2048]{1,0:T(8,128)(2,1)}...) custom-call(s32[10]{0:T(128)S(1)} %pad_add_fusion.info, ...), custom_call_target="tpu_custom_call", output_to_operand_aliasing={{0}: (10, {}), {1}: (11, {}), {2}: (12, {}), {3}: (13, {}),... | custom-call | flops 8000000000 | bytes 8000000 | tf_op jit(solution)/shard_map/attend/pallas_call | solution.py:473
  64.2 3.0 project.2
  67.2 2.8 collective-permute-done.16
  73.0 4.0 project.3
  77.0 6.6 %collective-permute-done.18.refs_2_ = bf16[256,1024]{1,0:T(8,128)(2,1)S(1)} collective-permute-done((bf16[256,1024]{1,0:T(8,128)(2,1)S(1)}, bf16[256,1024]{1,0:T(8,128)(2,1)S(1)}, u32[]{:S(2)}, u32[]{:S(2)}) %collective-permute-start.18) | collective-permute-done | bytes 524320 | tf_op jit(solution)/shard_map/ppermute | solution.py:77
  86.2 10.7 %feed.2 = (bf16[1024,1024]{1,0:T(8,128)(2,1)}, bf16[1024,1024]{1,0:T(8,128)(2,1)}, bf16[1024,1024]{1,0:T(8,128)(2,1)}, bf16[1024,1024]{1,0:T(8,128)(2,1)}, bf16[...) custom-call(bf16[256,1024]{1,0:T(8,128)(2,1)S(1)} %get-tuple-element, ...), custom_call_target="tpu_custom_call" | custom-call | flops 6442450944 | bytes 20000000 | tf_op jit(solution)/shard_map/feed/pallas_call | solution.py:736
  101.6 10.7 %feed.3 = (bf16[1024,1024]{1,0:T(8,128)(2,1)}, bf16[1024,1024]{1,0:T(8,128)(2,1)}, bf16[1024,1024]{1,0:T(8,128)(2,1)}, bf16[1024,1024]{1,0:T(8,128)(2,1)}, bf16[...) custom-call(bf16[256,1024]{1,0:T(8,128)(2,1)S(1)} %get-tuple-element, ...), custom_call_target="tpu_custom_call" | custom-call | flops 6442450944 | bytes 20000000 | tf_op jit(solution)/shard_map/feed/pallas_call | solution.py:736
  112.3 1.7 collective-permute-done.26.refs_2_
  114.6 2.4 collective-permute-done.27.refs_6_
  117.0 4.2 middle.2
  122.8 12.5 %collective-permute-done.31.refs_2_ = bf16[256,1024]{1,0:T(8,128)(2,1)S(1)} collective-permute-done((bf16[256,1024]{1,0:T(8,128)(2,1)S(1)}, bf16[256,1024]{1,0:T(8,128)(2,1)S(1)}, u32[]{:S(2)}, u32[]{:S(2)}) %collective-permute-start.31) | collective-permute-done | bytes 524320 | tf_op jit(solution)/shard_map/ppermute | solution.py:77
  137.2 25.0 %unfeed.2 = (bf16[1024,1024]{1,0:T(8,128)(2,1)}, bf16[1024,1024]{1,0:T(8,128)(2,1)}, f32[1,1024]{1,0:T(1,128)S(1)}, f32[1,1024]{1,0:T(1,128)S(1)}, bf16[256,1024...) custom-call(bf16[256,1024]{1,0:T(8,128)(2,1)S(1)} %get-tuple-element, ...), custom_call_target="tpu_custom_call" | custom-call | flops 6442450944 | bytes 20000000 | tf_op jit(solution)/shard_map/unfeed/pallas_call | solution.py:958
  162.9 4.8 %middle.3 = (bf16[512,256]{1,0:T(8,128)(2,1)}, bf16[512,256]{1,0:T(8,128)(2,1)}, bf16[2,512,256]{2,1,0:T(8,128)(2,1)}, bf16[256,1024]{1,0:T(8,128)(2,1)}, f32[256,1024]{1,0:T(8,128)}, /*index=5*/f32[1,1024]{1,0:T(1,128)S(1)}) custom-call(s32[10]{0:T(128)S(1)} %pad_add_fusion.info, ...), custom_call_target="tpu_custom_call", output_to_operand_aliasing={{0}: (10, {}), {1}: (11, {}), {2}: (12, {})} | custom-call | flops 15728640 | bytes 6291456 | tf_op jit(solution)/shard_map/middle/pallas_call | solution.py:796
  169.9 10.9 %weigh_feed.1 = (f32[1024,1024]{1,0:T(8,128)}, f32[1024,1024]{1,0:T(8,128)}, f32[1024,1024]{1,0:T(8,128)}) custom-call(bf16[1024,1024]{1,0:T(8,128)(2,1)S(1)} %copy-done.77, bf16[1024,1024]{1,0:T(8,128)(2,1)S(1)} %copy-done.78, bf16[1024,1024]{1,0:T(8,128)(2,1)} %get-tuple-element.514.z_ref, bf16[1024,1024]{1,0:T(8,128)(2,1)} %get-tuple-element.496.u_ref, ...), custom_call_target="tpu_custom_call" | custom-call | flops 6442450944 | bytes 20000000 | tf_op jit(solution)/shard_map/weigh_feed/pallas_call | solution.py:853
  180.8 2.0 collective-permute-done.36.refs_2_
  188.1 4.0 add_convert_fusion.2
  192.8 13.2 %unfeed.3 = (bf16[1024,1024]{1,0:T(8,128)(2,1)}, bf16[1024,1024]{1,0:T(8,128)(2,1)}, f32[1,1024]{1,0:T(1,128)S(1)}, f32[1,1024]{1,0:T(1,128)S(1)}, bf16[256,1024...) custom-call(bf16[1024,1024]{1,0:T(8,128)(2,1)S(1)} %join.1.refs_0_, ...), custom_call_target="tpu_custom_call" | custom-call | flops 6442450944 | bytes 20000000 | tf_op jit(solution)/shard_map/unfeed/pallas_call | solution.py:958
  206.6 4.2 fusion.28
  212.1 5.2 %collective-permute-done.40 = bf16[512,1024]{1,0:T(8,128)(2,1)S(1)} collective-permute-done((bf16[512,1024]{1,0:T(8,128)(2,1)S(1)}, bf16[512,1024]{1,0:T(8,128)(2,1)S(1)}, u32[]{:S(2)}, u32[]{:S(2)}) %collective-permute-start.40) | collective-permute-done | bytes 1048608 | tf_op jit(solution)/shard_map/ppermute | solution.py:77
  220.3 2.5 fusion.29
  224.3 4.4 unproject.2
  228.7 2.0 collective-permute-done.44
  232.5 2.5 collective-permute-start.47
  235.1 4.4 unproject.3
  241.1 2.7 convolution_convert_fusion
  243.8 3.1 collective-permute-done.47
  249.6 1.7 collective-permute-start.54
  252.9 16.9 %unattend.2 = (bf16[3,128,2048]{2,1,0:T(8,128)(2,1)}, f32[128,1]{1,0:T(8,128)S(1)}) custom-call(s32[10]{0:T(128)S(1)} %pad_add_fusion.info, bf16[256,256]{1,0:T(8,128)(2,1)S(1)} %get-tuple-element.620.refs_0_, bf16[256,256]{1,0:T(8,128)(2,1)S(1)} %collective-permute-done.45.refs_1_, bf16[256,256]{1,0:T(8,128)(2,1)S(1)} %get-tuple-element.715.refs_2_, ...), custom_call_target="tpu_custom_call" | custom-call | flops 22000001024 | bytes 6000000 | tf_op jit(solution)/shard_map/unattend/pallas_call | solution.py:601
  271.6 2.9 collective-permute-start.59
  274.7 3.0 weigh.2
  278.3 2.0 collective-permute-start.60
  280.4 17.1 %unattend.3 = (bf16[3,128,2048]{2,1,0:T(8,128)(2,1)}, f32[128,1]{1,0:T(8,128)S(1)}) custom-call(s32[10]{0:T(128)S(1)} %pad_add_fusion.info, bf16[256,256]{1,0:T(8,128)(2,1)S(1)} %get-tuple-element.620.refs_0_, bf16[256,256]{1,0:T(8,128)(2,1)S(1)} %collective-permute-done.45.refs_1_, bf16[256,256]{1,0:T(8,128)(2,1)S(1)} %get-tuple-element.715.refs_2_, ...), custom_call_target="tpu_custom_call" | custom-call | flops 22000001024 | bytes 6000000 | tf_op jit(solution)/shard_map/unattend/pallas_call | solution.py:601
  297.5 4.6 collective-permute-done.60
  302.4 2.2 collective-permute-start.65
  306.0 2.2 collective-permute-start.63
  308.2 3.1 weigh.3
  314.9 7.5 %spread.2 = (bf16[1024,256]{1,0:T(8,128)(2,1)S(1)}, bf16[1024,256]{1,0:T(8,128)(2,1)S(1)}, bf16[2,1024,256]{2,1,0:T(8,128)(2,1)}) custom-call(s32[10]{0:T(128)S(1)} %pad_add_fusion.info, bf16[384,2048]{1,0:T(8,128)(2,1)S(1)} %bitcast.76, bf16[384,2048]{1,0:T(8,128)(2,1)S(1)} %bitcast.79, bf16[768,1024]{1,0:T(8,128)(2,1)S(1)} %copy-done.67, ...), custom_call_target="tpu_custom_call" | custom-call | flops 1610612736 | bytes 8000000 | tf_op jit(solution)/shard_map/spread/pallas_call | solution.py:1073
  324.7 2.3 collective-permute-done.63
  330.1 2.9 collective-permute-start.70
  337.0 7.7 %spread.3 = (bf16[1024,256]{1,0:T(8,128)(2,1)S(1)}, bf16[1024,256]{1,0:T(8,128)(2,1)S(1)}, bf16[2,1024,256]{2,1,0:T(8,128)(2,1)}) custom-call(s32[10]{0:T(128)S(1)} %pad_add_fusion.info, bf16[384,2048]{1,0:T(8,128)(2,1)S(1)} %bitcast.77, bf16[384,2048]{1,0:T(8,128)(2,1)S(1)} %bitcast.80, bf16[768,1024]{1,0:T(8,128)(2,1)S(1)} %copy-done.68, ...), custom_call_target="tpu_custom_call" | custom-call | flops 1610612736 | bytes 8000000 | tf_op jit(solution)/shard_map/spread/pallas_call | solution.py:1073
  344.8 3.5 collective-permute-done.69
  348.4 3.3 collective-permute-done.71
  354.1 1.9 pad_maximum_fusion.10
  356.0 2.0 collective-permute-start.77
  361.1 1.7 collective-permute-start.74
  362.8 1.7 collective-permute-start.75
  364.5 17.3 %collective-permute-done.73 = bf16[144,1024]{1,0:T(8,128)(2,1)} collective-permute-done((bf16[144,1024]{1,0:T(8,128)(2,1)}, bf16[144,1024]{1,0:T(8,128)(2,1)}, u32[]{:S(2)}, u32[]{:S(2)}) %collective-permute-start.73) | collective-permute-done | bytes 294944 | tf_op jit(solution)/shard_map/ppermute | solution.py:77
  381.9 3.1 collective-permute-done.74
  385.0 1.9 add_convert_fusion.17
  391.0 6.2 %collective-permute-start.78 = (bf16[144,1024]{1,0:T(8,128)(2,1)S(1)}, bf16[144,1024]{1,0:T(8,128)(2,1)S(1)}, u32[]{:S(2)}, u32[]{:S(2)}) collective-permute-start(bf16[144,1024]{1,0:T(8,128)(2,1)S(1)} %add_convert_fusion.17), channel_id=1, source_target_pairs={{0,8},{4,12},{8,0},{12,4},{16,24},{20,28},{24,16},{28,20},{1,9},{5... | collective-permute-start | bytes 884744 | tf_op jit(solution)/shard_map/ppermute | solution.py:77
  398.7 1.9 slice_bitcast_fusion.2
  400.7 6.6 %collective-permute-done.78 = bf16[144,1024]{1,0:T(8,128)(2,1)S(1)} collective-permute-done((bf16[144,1024]{1,0:T(8,128)(2,1)S(1)}, bf16[144,1024]{1,0:T(8,128)(2,1)S(1)}, u32[]{:S(2)}, u32[]{:S(2)}) %collective-permute-start.78) | collective-permute-done | bytes 294944 | tf_op jit(solution)/shard_map/ppermute | solution.py:77
  407.3 10.4 %collective-permute-done.79 = bf16[144,1024]{1,0:T(8,128)(2,1)S(1)} collective-permute-done((bf16[144,1024]{1,0:T(8,128)(2,1)S(1)}, bf16[144,1024]{1,0:T(8,128)(2,1)S(1)}, u32[]{:S(2)}, u32[]{:S(2)}) %collective-permute-start.79) | collective-permute-done | bytes 294944 | tf_op jit(solution)/shard_map/ppermute | solution.py:77
  417.7 5.1 %collective-permute-done.80 = bf16[144,1024]{1,0:T(8,128)(2,1)S(1)} collective-permute-done((bf16[144,1024]{1,0:T(8,128)(2,1)S(1)}, bf16[144,1024]{1,0:T(8,128)(2,1)S(1)}, u32[]{:S(2)}, u32[]{:S(2)}) %collective-permute-start.80) | collective-permute-done | bytes 294944 | tf_op jit(solution)/shard_map/ppermute | solution.py:77
  427.4 2.3 assemble.5
  429.8 2.5 settle.1
  432.3 2.3 assemble.3
  434.7 2.3 assemble.4
  439.4 13.1 %collective-permute-done.85.other_ref = bf16[576,1024]{1,0:T(8,128)(2,1)} collective-permute-done((bf16[576,1024]{1,0:T(8,128)(2,1)S(1)}, bf16[576,1024]{1,0:T(8,128)(2,1)}, u32[]{:S(2)}, u32[]{:S(2)}) %collective-permute-start.85) | collective-permute-done | bytes 1179680 | tf_op jit(solution)/shard_map/ppermute | solution.py:77
  452.4 5.1 %assemble_turned.1 = (f32[1024,256]{1,0:T(8,128)}, f32[1024,256]{1,0:T(8,128)}, f32[1024,256]{1,0:T(8,128)}, f32[256,1024]{1,0:T(8,128)}, f32[8,1024]{1,0:T(8,128)S(1)}) custom-call(s32[1]{0:T(128)} %bitcast.32.place, s32[10]{0:T(128)S(1)} %pad_add_fusion.info, bf16[576,1024]{1,0:T(8,128)(2,1)S(1)} %pad_maximum_fusion.own_ref, ...), custom_call_target="tpu_custom_call" | custom-call | bytes 6291456 | tf_op jit(solution)/shard_map/assemble_turned/pallas_call | solution.py:277
  (446 shorter events, 99.0 us)
Async XLA Ops:
  2.1 13.7 %collective-permute-start = (bf16[1024,256]{1,0:T(8,128)(2,1)S(1)}, bf16[1024,256]{1,0:T(8,128)(2,1)S(1)}, u32[]{:S(2)}, u32[]{:S(2)}) collective-permute-start(bf16[1024,256]{1,0:T(8,128)(2,1)S(1)} %get-tuple-element.357.refs_0_.refs_8_), channel_id=1, source_target_pairs={{0,2},{1,3},{2,0},{3,1},{4,6},{5,7},{6,4},{7,5},{8,10},{9,11},{10,... | collective-permute-start | bytes 1572872 | tf_op jit(solution)/shard_map/ppermute | solution.py:77
  17.4 13.4 %collective-permute-start.3 = (bf16[256,512]{1,0:T(8,128)(2,1)S(1)}, bf16[256,512]{1,0:T(8,128)(2,1)S(1)}, u32[]{:S(2)}, u32[]{:S(2)}) collective-permute-start(bf16[256,512]{1,0:T(8,128)(2,1)S(1)} %get-tuple-element.374), channel_id=1, source_target_pairs={{0,2},{1,3},{2,0},{3,1},{4,6},{5,7},{6,4},{7,5},{8,10},{9,11},{10,... | collective-permute-start | bytes 786440 | tf_op jit(solution)/shard_map/ppermute | solution.py:77
  19.0 18.0 %collective-permute-start.4 = (bf16[1024,256]{1,0:T(8,128)(2,1)S(1)}, bf16[1024,256]{1,0:T(8,128)(2,1)}, u32[]{:S(2)}, u32[]{:S(2)}) collective-permute-start(bf16[1024,256]{1,0:T(8,128)(2,1)S(1)} %get-tuple-element.376.refs_0_.refs_8_.refs_4_), channel_id=1, source_target_pairs={{0,2},{1,3},{2,0},{3,1},{4,6},{5,7},{6,4},{7,5},{8,10},{9,11},{10,... | collective-permute-start | bytes 1572872 | tf_op jit(solution)/shard_map/ppermute | solution.py:77
  37.5 23.3 %collective-permute-start.10 = (bf16[2,512,256]{2,1,0:T(8,128)(2,1)}, bf16[2,512,256]{2,1,0:T(8,128)(2,1)S(1)}, u32[]{:S(2)}, u32[]{:S(2)}) collective-permute-start(bf16[2,512,256]{2,1,0:T(8,128)(2,1)} %copy-done.71), channel_id=1, source_target_pairs={{0,2},{1,3},{2,0},{3,1},{4,6},{5,7},{6,4},{7,5},{8,10},{9,11},{10,... | collective-permute-start | bytes 1572872 | tf_op jit(solution)/shard_map/ppermute | solution.py:77
  39.1 21.7 %collective-permute-start.9 = (bf16[512,256]{1,0:T(8,128)(2,1)}, bf16[512,256]{1,0:T(8,128)(2,1)S(1)}, u32[]{:S(2)}, u32[]{:S(2)}) collective-permute-start(bf16[512,256]{1,0:T(8,128)(2,1)} %copy-done.72), channel_id=1, source_target_pairs={{0,1},{1,0},{2,3},{3,2},{4,5},{5,4},{6,7},{7,6},{8,9},{9,8},{10,11... | collective-permute-start | bytes 786440 | tf_op jit(solution)/shard_map/ppermute | solution.py:77
  39.1 21.7 %collective-permute-start.11 = (bf16[256,512]{1,0:T(8,128)(2,1)}, bf16[256,512]{1,0:T(8,128)(2,1)S(1)}, u32[]{:S(2)}, u32[]{:S(2)}) collective-permute-start(bf16[256,512]{1,0:T(8,128)(2,1)} %copy-done.106), channel_id=1, source_target_pairs={{0,4},{4,0},{8,12},{12,8},{16,20},{20,16},{24,28},{28,24},{1,5},{5... | collective-permute-start | bytes 786440 | tf_op jit(solution)/shard_map/ppermute | solution.py:77
  40.6 20.2 %collective-permute-start.8 = (bf16[2,256,256]{2,1,0:T(8,128)(2,1)}, bf16[2,256,256]{2,1,0:T(8,128)(2,1)S(1)}, u32[]{:S(2)}, u32[]{:S(2)}) collective-permute-start(bf16[2,256,256]{2,1,0:T(8,128)(2,1)} %get-tuple-element.400), channel_id=1, source_target_pairs={{0,2},{1,3},{2,0},{3,1},{4,6},{5,7},{6,4},{7,5},{8,10},{9,11},{10,... | collective-permute-start | bytes 786440 | tf_op jit(solution)/shard_map/ppermute | solution.py:77
  41.1 19.1 %collective-permute-start.7 = (bf16[256,256]{1,0:T(8,128)(2,1)}, bf16[256,256]{1,0:T(8,128)(2,1)S(1)}, u32[]{:S(2)}, u32[]{:S(2)}) collective-permute-start(bf16[256,256]{1,0:T(8,128)(2,1)} %get-tuple-element.399), channel_id=1, source_target_pairs={{0,1},{1,0},{2,3},{3,2},{4,5},{5,4},{6,7},{7,6},{8,9},{9,8},{10,11... | collective-permute-start | bytes 393224 | tf_op jit(solution)/shard_map/ppermute | solution.py:77
  61.1 8.9 %collective-permute-start.16 = (bf16[2,256,256]{2,1,0:T(8,128)(2,1)}, bf16[2,256,256]{2,1,0:T(8,128)(2,1)S(1)}, u32[]{:S(2)}, u32[]{:S(2)}) collective-permute-start(bf16[2,256,256]{2,1,0:T(8,128)(2,1)} %get-tuple-element.420), channel_id=1, source_target_pairs={{0,2},{1,3},{2,0},{3,1},{4,6},{5,7},{6,4},{7,5},{8,10},{9,11},{10,... | collective-permute-start | bytes 786440 | tf_op jit(solution)/shard_map/ppermute | solution.py:77
  70.0 13.5 %collective-permute-start.18 = (bf16[256,1024]{1,0:T(8,128)(2,1)S(1)}, bf16[256,1024]{1,0:T(8,128)(2,1)S(1)}, u32[]{:S(2)}, u32[]{:S(2)}) collective-permute-start(bf16[256,1024]{1,0:T(8,128)(2,1)S(1)} %get-tuple-element.434.refs_0_), channel_id=1, source_target_pairs={{0,2},{1,3},{2,0},{3,1},{4,6},{5,7},{6,4},{7,5},{8,10},{9,11},{10,... | collective-permute-start | bytes 1572872 | tf_op jit(solution)/shard_map/ppermute | solution.py:77
  84.0 13.8 %collective-permute-start.21 = (bf16[256,1024]{1,0:T(8,128)(2,1)S(1)}, bf16[256,1024]{1,0:T(8,128)(2,1)S(1)}, u32[]{:S(2)}, u32[]{:S(2)}) collective-permute-start(bf16[256,1024]{1,0:T(8,128)(2,1)S(1)} %get-tuple-element.449.refs_0_), channel_id=1, source_target_pairs={{0,2},{1,3},{2,0},{3,1},{4,6},{5,7},{6,4},{7,5},{8,10},{9,11},{10,... | collective-permute-start | bytes 1572872 | tf_op jit(solution)/shard_map/ppermute | solution.py:77
  98.4 13.9 %collective-permute-start.25 = (bf16[256,1024]{1,0:T(8,128)(2,1)S(1)}, bf16[256,1024]{1,0:T(8,128)(2,1)S(1)}, u32[]{:S(2)}, u32[]{:S(2)}) collective-permute-start(bf16[256,1024]{1,0:T(8,128)(2,1)S(1)} %get-tuple-element.459), channel_id=1, source_target_pairs={{0,1},{1,0},{2,3},{3,2},{4,5},{5,4},{6,7},{7,6},{8,9},{9,8},{10,11... | collective-permute-start | bytes 1572872 | tf_op jit(solution)/shard_map/ppermute | solution.py:77
  100.0 14.0 %collective-permute-start.26 = (bf16[256,1024]{1,0:T(8,128)(2,1)S(1)}, bf16[256,1024]{1,0:T(8,128)(2,1)S(1)}, u32[]{:S(2)}, u32[]{:S(2)}) collective-permute-start(bf16[256,1024]{1,0:T(8,128)(2,1)S(1)} %add_convert_fusion.15), channel_id=1, source_target_pairs={{0,2},{1,3},{2,0},{3,1},{4,6},{5,7},{6,4},{7,5},{8,10},{9,11},{10,... | collective-permute-start | bytes 1572872 | tf_op jit(solution)/shard_map/ppermute | solution.py:77
  114.0 7.2 %collective-permute-start.28 = (bf16[256,1024]{1,0:T(8,128)(2,1)S(1)}, bf16[256,1024]{1,0:T(8,128)(2,1)S(1)}, u32[]{:S(2)}, u32[]{:S(2)}) collective-permute-start(bf16[256,1024]{1,0:T(8,128)(2,1)S(1)} %get-tuple-element.474), channel_id=1, source_target_pairs={{0,1},{1,0},{2,3},{3,2},{4,5},{5,4},{6,7},{7,6},{8,9},{9,8},{10,11... | collective-permute-start | bytes 1572872 | tf_op jit(solution)/shard_map/ppermute | solution.py:77
  114.0 7.2 %collective-permute-start.29 = (bf16[256,1024]{1,0:T(8,128)(2,1)S(1)}, bf16[256,1024]{1,0:T(8,128)(2,1)S(1)}, u32[]{:S(2)}, u32[]{:S(2)}) collective-permute-start(bf16[256,1024]{1,0:T(8,128)(2,1)S(1)} %get-tuple-element.475), channel_id=1, source_target_pairs={{0,1},{1,0},{2,3},{3,2},{4,5},{5,4},{6,7},{7,6},{8,9},{9,8},{10,11... | collective-permute-start | bytes 1572872 | tf_op jit(solution)/shard_map/ppermute | solution.py:77
  121.2 14.0 %collective-permute-start.31 = (bf16[256,1024]{1,0:T(8,128)(2,1)S(1)}, bf16[256,1024]{1,0:T(8,128)(2,1)S(1)}, u32[]{:S(2)}, u32[]{:S(2)}) collective-permute-start(bf16[256,1024]{1,0:T(8,128)(2,1)S(1)} %get-tuple-element.481.refs_0_), channel_id=1, source_target_pairs={{0,2},{1,3},{2,0},{3,1},{4,6},{5,7},{6,4},{7,5},{8,10},{9,11},{10,... | collective-permute-start | bytes 1572872 | tf_op jit(solution)/shard_map/ppermute | solution.py:77
  122.8 14.2 %collective-permute-start.30 = (bf16[256,1024]{1,0:T(8,128)(2,1)S(1)}, bf16[256,1024]{1,0:T(8,128)(2,1)S(1)}, u32[]{:S(2)}, u32[]{:S(2)}) collective-permute-start(bf16[256,1024]{1,0:T(8,128)(2,1)S(1)} %get-tuple-element.481.refs_0_), channel_id=1, source_target_pairs={{0,1},{1,0},{2,3},{3,2},{4,5},{5,4},{6,7},{7,6},{8,9},{9,8},{10,11... | collective-permute-start | bytes 1572872 | tf_op jit(solution)/shard_map/ppermute | solution.py:77
  135.5 26.8 %collective-permute-start.33 = (bf16[256,1024]{1,0:T(8,128)(2,1)S(1)}, bf16[256,1024]{1,0:T(8,128)(2,1)S(1)}, u32[]{:S(2)}, u32[]{:S(2)}) collective-permute-start(bf16[256,1024]{1,0:T(8,128)(2,1)S(1)} %add_convert_fusion.14), channel_id=1, source_target_pairs={{0,2},{1,3},{2,0},{3,1},{4,6},{5,7},{6,4},{7,5},{8,10},{9,11},{10,... | collective-permute-start | bytes 1572872 | tf_op jit(solution)/shard_map/ppermute | solution.py:77
  168.5 14.3 %collective-permute-start.36 = (bf16[256,1024]{1,0:T(8,128)(2,1)}, bf16[256,1024]{1,0:T(8,128)(2,1)S(1)}, u32[]{:S(2)}, u32[]{:S(2)}) collective-permute-start(bf16[256,1024]{1,0:T(8,128)(2,1)} %get-tuple-element.526.refs_0_), channel_id=1, source_target_pairs={{0,2},{1,3},{2,0},{3,1},{4,6},{5,7},{6,4},{7,5},{8,10},{9,11},{10,... | collective-permute-start | bytes 1572872 | tf_op jit(solution)/shard_map/ppermute | solution.py:77
  185.2 20.8 %collective-permute-start.39 = (bf16[256,1024]{1,0:T(8,128)(2,1)S(1)}, bf16[256,1024]{1,0:T(8,128)(2,1)S(1)}, u32[]{:S(2)}, u32[]{:S(2)}) collective-permute-start(bf16[256,1024]{1,0:T(8,128)(2,1)S(1)} %add_convert_fusion.13), channel_id=1, source_target_pairs={{0,2},{1,3},{2,0},{3,1},{4,6},{5,7},{6,4},{7,5},{8,10},{9,11},{10,... | collective-permute-start | bytes 1572872 | tf_op jit(solution)/shard_map/ppermute | solution.py:77
  192.2 25.0 %collective-permute-start.40 = (bf16[512,1024]{1,0:T(8,128)(2,1)S(1)}, bf16[512,1024]{1,0:T(8,128)(2,1)S(1)}, u32[]{:S(2)}, u32[]{:S(2)}) collective-permute-start(bf16[512,1024]{1,0:T(8,128)(2,1)S(1)} %constant_dynamic-slice_fusion.11), channel_id=1, source_target_pairs={{0,4},{4,0},{8,12},{12,8},{16,20},{20,16},{24,28},{28,24},{1,5},{5... | collective-permute-start | bytes 3145736 | tf_op jit(solution)/shard_map/ppermute | solution.py:77
  206.0 6.0 %collective-permute-start.41 = (bf16[256,1024]{1,0:T(8,128)(2,1)S(1)}, bf16[256,1024]{1,0:T(8,128)(2,1)S(1)}, u32[]{:S(2)}, u32[]{:S(2)}) collective-permute-start(bf16[256,1024]{1,0:T(8,128)(2,1)S(1)} %get-tuple-element.547), channel_id=1, source_target_pairs={{0,1},{1,0},{2,3},{3,2},{4,5},{5,4},{6,7},{7,6},{8,9},{9,8},{10,11... | collective-permute-start | bytes 1572872 | tf_op jit(solution)/shard_map/ppermute | solution.py:77
  206.1 5.9 %collective-permute-start.42 = (bf16[256,1024]{1,0:T(8,128)(2,1)S(1)}, bf16[256,1024]{1,0:T(8,128)(2,1)S(1)}, u32[]{:S(2)}, u32[]{:S(2)}) collective-permute-start(bf16[256,1024]{1,0:T(8,128)(2,1)S(1)} %get-tuple-element.548), channel_id=1, source_target_pairs={{0,1},{1,0},{2,3},{3,2},{4,5},{5,4},{6,7},{7,6},{8,9},{9,8},{10,11... | collective-permute-start | bytes 1572872 | tf_op jit(solution)/shard_map/ppermute | solution.py:77
  217.8 12.9 %collective-permute-start.44 = (bf16[256,1024]{1,0:T(8,128)(2,1)S(1)}, bf16[256,1024]{1,0:T(8,128)(2,1)S(1)}, u32[]{:S(2)}, u32[]{:S(2)}) collective-permute-start(bf16[256,1024]{1,0:T(8,128)(2,1)S(1)} %constant_dynamic-slice_fusion.10), channel_id=1, source_target_pairs={{0,8},{4,12},{8,0},{12,4},{16,24},{20,28},{24,16},{28,20},{1,9},{5... | collective-permute-start | bytes 1572872 | tf_op jit(solution)/shard_map/ppermute | solution.py:77
  218.5 12.7 %collective-permute-start.43 = (bf16[256,1024]{1,0:T(8,128)(2,1)S(1)}, bf16[256,1024]{1,0:T(8,128)(2,1)S(1)}, u32[]{:S(2)}, u32[]{:S(2)}) collective-permute-start(bf16[256,1024]{1,0:T(8,128)(2,1)S(1)} %add_convert_fusion.12), channel_id=1, source_target_pairs={{0,2},{1,3},{2,0},{3,1},{4,6},{5,7},{6,4},{7,5},{8,10},{9,11},{10,... | collective-permute-start | bytes 1572872 | tf_op jit(solution)/shard_map/ppermute | solution.py:77
  219.7 27.2 %collective-permute-start.48 = (bf16[512,1024]{1,0:T(8,128)(2,1)S(1)}, bf16[512,1024]{1,0:T(8,128)(2,1)S(1)}, u32[]{:S(2)}, u32[]{:S(2)}) collective-permute-start(bf16[512,1024]{1,0:T(8,128)(2,1)S(1)} %constant_dynamic-slice_fusion.9), channel_id=1, source_target_pairs={{0,4},{4,0},{8,12},{12,8},{16,20},{20,16},{24,28},{28,24},{1,5},{5... | collective-permute-start | bytes 3145736 | tf_op jit(solution)/shard_map/ppermute | solution.py:77
  231.1 8.3 %collective-permute-start.46 = (bf16[2,256,256]{2,1,0:T(8,128)(2,1)S(1)}, bf16[2,256,256]{2,1,0:T(8,128)(2,1)S(1)}, u32[]{:S(2)}, u32[]{:S(2)}) collective-permute-start(bf16[2,256,256]{2,1,0:T(8,128)(2,1)S(1)} %get-tuple-element.585), channel_id=1, source_target_pairs={{0,2},{1,3},{2,0},{3,1},{4,6},{5,7},{6,4},{7,5},{8,10},{9,11},{10,... | collective-permute-start | bytes 786440 | tf_op jit(solution)/shard_map/ppermute | solution.py:77
  232.3 7.2 %collective-permute-start.45 = (bf16[256,256]{1,0:T(8,128)(2,1)S(1)}, bf16[256,256]{1,0:T(8,128)(2,1)S(1)}, u32[]{:S(2)}, u32[]{:S(2)}) collective-permute-start(bf16[256,256]{1,0:T(8,128)(2,1)S(1)} %get-tuple-element.584), channel_id=1, source_target_pairs={{0,1},{1,0},{2,3},{3,2},{4,5},{5,4},{6,7},{7,6},{8,9},{9,8},{10,11... | collective-permute-start | bytes 393224 | tf_op jit(solution)/shard_map/ppermute | solution.py:77
  232.5 14.4 %collective-permute-start.47 = (bf16[128,1024]{1,0:T(8,128)(2,1)S(1)}, bf16[128,1024]{1,0:T(8,128)(2,1)S(1)}, u32[]{:S(2)}, u32[]{:S(2)}) collective-permute-start(bf16[128,1024]{1,0:T(8,128)(2,1)S(1)} %constant_dynamic-slice_fusion.8), channel_id=1, source_target_pairs={{0,16},{4,20},{8,24},{12,28},{16,0},{20,4},{24,8},{28,12},{1,17},{... | collective-permute-start | bytes 786440 | tf_op jit(solution)/shard_map/ppermute | solution.py:77
  239.5 8.5 %collective-permute-start.50 = (bf16[2,256,256]{2,1,0:T(8,128)(2,1)S(1)}, bf16[2,256,256]{2,1,0:T(8,128)(2,1)S(1)}, u32[]{:S(2)}, u32[]{:S(2)}) collective-permute-start(bf16[2,256,256]{2,1,0:T(8,128)(2,1)S(1)} %get-tuple-element.589), channel_id=1, source_target_pairs={{0,2},{1,3},{2,0},{3,1},{4,6},{5,7},{6,4},{7,5},{8,10},{9,11},{10,... | collective-permute-start | bytes 786440 | tf_op jit(solution)/shard_map/ppermute | solution.py:77
  240.5 6.5 %collective-permute-start.49 = (bf16[256,256]{1,0:T(8,128)(2,1)S(1)}, bf16[256,256]{1,0:T(8,128)(2,1)S(1)}, u32[]{:S(2)}, u32[]{:S(2)}) collective-permute-start(bf16[256,256]{1,0:T(8,128)(2,1)S(1)} %get-tuple-element.588), channel_id=1, source_target_pairs={{0,1},{1,0},{2,3},{3,2},{4,5},{5,4},{6,7},{7,6},{8,9},{9,8},{10,11... | collective-permute-start | bytes 393224 | tf_op jit(solution)/shard_map/ppermute | solution.py:77
  240.5 11.0 %collective-permute-start.51 = (bf16[256,256]{1,0:T(8,128)(2,1)S(1)}, bf16[256,256]{1,0:T(8,128)(2,1)S(1)}, u32[]{:S(2)}, u32[]{:S(2)}) collective-permute-start(bf16[256,256]{1,0:T(8,128)(2,1)S(1)} %get-tuple-element.714), channel_id=1, source_target_pairs={{0,1},{1,0},{2,3},{3,2},{4,5},{5,4},{6,7},{7,6},{8,9},{9,8},{10,11... | collective-permute-start | bytes 393224 | tf_op jit(solution)/shard_map/ppermute | solution.py:77
  248.3 21.7 %collective-permute-start.55 = (bf16[272,1024]{1,0:T(8,128)(2,1)S(1)}, bf16[272,1024]{1,0:T(8,128)(2,1)S(1)}, u32[]{:S(2)}, u32[]{:S(2)}) collective-permute-start(bf16[272,1024]{1,0:T(8,128)(2,1)S(1)} %get-tuple-element.724), channel_id=1, source_target_pairs={{0,1},{1,0},{2,3},{3,2},{4,5},{5,4},{6,7},{7,6},{8,9},{9,8},{10,11... | collective-permute-start | bytes 1671176 | tf_op jit(solution)/shard_map/ppermute | solution.py:77
  248.4 21.7 %collective-permute-start.56 = (bf16[272,1024]{1,0:T(8,128)(2,1)S(1)}, bf16[272,1024]{1,0:T(8,128)(2,1)S(1)}, u32[]{:S(2)}, u32[]{:S(2)}) collective-permute-start(bf16[272,1024]{1,0:T(8,128)(2,1)S(1)} %get-tuple-element.723), channel_id=1, source_target_pairs={{0,1},{1,0},{2,3},{3,2},{4,5},{5,4},{6,7},{7,6},{8,9},{9,8},{10,11... | collective-permute-start | bytes 1671176 | tf_op jit(solution)/shard_map/ppermute | solution.py:77
  249.6 20.5 %collective-permute-start.54 = (bf16[256,1024]{1,0:T(8,128)(2,1)S(1)}, bf16[256,1024]{1,0:T(8,128)(2,1)S(1)}, u32[]{:S(2)}, u32[]{:S(2)}) collective-permute-start(bf16[256,1024]{1,0:T(8,128)(2,1)S(1)} %constant_dynamic-slice_fusion.7), channel_id=1, source_target_pairs={{0,8},{4,12},{8,0},{12,4},{16,24},{20,28},{24,16},{28,20},{1,9},{5... | collective-permute-start | bytes 1572872 | tf_op jit(solution)/shard_map/ppermute | solution.py:77
  251.5 18.6 %collective-permute-start.53 = (bf16[128,1024]{1,0:T(8,128)(2,1)S(1)}, bf16[128,1024]{1,0:T(8,128)(2,1)S(1)}, u32[]{:S(2)}, u32[]{:S(2)}) collective-permute-start(bf16[128,1024]{1,0:T(8,128)(2,1)S(1)} %add_convert_fusion.20), channel_id=1, source_target_pairs={{0,16},{4,20},{8,24},{12,28},{16,0},{20,4},{24,8},{28,12},{1,17},{... | collective-permute-start | bytes 786440 | tf_op jit(solution)/shard_map/ppermute | solution.py:77
  252.2 25.6 %collective-permute-start.57 = (bf16[512,1024]{1,0:T(8,128)(2,1)S(1)}, bf16[512,1024]{1,0:T(8,128)(2,1)S(1)}, u32[]{:S(2)}, u32[]{:S(2)}) collective-permute-start(bf16[512,1024]{1,0:T(8,128)(2,1)S(1)} %constant_dynamic-slice_fusion.6), channel_id=1, source_target_pairs={{0,4},{4,0},{8,12},{12,8},{16,20},{20,16},{24,28},{28,24},{1,5},{5... | collective-permute-start | bytes 3145736 | tf_op jit(solution)/shard_map/ppermute | solution.py:77
  270.3 27.2 %collective-permute-start.62 = (bf16[272,1024]{1,0:T(8,128)(2,1)S(1)}, bf16[272,1024]{1,0:T(8,128)(2,1)S(1)}, u32[]{:S(2)}, u32[]{:S(2)}) collective-permute-start(bf16[272,1024]{1,0:T(8,128)(2,1)S(1)} %add_convert_fusion.8), channel_id=1, source_target_pairs={{0,2},{1,3},{2,0},{3,1},{4,6},{5,7},{6,4},{7,5},{8,10},{9,11},{10,... | collective-permute-start | bytes 1671176 | tf_op jit(solution)/shard_map/ppermute | solution.py:77
  271.6 26.0 %collective-permute-start.59 = (bf16[128,1024]{1,0:T(8,128)(2,1)S(1)}, bf16[128,1024]{1,0:T(8,128)(2,1)S(1)}, u32[]{:S(2)}, u32[]{:S(2)}) collective-permute-start(bf16[128,1024]{1,0:T(8,128)(2,1)S(1)} %constant_dynamic-slice_fusion.5), channel_id=1, source_target_pairs={{0,16},{4,20},{8,24},{12,28},{16,0},{20,4},{24,8},{28,12},{1,17},{... | collective-permute-start | bytes 786440 | tf_op jit(solution)/shard_map/ppermute | solution.py:77
  274.5 23.0 %collective-permute-start.58 = (bf16[256,1024]{1,0:T(8,128)(2,1)S(1)}, bf16[256,1024]{1,0:T(8,128)(2,1)S(1)}, u32[]{:S(2)}, u32[]{:S(2)}) collective-permute-start(bf16[256,1024]{1,0:T(8,128)(2,1)S(1)} %pad_maximum_fusion.8), channel_id=1, source_target_pairs={{0,8},{4,12},{8,0},{12,4},{16,24},{20,28},{24,16},{28,20},{1,9},{5... | collective-permute-start | bytes 1572872 | tf_op jit(solution)/shard_map/ppermute | solution.py:77
  278.3 23.8 %collective-permute-start.60 = (bf16[256,1024]{1,0:T(8,128)(2,1)S(1)}, bf16[256,1024]{1,0:T(8,128)(2,1)S(1)}, u32[]{:S(2)}, u32[]{:S(2)}) collective-permute-start(bf16[256,1024]{1,0:T(8,128)(2,1)S(1)} %constant_dynamic-slice_fusion.4), channel_id=1, source_target_pairs={{0,8},{4,12},{8,0},{12,4},{16,24},{20,28},{24,16},{28,20},{1,9},{5... | collective-permute-start | bytes 1572872 | tf_op jit(solution)/shard_map/ppermute | solution.py:77
  280.4 17.2 %collective-permute-start.61 = (bf16[192,1024]{1,0:T(8,128)(2,1)S(1)}, bf16[192,1024]{1,0:T(8,128)(2,1)S(1)}, u32[]{:S(2)}, u32[]{:S(2)}) collective-permute-start(bf16[192,1024]{1,0:T(8,128)(2,1)S(1)} %constant_dynamic-slice_fusion.3), channel_id=1, source_target_pairs={{0,4},{4,0},{8,12},{12,8},{16,20},{20,16},{24,28},{28,24},{1,5},{5... | collective-permute-start | bytes 1179656 | tf_op jit(solution)/shard_map/ppermute | solution.py:77
  302.4 24.6 %collective-permute-start.65 = (bf16[512,1024]{1,0:T(8,128)(2,1)S(1)}, bf16[512,1024]{1,0:T(8,128)(2,1)S(1)}, u32[]{:S(2)}, u32[]{:S(2)}) collective-permute-start(bf16[512,1024]{1,0:T(8,128)(2,1)S(1)} %pad_maximum_fusion.5.own_ref), channel_id=1, source_target_pairs={{0,4},{4,0},{8,12},{12,8},{16,20},{20,16},{24,28},{28,24},{1,5},{5... | collective-permute-start | bytes 3145736 | tf_op jit(solution)/shard_map/ppermute | solution.py:77
  305.0 19.7 %collective-permute-start.64 = (bf16[128,1024]{1,0:T(8,128)(2,1)S(1)}, bf16[128,1024]{1,0:T(8,128)(2,1)S(1)}, u32[]{:S(2)}, u32[]{:S(2)}) collective-permute-start(bf16[128,1024]{1,0:T(8,128)(2,1)S(1)} %constant_dynamic-slice_fusion.2), channel_id=1, source_target_pairs={{0,16},{4,20},{8,24},{12,28},{16,0},{20,4},{24,8},{28,12},{1,17},{... | collective-permute-start | bytes 786440 | tf_op jit(solution)/shard_map/ppermute | solution.py:77
  306.0 21.0 %collective-permute-start.63 = (bf16[128,1024]{1,0:T(8,128)(2,1)S(1)}, bf16[128,1024]{1,0:T(8,128)(2,1)S(1)}, u32[]{:S(2)}, u32[]{:S(2)}) collective-permute-start(bf16[128,1024]{1,0:T(8,128)(2,1)S(1)} %add_convert_fusion.19), channel_id=1, source_target_pairs={{0,16},{4,20},{8,24},{12,28},{16,0},{20,4},{24,8},{28,12},{1,17},{... | collective-permute-start | bytes 786440 | tf_op jit(solution)/shard_map/ppermute | solution.py:77
  311.3 15.8 %collective-permute-start.67 = (bf16[2,512,256]{2,1,0:T(8,128)(2,1)S(1)}, bf16[2,512,256]{2,1,0:T(8,128)(2,1)S(1)}, u32[]{:S(2)}, u32[]{:S(2)}) collective-permute-start(bf16[2,512,256]{2,1,0:T(8,128)(2,1)S(1)} %copy-done.100), channel_id=1, source_target_pairs={{0,2},{1,3},{2,0},{3,1},{4,6},{5,7},{6,4},{7,5},{8,10},{9,11},{10,... | collective-permute-start | bytes 1572872 | tf_op jit(solution)/shard_map/ppermute | solution.py:77
  312.4 11.6 %collective-permute-start.66 = (bf16[512,256]{1,0:T(8,128)(2,1)S(1)}, bf16[512,256]{1,0:T(8,128)(2,1)S(1)}, u32[]{:S(2)}, u32[]{:S(2)}) collective-permute-start(bf16[512,256]{1,0:T(8,128)(2,1)S(1)} %copy-done.105), channel_id=1, source_target_pairs={{0,1},{1,0},{2,3},{3,2},{4,5},{5,4},{6,7},{7,6},{8,9},{9,8},{10,11... | collective-permute-start | bytes 786440 | tf_op jit(solution)/shard_map/ppermute | solution.py:77
  328.1 23.6 %collective-permute-start.72 = (bf16[2,1024,256]{2,1,0:T(8,128)(2,1)}, bf16[2,1024,256]{2,1,0:T(8,128)(2,1)}, u32[]{:S(2)}, u32[]{:S(2)}) collective-permute-start(bf16[2,1024,256]{2,1,0:T(8,128)(2,1)} %get-tuple-element.658), channel_id=1, source_target_pairs={{0,1},{1,0},{2,3},{3,2},{4,5},{5,4},{6,7},{7,6},{8,9},{9,8},{10,11... | collective-permute-start | bytes 3145736 | tf_op jit(solution)/shard_map/ppermute | solution.py:77
  328.1 20.3 %collective-permute-start.69 = (bf16[384,1024]{1,0:T(8,128)(2,1)}, bf16[384,1024]{1,0:T(8,128)(2,1)}, u32[]{:S(2)}, u32[]{:S(2)}) collective-permute-start(bf16[384,1024]{1,0:T(8,128)(2,1)} %constant_dynamic-slice_fusion.1), channel_id=1, source_target_pairs={{0,4},{4,0},{8,12},{12,8},{16,20},{20,16},{24,28},{28,24},{1,5},{5... | collective-permute-start | bytes 2359304 | tf_op jit(solution)/shard_map/ppermute | solution.py:77
  330.1 21.6 %collective-permute-start.70 = (bf16[256,1024]{1,0:T(8,128)(2,1)}, bf16[256,1024]{1,0:T(8,128)(2,1)}, u32[]{:S(2)}, u32[]{:S(2)}) collective-permute-start(bf16[256,1024]{1,0:T(8,128)(2,1)} %pad_maximum_fusion.9), channel_id=1, source_target_pairs={{0,8},{4,12},{8,0},{12,4},{16,24},{20,28},{24,16},{28,20},{1,9},{5... | collective-permute-start | bytes 1572872 | tf_op jit(solution)/shard_map/ppermute | solution.py:77
  333.7 18.0 %collective-permute-start.71 = (bf16[128,1024]{1,0:T(8,128)(2,1)}, bf16[128,1024]{1,0:T(8,128)(2,1)}, u32[]{:S(2)}, u32[]{:S(2)}) collective-permute-start(bf16[128,1024]{1,0:T(8,128)(2,1)} %add_convert_fusion.18), channel_id=1, source_target_pairs={{0,16},{4,20},{8,24},{12,28},{16,0},{20,4},{24,8},{28,12},{1,17},{... | collective-permute-start | bytes 786440 | tf_op jit(solution)/shard_map/ppermute | solution.py:77
  352.9 32.0 %collective-permute-start.76 = (bf16[512,1024]{1,0:T(8,128)(2,1)S(1)}, bf16[512,1024]{1,0:T(8,128)(2,1)S(1)}, u32[]{:S(2)}, u32[]{:S(2)}) collective-permute-start(bf16[512,1024]{1,0:T(8,128)(2,1)S(1)} %pad_maximum_fusion.6.own_ref), channel_id=1, source_target_pairs={{0,4},{4,0},{8,12},{12,8},{16,20},{20,16},{24,28},{28,24},{1,5},{5... | collective-permute-start | bytes 3145736 | tf_op jit(solution)/shard_map/ppermute | solution.py:77
  356.0 29.0 %collective-permute-start.77 = (bf16[256,1024]{1,0:T(8,128)(2,1)}, bf16[256,1024]{1,0:T(8,128)(2,1)}, u32[]{:S(2)}, u32[]{:S(2)}) collective-permute-start(bf16[256,1024]{1,0:T(8,128)(2,1)} %pad_maximum_fusion.10), channel_id=1, source_target_pairs={{0,8},{4,12},{8,0},{12,4},{16,24},{20,28},{24,16},{28,20},{1,9},{5... | collective-permute-start | bytes 1572872 | tf_op jit(solution)/shard_map/ppermute | solution.py:77
  361.0 20.8 %collective-permute-start.73 = (bf16[144,1024]{1,0:T(8,128)(2,1)}, bf16[144,1024]{1,0:T(8,128)(2,1)}, u32[]{:S(2)}, u32[]{:S(2)}) collective-permute-start(bf16[144,1024]{1,0:T(8,128)(2,1)} %get-tuple-element.704), channel_id=1, source_target_pairs={{0,8},{4,12},{8,0},{12,4},{16,24},{20,28},{24,16},{28,20},{1,9},{5... | collective-permute-start | bytes 884744 | tf_op jit(solution)/shard_map/ppermute | solution.py:77
  361.1 23.8 %collective-permute-start.74 = (bf16[144,1024]{1,0:T(8,128)(2,1)}, bf16[144,1024]{1,0:T(8,128)(2,1)}, u32[]{:S(2)}, u32[]{:S(2)}) collective-permute-start(bf16[144,1024]{1,0:T(8,128)(2,1)} %get-tuple-element.705), channel_id=1, source_target_pairs={{0,16},{4,20},{8,24},{12,28},{16,0},{20,4},{24,8},{28,12},{1,17},{... | collective-permute-start | bytes 884744 | tf_op jit(solution)/shard_map/ppermute | solution.py:77
  362.8 22.1 %collective-permute-start.75 = (bf16[144,1024]{1,0:T(8,128)(2,1)}, bf16[144,1024]{1,0:T(8,128)(2,1)}, u32[]{:S(2)}, u32[]{:S(2)}) collective-permute-start(bf16[144,1024]{1,0:T(8,128)(2,1)} %get-tuple-element.703), channel_id=1, source_target_pairs={{0,24},{4,28},{8,16},{12,20},{16,8},{20,12},{24,0},{28,4},{1,25},{... | collective-permute-start | bytes 884744 | tf_op jit(solution)/shard_map/ppermute | solution.py:77
  388.1 34.7 %collective-permute-start.81 = (bf16[512,1024]{1,0:T(8,128)(2,1)S(1)}, bf16[512,1024]{1,0:T(8,128)(2,1)S(1)}, u32[]{:S(2)}, u32[]{:S(2)}) collective-permute-start(bf16[512,1024]{1,0:T(8,128)(2,1)S(1)} %pad_maximum_fusion.7.own_ref), channel_id=1, source_target_pairs={{0,4},{4,0},{8,12},{12,8},{16,20},{20,16},{24,28},{28,24},{1,5},{5... | collective-permute-start | bytes 3145736 | tf_op jit(solution)/shard_map/ppermute | solution.py:77
  389.9 10.8 %collective-permute-start.82 = (bf16[1024,256]{1,0:T(8,128)(2,1)S(1)}, bf16[1024,256]{1,0:T(8,128)(2,1)S(1)}, u32[]{:S(2)}, u32[]{:S(2)}) collective-permute-start(bf16[1024,256]{1,0:T(8,128)(2,1)S(1)} %fusion.4), channel_id=1, source_target_pairs={{0,2},{1,3},{2,0},{3,1},{4,6},{5,7},{6,4},{7,5},{8,10},{9,11},{10,... | collective-permute-start | bytes 1572872 | tf_op jit(solution)/shard_map/ppermute | solution.py:77
  391.0 16.3 %collective-permute-start.78 = (bf16[144,1024]{1,0:T(8,128)(2,1)S(1)}, bf16[144,1024]{1,0:T(8,128)(2,1)S(1)}, u32[]{:S(2)}, u32[]{:S(2)}) collective-permute-start(bf16[144,1024]{1,0:T(8,128)(2,1)S(1)} %add_convert_fusion.17), channel_id=1, source_target_pairs={{0,8},{4,12},{8,0},{12,4},{16,24},{20,28},{24,16},{28,20},{1,9},{5... | collective-permute-start | bytes 884744 | tf_op jit(solution)/shard_map/ppermute | solution.py:77
  397.2 20.5 %collective-permute-start.79 = (bf16[144,1024]{1,0:T(8,128)(2,1)S(1)}, bf16[144,1024]{1,0:T(8,128)(2,1)S(1)}, u32[]{:S(2)}, u32[]{:S(2)}) collective-permute-start(bf16[144,1024]{1,0:T(8,128)(2,1)S(1)} %add_convert_fusion.17), channel_id=1, source_target_pairs={{0,16},{4,20},{8,24},{12,28},{16,0},{20,4},{24,8},{28,12},{1,17},{... | collective-permute-start | bytes 884744 | tf_op jit(solution)/shard_map/ppermute | solution.py:77
  397.6 25.2 %collective-permute-start.80 = (bf16[144,1024]{1,0:T(8,128)(2,1)S(1)}, bf16[144,1024]{1,0:T(8,128)(2,1)S(1)}, u32[]{:S(2)}, u32[]{:S(2)}) collective-permute-start(bf16[144,1024]{1,0:T(8,128)(2,1)S(1)} %add_convert_fusion.17), channel_id=1, source_target_pairs={{0,24},{4,28},{8,16},{12,20},{16,8},{20,12},{24,0},{28,4},{1,25},{... | collective-permute-start | bytes 884744 | tf_op jit(solution)/shard_map/ppermute | solution.py:77
  423.9 13.1 %collective-permute-start.83 = (bf16[2,1024,256]{2,1,0:T(8,128)(2,1)}, bf16[2,1024,256]{2,1,0:T(8,128)(2,1)}, u32[]{:S(2)}, u32[]{:S(2)}) collective-permute-start(bf16[2,1024,256]{2,1,0:T(8,128)(2,1)} %get-tuple-element.680), channel_id=1, source_target_pairs={{0,1},{1,0},{2,3},{3,2},{4,5},{5,4},{6,7},{7,6},{8,9},{9,8},{10,11... | collective-permute-start | bytes 3145736 | tf_op jit(solution)/shard_map/ppermute | solution.py:77
  424.0 28.5 %collective-permute-start.85 = (bf16[576,1024]{1,0:T(8,128)(2,1)S(1)}, bf16[576,1024]{1,0:T(8,128)(2,1)}, u32[]{:S(2)}, u32[]{:S(2)}) collective-permute-start(bf16[576,1024]{1,0:T(8,128)(2,1)S(1)} %pad_maximum_fusion.own_ref), channel_id=1, source_target_pairs={{0,4},{4,0},{8,12},{12,8},{16,20},{20,16},{24,28},{28,24},{1,5},{5... | collective-permute-start | bytes 3538952 | tf_op jit(solution)/shard_map/ppermute | solution.py:77
  438.2 21.2 %collective-permute-start.84 = (bf16[1024,256]{1,0:T(8,128)(2,1)S(1)}, bf16[1024,256]{1,0:T(8,128)(2,1)S(1)}, u32[]{:S(2)}, u32[]{:S(2)}) collective-permute-start(bf16[1024,256]{1,0:T(8,128)(2,1)S(1)} %fusion.2), channel_id=1, source_target_pairs={{0,2},{1,3},{2,0},{3,1},{4,6},{5,7},{6,4},{7,5},{8,10},{9,11},{10,... | collective-permute-start | bytes 1572872 | tf_op jit(solution)/shard_map/ppermute | solution.py:77
  (136 other events, 1022.9 us)
where the time goes:
time: 467 us; the launch traced here: 462 us
  Pallas kernels  196 us (42%)
  waiting for transfers between devices  123 us (26%)
  starting transfers between devices  72 us (15%)
  other arithmetic  30.4 us (7%)
  local copies, waits for them, and re-layouts  24.9 us (5%)
  matrix products  13.3 us (3%)
    ppermute x86, waiting for transfers between devices, swap(): return lax.ppermute(value, axis, [(i, i ^ mask) for i in range(size)])  123 us
    ppermute x86, starting transfers between devices, swap(): return lax.ppermute(value, axis, [(i, i ^ mask) for i in range(size)])  72 us
    pallas_call x2, Pallas kernels, unfeed(): pl.pallas_call(functools.partial(unfeed_kernel, n_head, n_in, rows), grid...  38.2 us
    pallas_call x2, Pallas kernels, unattend(): pl.pallas_call(functools.partial(unattend_kernel, n_head, chunks, row_len...  33.9 us
    pallas_call x2, Pallas kernels, attend_chunk(): pl.pallas_call(body, grid_spec=pltpu.PrefetchScalarGridSpec(num_scalar_pr...  27.9 us
    pallas_call x2, Pallas kernels, feed(): pl.pallas_call(functools.partial(feed_kernel, n_head, rows), grid=(hidden...  21.4 us
    unnamed x228, local copies, waits for them, and re-layouts  17.1 us
    pallas_call x2, Pallas kernels, spread(): pl.pallas_call(functools.partial(spread_kernel, n_head, share, len(d_all)...  15.2 us
  transfers between devices with their start and end apart: 86, of which 31 were waited for; matrix products, arithmetic and copies ran while one was open for 9% of the time, Pallas kernels for 42%

commit v1 on v0

--- a/solution.py
+++ b/solution.py
@@ -261,7 +261,7 @@
     rows, model = parts[0].shape
     share = model // n_head
 
-    def body(place, info, own_ref, other_ref, q_out, k_out, v_out, o_out, small_out, room):
+    def body(place, info, own_ref, other_ref, q_out, k_out, v_out, o_out, room):
         store_blocks(place[0], summed, (own_ref, other_ref), room)
         for g in range(pairs):
             for i, out in enumerate((q_out, k_out, v_out)):
@@ -270,9 +270,8 @@
                     for e in range(n_head):
                         at = pl.ds(pl.multiple_of((info[0] ^ e) * share, share), share)
                         out[at, lanes] = room[row : row + count, e * share : (e + 1) * share].T
-        for out, first, rows in ((o_out, 3 * cols, cols), (small_out, 4 * cols, 8)):
-            for row, offset, count in segments(first, rows, ranges):
-                out[offset : offset + count, :] = room[row : row + count, :]
+        for row, offset, count in segments(3 * cols, cols, ranges):
+            o_out[offset : offset + count, :] = room[row : row + count, :]
 
     return pl.pallas_call(
         body,
@@ -280,10 +279,10 @@
             num_scalar_prefetch=2,
             grid=(1,),
             in_specs=[whole((rows, model))] * 2,
-            out_specs=[whole((model, cols))] * 3 + [whole((cols, model)), whole((8, model))],
+            out_specs=[whole((model, cols))] * 3 + [whole((cols, model))],
             scratch_shapes=[pltpu.VMEM((2 * rows, model), F32)],
         ),
-        out_shape=[shape((model, cols), F32)] * 3 + [shape((n, model), F32) for n in (cols, 8)],
+        out_shape=[shape((model, cols), F32)] * 3 + [shape((cols, model), F32)],
         compiler_params=params(32),
         cost_estimate=cost(0, cols * model * 24),
         name="assemble_turned",
@@ -767,6 +766,7 @@
     refs = refs[n_terms + n_head + 2 + kept :]
     own_ref, near_ref, far_ref, dz_ref, direct_ref, grad_ref, two_s, cot_s = refs
     me = info[0]
+    step = pl.program_id(0)
     z = z_refs[0][...].astype(F32)
     for r in z_refs[1:]:
         z += r[...].astype(F32)
@@ -782,7 +782,16 @@
             far_ref[e - 2] = two_s[:, at]
         cot_s[:, at] = c_refs[e][...]
     grad = norm_back(cot_s[...].astype(F32), h_two, factor)
-    grad_ref[...] = jnp.sum(grad * (h_ffn - h_one), axis=0, keepdims=True)
+    summed = jnp.sum(grad * (h_ffn - h_one), axis=0, keepdims=True)
+
+    @pl.when(step == 0)
+    def _():
+        grad_ref[...] = summed
+
+    @pl.when(step > 0)
+    def _():
+        grad_ref[...] += summed
+
     direct_ref[...] = grad * (1.0 - alpha)
     dz_ref[...] = norm_back(grad * alpha, h_ffn, z_factor).astype(BF16)
 
@@ -791,23 +800,25 @@
     n_head, n_terms = len(cot_pieces), len(z_terms)
     rows, model = h_one.shape
     share = cot_pieces[0].shape[1]
-    mine = pl.BlockSpec((rows, share), lambda i, info: (chunk * n_head + info[0], 0))
-    theirs = pl.BlockSpec((rows, share), lambda i, info: (chunk, 0))
+    part = rows // 2
+    mine = pl.BlockSpec((part, share), lambda i, info: (2 * (chunk * n_head + info[0]) + i, 0))
+    theirs = pl.BlockSpec((part, share), lambda i, info: (2 * chunk + i, 0))
+    by_row = pl.BlockSpec((part, model), lambda i, info: (i, 0))
     outs = pl.pallas_call(
         functools.partial(middle_kernel, n_head, n_terms, share, len(kept)),
         grid_spec=pltpu.PrefetchScalarGridSpec(
             num_scalar_prefetch=1,
-            grid=(1,),
-            in_specs=[term_spec(t) for t in z_terms]
+            grid=(2,),
+            in_specs=[by_row] * n_terms
             + [mine]
             + [theirs] * (n_head - 1)
-            + [whole((rows, model)), whole((1, model))]
+            + [by_row, whole((1, model))]
             + [pl.BlockSpec(memory_space=pl.ANY)] * len(kept),
             out_specs=[theirs] * 2
-            + [pl.BlockSpec((n_head - 2, rows, share), lambda i, info: (0, chunk, 0))]
-            + [whole((rows, model))] * 2
+            + [pl.BlockSpec((n_head - 2, part, share), lambda i, info: (0, 2 * chunk + i, 0))]
+            + [by_row] * 2
             + [whole((1, model))],
-            scratch_shapes=[pltpu.VMEM((rows, model), BF16), pltpu.VMEM((rows, model), BF16)],
+            scratch_shapes=[pltpu.VMEM((part, model), BF16), pltpu.VMEM((part, model), BF16)],
         ),
         input_output_aliases={n_terms + n_head + 3 + i: i for i in range(len(kept))},
         out_shape=[kept_shape((CHUNKS * rows, share), BF16)] * 2
@@ -845,9 +856,9 @@
     tile = min(256, hidden // 2)
 
     def body(m_ref, h_ref, z_ref, u_ref, g_ref, down, up, gate):
-        down[...] = dot(m_ref[...], z_ref[...], 0, 0)
-        up[...] = dot(h_ref[...], u_ref[...], 0, 0)
-        gate[...] = dot(h_ref[...], g_ref[...], 0, 0)
+        down[...] = dot(m_ref[...], z_ref[...], 0, 0).astype(BF16)
+        up[...] = dot(h_ref[...], u_ref[...], 0, 0).astype(BF16)
+        gate[...] = dot(h_ref[...], g_ref[...], 0, 0).astype(BF16)
 
     by_col = lambda height: pl.BlockSpec((height, tile), lambda n: (0, n))
     return pl.pallas_call(
@@ -861,7 +872,7 @@
         ],
         out_specs=[pl.BlockSpec((tile, model), lambda n: (n, 0)), by_col(model), by_col(model)],
         grid=(hidden // tile,),
-        out_shape=[kept_shape((hidden, model), F32)] + [kept_shape((model, hidden), F32)] * 2,
+        out_shape=[kept_shape((hidden, model), BF16)] + [kept_shape((model, hidden), BF16)] * 2,
         compiler_params=params(48),
         cost_estimate=cost(6.0 * count * hidden * model, 20e6),
         name="weigh_feed",
@@ -1333,7 +1344,7 @@
         lambda first: join([first] + dz_pieces[1:]), dz_pieces[0], need=dz_pieces[1:] + [sent]
     )
     grad_down, _ = order.run(
-        lambda v: (firsts[0] + dot(fed[1][0], v, 0, 0)).astype(BF16), dz_last
+        lambda v: (firsts[0].astype(F32) + dot(fed[1][0], v, 0, 0)).astype(BF16), dz_last
     )
     sum_down = BatchSum(grad_down, n_batch)
     (low_last, scales_last, dh_even, dh_odd, _), dh_terms = unfeed_step(
@@ -1359,16 +1370,16 @@
         alphas.append(grad_alpha_attn)
         return d_pieces[0], Exchange(d_pieces[1], d_pieces[2], n_head), beside
 
-    def beside_sums(step, value, sums, beside=(), need=()):
+    def beside_sums(step, value, sums, beside=(), need=(), first=False):
         out, (got, beside) = order.run(
             step, value, need=need, beside=([b.flying for b in sums], beside)
         )
-        for b, v in zip(sums, got, strict=True):
-            b.advance(v)
+        for i, (b, v) in enumerate(zip(sums, got, strict=True)):
+            b.advance(after(v, sums[0].sent) if i and first else v)
         return out, beside
 
     grad_up, dh_near = beside_sums(
-        lambda v: (firsts[1] + dot(fed[1][1], v, 0, 0)).astype(BF16),
+        lambda v: (firsts[1].astype(F32) + dot(fed[1][1], v, 0, 0)).astype(BF16),
         low_last[0],
         [sum_down],
         dh_near,
@@ -1376,7 +1387,7 @@
     sum_up = BatchSum(grad_up, n_batch)
     dh_first, (dh_terms, sent) = dh_terms, reduce_far(dh_even, dh_near, n_head)
     grad_gate, _ = order.run(
-        lambda v: (firsts[2] + dot(fed[1][1], v, 0, 0)).astype(BF16),
+        lambda v: (firsts[2].astype(F32) + dot(fed[1][1], v, 0, 0)).astype(BF16),
         low_last[1],
         need=[sent, sum_down.sent, sum_up.sent],
     )
@@ -1435,11 +1446,17 @@
         out_flying, _ = reduce_far(out_blocks[::2], out_near, n_head)
     ahead = [BatchSum(g, n_batch) for g in grads] if n_batch == 8 else []
     d_pair, out_flying = attention_back(
-        pairs - 1, big + ahead, out_flying, need=[sum_gate.sent] + [b.sent for b in ahead]
+        pairs - 1,
+        [sum_down, sum_up] + ahead,
+        out_flying,
+        need=[sum_gate.sent] + [b.sent for b in ahead],
     )
     out_sum = term_sum(out_flying)
-    grad_pair, _ = order.run(
-        lambda d: weigh(d, x_pieces, chunk_len), d_pair, need=[sum_down.sent, sum_up.sent, sum_gate.sent]
+    grad_pair, _ = beside_sums(
+        lambda d: weigh(d, x_pieces, chunk_len),
+        d_pair,
+        [sum_gate],
+        need=[sum_down.sent, sum_up.sent],
     )
     small = jnp.concatenate(
         [out_sum[cols : cols + 2]]
@@ -1449,10 +1466,11 @@
         ],
         axis=0,
     )
-    small = jnp.pad(small, ((0, -(4 * cols + 5) % (16 * n_batch)), (0, 0)))
     if ahead:
         grads = []
-    grads += [grad_pair, out_sum[:cols].astype(BF16), small.astype(BF16)]
+    grads += [grad_pair, out_sum[:cols].astype(BF16)]
+    if 4 * cols % (16 * n_batch):
+        grads.append(jnp.zeros((-4 * cols % (16 * n_batch), model), BF16))
     grads = jnp.concatenate(grads, axis=0)
     ranges = [2 * b.values.shape[0] for b in ahead] + [grads.shape[0]]
     sum_attn = BatchSum(grads, n_batch, direct=True, before=[b.values for b in ahead])
@@ -1464,6 +1482,7 @@
             sums,
             beside,
             need=need,
+            first=c > 0,
         )
 
     def land(sums, beside=()):
@@ -1478,13 +1497,21 @@
     )
     two_pieces = two_moving.finish(two_came)
     dx_near = reduce_near(d_first[-1], n_head)
-    d_last, dx_near = spread_step(
-        1, [sum_attn, sum_up, sum_gate], dx_near, need=[sum_up.sent, sum_gate.sent]
-    )
+    small_swaps = [1 << i for i in range(n_batch.bit_length() - 1)]
+    d_last, (dx_near, small_far) = spread_step(
+        1,
+        [sum_attn, sum_up, sum_gate],
+        (dx_near, swap(small, "batch", small_swaps.pop(0), n_batch)),
+        need=[sum_up.sent, sum_gate.sent],
+    )
+    small = small + small_far
     dx_first, _ = reduce_far(d_first[:-1], dx_near, n_head)
     down_done = assemble(sum_down.finish(), place)
     land([sum_attn, sum_up, sum_gate])
     dx_first = land([sum_attn, sum_gate], dx_first)
+    small = after(small, sum_attn.sent)
+    for bit_now in small_swaps:
+        small = small + swap(small, "batch", bit_now, n_batch)
     dx_near = reduce_near(after(d_last[-1], sum_attn.sent), n_head)
     dx_last, _ = reduce_far(d_last[:-1], dx_near, n_head)
     while len(sum_attn.todo) > 1:
@@ -1493,7 +1520,7 @@
     grad_down = down_done
     grad_up = assemble(sum_up.finish(), place)
     grad_gate = assemble(sum_gate.finish(), place)
-    grad_query, grad_key, grad_value, grad_out, small = assemble_turned(
+    grad_query, grad_key, grad_value, grad_out = assemble_turned(
         sum_attn.finish(), place, info, cols, n_head, pairs, ranges
     )
     grad_hidden = jnp.concatenate([term_sum(dx_first), term_sum(dx_last)], axis=0)[None]

time: 467 us -> 449 us (0.961)
  Pallas kernels: 196 us -> 183 us
  waiting for transfers between devices: 123 us -> 111 us
  starting transfers between devices: 72 us -> 77.2 us
    ppermute x86 -> x89, waiting for transfers between devices: 123 us -> 111 us  [swap(): return lax.ppermute(value, axis, [(i, i ^ mask) for i in range(size)])]
    pallas_call x2, Pallas kernels: 38.2 us -> 27.1 us  [unfeed(): pl.pallas_call(functools.partial(unfeed_kernel, n_head, n_in, rows), grid...]
    ppermute x86 -> x89, starting transfers between devices: 72 us -> 77.2 us  [swap(): return lax.ppermute(value, axis, [(i, i ^ mask) for i in range(size)])]
    unnamed x228 -> x256, local copies, waits for them, and re-layouts: 17.1 us -> 16.9 us
  transfers between devices with their start and end apart: 86 -> 89, of which waited for: 31 -> 28; matrix products, arithmetic and copies ran while one was open for 9% -> 9% of each run, Pallas kernels for 42% -> 41%
where the time goes in v1:
time: 449 us; the launch traced here: 441 us
  Pallas kernels  183 us (41%)
  waiting for transfers between devices  111 us (25%)
  starting transfers between devices  77.2 us (17%)
  other arithmetic  29.6 us (7%)
  local copies, waits for them, and re-layouts  24.5 us (5%)
  matrix products  12.2 us (3%)
    ppermute x89, waiting for transfers between devices, swap(): return lax.ppermute(value, axis, [(i, i ^ mask) for i in range(size)])  111 us
    ppermute x89, starting transfers between devices, swap(): return lax.ppermute(value, axis, [(i, i ^ mask) for i in range(size)])  77.2 us
    pallas_call x2, Pallas kernels, unattend(): pl.pallas_call(functools.partial(unattend_kernel, n_head, chunks, row_len...  31.8 us
    pallas_call x2, Pallas kernels, attend_chunk(): pl.pallas_call(body, grid_spec=pltpu.PrefetchScalarGridSpec(num_scalar_pr...  27.9 us
    pallas_call x2, Pallas kernels, unfeed(): pl.pallas_call(functools.partial(unfeed_kernel, n_head, n_in, rows), grid...  27.1 us
    pallas_call x2, Pallas kernels, feed(): pl.pallas_call(functools.partial(feed_kernel, n_head, rows), grid=(hidden...  21.5 us
    unnamed x256, local copies, waits for them, and re-layouts  16.9 us
    pallas_call x2, Pallas kernels, spread(): pl.pallas_call(functools.partial(spread_kernel, n_head, share, len(d_all)...  15.3 us
  transfers between devices with their start and end apart: 89, of which 28 were waited for; matrix products, arithmetic and copies ran while one was open for 9% of the time, Pallas kernels for 41%

profile of v1, /device:TPU:8, one launch (start us, length us, event | category | flops | bytes accessed | tf_op | source)
XLA Modules:
  0.0 440.8 jit_solution(799516249534480063)
XLA Ops:
  2.1 1.6 collective-permute-start
  4.4 3.9 subtract_convert_fusion
  13.5 2.4 collective-permute-done.refs_2_.refs_10_
  17.4 1.6 collective-permute-start.3
  19.5 11.2 %attend.2 = (bf16[4,2048,64]{2,1,0:T(8,128)(2,1)}, bf16[4,80,2048]{2,1,0:T(8,128)(2,1)}, bf16[4,2048,64]{2,1,0:T(8,128)(2,1)}, bf16[256,2048]{1,0:T(8,128)(2,1)}...) custom-call(s32[10]{0:T(128)S(1)} %pad_add_fusion.info, ...), custom_call_target="tpu_custom_call" | custom-call | flops 8000000000 | bytes 8000000 | tf_op jit(solution)/shard_map/attend/pallas_call | solution.py:472
  30.8 6.2 %collective-permute-done.4.refs_2_.refs_10_.refs_6_ = bf16[1024,256]{1,0:T(8,128)(2,1)} collective-permute-done((bf16[1024,256]{1,0:T(8,128)(2,1)S(1)}, bf16[1024,256]{1,0:T(8,128)(2,1)}, u32[]{:S(2)}, u32[]{:S(2)}) %collective-permute-start.4) | collective-permute-done | bytes 524320 | tf_op jit(solution)/shard_map/ppermute | solution.py:77
  37.5 1.6 collective-permute-start.10
  43.5 16.7 %attend.3 = (bf16[4,2048,64]{2,1,0:T(8,128)(2,1)}, bf16[4,80,2048]{2,1,0:T(8,128)(2,1)}, bf16[4,2048,64]{2,1,0:T(8,128)(2,1)}, bf16[256,2048]{1,0:T(8,128)(2,1)}...) custom-call(s32[10]{0:T(128)S(1)} %pad_add_fusion.info, ...), custom_call_target="tpu_custom_call", output_to_operand_aliasing={{0}: (10, {}), {1}: (11, {}), {2}: (12, {}), {3}: (13, {}),... | custom-call | flops 8000000000 | bytes 8000000 | tf_op jit(solution)/shard_map/attend/pallas_call | solution.py:472
  64.1 3.0 project.2
  67.1 2.8 collective-permute-done.16
  72.9 4.0 project.3
  76.9 6.5 %collective-permute-done.18.refs_2_ = bf16[256,1024]{1,0:T(8,128)(2,1)S(1)} collective-permute-done((bf16[256,1024]{1,0:T(8,128)(2,1)S(1)}, bf16[256,1024]{1,0:T(8,128)(2,1)S(1)}, u32[]{:S(2)}, u32[]{:S(2)}) %collective-permute-start.18) | collective-permute-done | bytes 524320 | tf_op jit(solution)/shard_map/ppermute | solution.py:77
  86.1 10.9 %feed.2 = (bf16[1024,1024]{1,0:T(8,128)(2,1)}, bf16[1024,1024]{1,0:T(8,128)(2,1)}, bf16[1024,1024]{1,0:T(8,128)(2,1)}, bf16[1024,1024]{1,0:T(8,128)(2,1)}, bf16[...) custom-call(bf16[256,1024]{1,0:T(8,128)(2,1)S(1)} %get-tuple-element, ...), custom_call_target="tpu_custom_call" | custom-call | flops 6442450944 | bytes 20000000 | tf_op jit(solution)/shard_map/feed/pallas_call | solution.py:735
  101.5 10.7 %feed.3 = (bf16[1024,1024]{1,0:T(8,128)(2,1)}, bf16[1024,1024]{1,0:T(8,128)(2,1)}, bf16[1024,1024]{1,0:T(8,128)(2,1)}, bf16[1024,1024]{1,0:T(8,128)(2,1)}, bf16[...) custom-call(bf16[256,1024]{1,0:T(8,128)(2,1)S(1)} %get-tuple-element, ...), custom_call_target="tpu_custom_call" | custom-call | flops 6442450944 | bytes 20000000 | tf_op jit(solution)/shard_map/feed/pallas_call | solution.py:735
  112.2 1.8 collective-permute-done.26.refs_2_
  114.6 2.4 collective-permute-done.27.refs_6_
  117.0 3.9 middle.2
  122.5 12.4 %collective-permute-done.31.refs_2_ = bf16[256,1024]{1,0:T(8,128)(2,1)S(1)} collective-permute-done((bf16[256,1024]{1,0:T(8,128)(2,1)S(1)}, bf16[256,1024]{1,0:T(8,128)(2,1)S(1)}, u32[]{:S(2)}, u32[]{:S(2)}) %collective-permute-start.31) | collective-permute-done | bytes 524320 | tf_op jit(solution)/shard_map/ppermute | solution.py:77
  136.8 14.2 %unfeed.2 = (bf16[1024,1024]{1,0:T(8,128)(2,1)}, bf16[1024,1024]{1,0:T(8,128)(2,1)}, f32[1,1024]{1,0:T(1,128)S(1)}, f32[1,1024]{1,0:T(1,128)S(1)}, bf16[256,1024...) custom-call(bf16[256,1024]{1,0:T(8,128)(2,1)S(1)} %get-tuple-element, ...), custom_call_target="tpu_custom_call" | custom-call | flops 6442450944 | bytes 20000000 | tf_op jit(solution)/shard_map/unfeed/pallas_call | solution.py:969
  151.6 4.4 %middle.3 = (bf16[512,256]{1,0:T(8,128)(2,1)}, bf16[512,256]{1,0:T(8,128)(2,1)}, bf16[2,512,256]{2,1,0:T(8,128)(2,1)}, bf16[256,1024]{1,0:T(8,128)(2,1)}, f32[256,1024]{1,0:T(8,128)}, /*index=5*/f32[1,1024]{1,0:T(1,128)S(1)}) custom-call(s32[10]{0:T(128)S(1)} %pad_add_fusion.info, ...), custom_call_target="tpu_custom_call", output_to_operand_aliasing={{0}: (10, {}), {1}: (11, {}), {2}: (12, {})} | custom-call | flops 15728640 | bytes 6291456 | tf_op jit(solution)/shard_map/middle/pallas_call | solution.py:807
  158.5 10.7 %weigh_feed.1 = (bf16[1024,1024]{1,0:T(8,128)(2,1)}, bf16[1024,1024]{1,0:T(8,128)(2,1)}, bf16[1024,1024]{1,0:T(8,128)(2,1)}) custom-call(bf16[1024,1024]{1,0:T(8,128)(2,1)S(1)} %copy-done.81, bf16[1024,1024]{1,0:T(8,128)(2,1)S(1)} %copy-done.82, bf16[1024,1024]{1,0:T(8,128)(2,1)} %get-tuple-element.518.z_ref, bf16[1024,1024]{1,0:T(8,128)(2,1)} %get-tuple-element.500.u_ref, ...), custom_call_target="tpu_custom_call" | custom-call | flops 6442450944 | bytes 20000000 | tf_op jit(solution)/shard_map/weigh_feed/pallas_call | solution.py:864
  169.2 2.0 collective-permute-done.36.refs_2_
  173.7 1.6 collective-permute-start.39
  176.8 2.4 add_convert_fusion.2
  180.0 13.0 %unfeed.3 = (bf16[1024,1024]{1,0:T(8,128)(2,1)}, bf16[1024,1024]{1,0:T(8,128)(2,1)}, f32[1,1024]{1,0:T(1,128)S(1)}, f32[1,1024]{1,0:T(1,128)S(1)}, bf16[256,1024...) custom-call(bf16[1024,1024]{1,0:T(8,128)(2,1)S(1)} %join.1.refs_0_, ...), custom_call_target="tpu_custom_call" | custom-call | flops 6442450944 | bytes 20000000 | tf_op jit(solution)/shard_map/unfeed/pallas_call | solution.py:969
  193.5 4.7 %add_convert_fusion.1 = bf16[1024,1024]{1,0:T(8,128)(2,1)S(1)} fusion(bf16[1024,1024]{1,0:T(8,128)(2,1)} %get-tuple-element.549, bf16[1024,1024]{1,0:T(8,128)(2,1)S(1)} %copy-done.123, bf16[1024,1024]{1,0:T(8,128)(2,1)} %get-tuple-element.550), kind=kOutput, calls=%fused_computation.1 | convolution fusion | flops 2150629376 | bytes 8388608 | tf_op jit(solution)/shard_map/dot_general | solution.py:25
  198.2 6.0 %collective-permute-done.40 = bf16[512,1024]{1,0:T(8,128)(2,1)S(1)} collective-permute-done((bf16[512,1024]{1,0:T(8,128)(2,1)S(1)}, bf16[512,1024]{1,0:T(8,128)(2,1)S(1)}, u32[]{:S(2)}, u32[]{:S(2)}) %collective-permute-start.40) | collective-permute-done | bytes 1048608 | tf_op jit(solution)/shard_map/ppermute | solution.py:77
  207.5 2.5 add_convert_fusion
  210.1 4.4 %unproject.2 = (bf16[512,1024]{1,0:T(8,128)(2,1)}, bf16[256,256]{1,0:T(8,128)(2,1)S(1)}, bf16[256,256]{1,0:T(8,128)(2,1)S(1)}, bf16[2,256,256]{2,1,0:T(8,128)(2,...) custom-call(bf16[256,1024]{1,0:T(8,128)(2,1)S(1)} %copy-done.48, bf16[256,1024]{1,0:T(8,128)(2,1)S(1)} %copy-done.50, ...), custom_call_target="tpu_custom_call" | custom-call | flops 536870912 | bytes 8000000 | tf_op jit(solution)/shard_map/unproject/pallas_call | solution.py:1036
  214.5 3.0 collective-permute-done.44
  218.0 1.7 collective-permute-start.46
  219.9 2.7 collective-permute-start.47
  222.6 4.4 unproject.3
  228.0 2.5 convolution_convert_fusion
  230.6 3.9 collective-permute-done.47
  240.6 15.9 %unattend.2 = (bf16[3,128,2048]{2,1,0:T(8,128)(2,1)}, f32[128,1]{1,0:T(8,128)S(1)}) custom-call(s32[10]{0:T(128)S(1)} %pad_add_fusion.info, bf16[256,256]{1,0:T(8,128)(2,1)S(1)} %get-tuple-element.624.refs_0_, bf16[256,256]{1,0:T(8,128)(2,1)S(1)} %collective-permute-done.45.refs_1_, bf16[256,256]{1,0:T(8,128)(2,1)S(1)} %get-tuple-element.723.refs_2_, ...), custom_call_target="tpu_custom_call" | custom-call | flops 22000001024 | bytes 6000000 | tf_op jit(solution)/shard_map/unattend/pallas_call | solution.py:600
  258.5 1.8 collective-permute-start.59
  260.4 2.9 collective-permute-start.58
  263.4 3.0 weigh.2
  268.9 15.9 %unattend.3 = (bf16[3,128,2048]{2,1,0:T(8,128)(2,1)}, f32[128,1]{1,0:T(8,128)S(1)}) custom-call(s32[10]{0:T(128)S(1)} %pad_add_fusion.info, bf16[256,256]{1,0:T(8,128)(2,1)S(1)} %get-tuple-element.624.refs_0_, bf16[256,256]{1,0:T(8,128)(2,1)S(1)} %collective-permute-done.45.refs_1_, bf16[256,256]{1,0:T(8,128)(2,1)S(1)} %get-tuple-element.723.refs_2_, ...), custom_call_target="tpu_custom_call" | custom-call | flops 22000001024 | bytes 6000000 | tf_op jit(solution)/shard_map/unattend/pallas_call | solution.py:600
  285.7 3.4 collective-permute-start.63
  289.5 3.5 weigh.3
  293.1 1.7 collective-permute-start.67
  297.8 7.8 %spread.2 = (bf16[1024,256]{1,0:T(8,128)(2,1)S(1)}, bf16[1024,256]{1,0:T(8,128)(2,1)S(1)}, bf16[2,1024,256]{2,1,0:T(8,128)(2,1)}) custom-call(s32[10]{0:T(128)S(1)} %pad_add_fusion.info, bf16[384,2048]{1,0:T(8,128)(2,1)S(1)} %bitcast.77, bf16[384,2048]{1,0:T(8,128)(2,1)S(1)} %bitcast.80, bf16[768,1024]{1,0:T(8,128)(2,1)S(1)} %copy-done.71, ...), custom_call_target="tpu_custom_call" | custom-call | flops 1610612736 | bytes 8000000 | tf_op jit(solution)/shard_map/spread/pallas_call | solution.py:1084
  307.9 2.3 collective-permute-done.64
  316.7 3.3 collective-permute-start.70
  327.8 7.5 %spread.3 = (bf16[1024,256]{1,0:T(8,128)(2,1)S(1)}, bf16[1024,256]{1,0:T(8,128)(2,1)S(1)}, bf16[2,1024,256]{2,1,0:T(8,128)(2,1)}) custom-call(s32[10]{0:T(128)S(1)} %pad_add_fusion.info, bf16[384,2048]{1,0:T(8,128)(2,1)S(1)} %bitcast.78, bf16[384,2048]{1,0:T(8,128)(2,1)S(1)} %bitcast.81, bf16[768,1024]{1,0:T(8,128)(2,1)S(1)} %copy-done.72, ...), custom_call_target="tpu_custom_call" | custom-call | flops 1610612736 | bytes 8000000 | tf_op jit(solution)/shard_map/spread/pallas_call | solution.py:1084
  335.3 3.4 collective-permute-done.71
  347.0 19.0 %collective-permute-done.74 = bf16[128,1024]{1,0:T(8,128)(2,1)S(1)} collective-permute-done((bf16[128,1024]{1,0:T(8,128)(2,1)}, bf16[128,1024]{1,0:T(8,128)(2,1)S(1)}, u32[]{:S(2)}, u32[]{:S(2)}) %collective-permute-start.74) | collective-permute-done | bytes 262176 | tf_op jit(solution)/shard_map/ppermute | solution.py:77
  366.1 3.1 collective-permute-done.75
  369.2 1.7 add_convert_fusion.16
  374.4 1.6 collective-permute-start.83
  376.0 5.2 %collective-permute-start.79 = (bf16[128,1024]{1,0:T(8,128)(2,1)S(1)}, bf16[128,1024]{1,0:T(8,128)(2,1)S(1)}, u32[]{:S(2)}, u32[]{:S(2)}) collective-permute-start(bf16[128,1024]{1,0:T(8,128)(2,1)S(1)} %add_convert_fusion.16), channel_id=1, source_target_pairs={{0,8},{4,12},{8,0},{12,4},{16,24},{20,28},{24,16},{28,20},{1,9},{5... | collective-permute-start | bytes 786440 | tf_op jit(solution)/shard_map/ppermute | solution.py:77
  382.6 1.9 slice_bitcast_fusion.2
  384.5 5.5 %collective-permute-done.79 = bf16[128,1024]{1,0:T(8,128)(2,1)S(1)} collective-permute-done((bf16[128,1024]{1,0:T(8,128)(2,1)S(1)}, bf16[128,1024]{1,0:T(8,128)(2,1)S(1)}, u32[]{:S(2)}, u32[]{:S(2)}) %collective-permute-start.79) | collective-permute-done | bytes 262176 | tf_op jit(solution)/shard_map/ppermute | solution.py:77
  390.0 9.0 %collective-permute-done.80 = bf16[128,1024]{1,0:T(8,128)(2,1)S(1)} collective-permute-done((bf16[128,1024]{1,0:T(8,128)(2,1)S(1)}, bf16[128,1024]{1,0:T(8,128)(2,1)S(1)}, u32[]{:S(2)}, u32[]{:S(2)}) %collective-permute-start.80) | collective-permute-done | bytes 262176 | tf_op jit(solution)/shard_map/ppermute | solution.py:77
  399.1 4.3 collective-permute-done.81
  409.0 2.3 assemble.5
  411.3 2.5 settle.1
  413.9 2.3 assemble.3
  416.2 2.1 collective-permute-start.88
  420.2 2.3 assemble.4
  424.4 7.7 %collective-permute-done.86.other_ref = bf16[512,1024]{1,0:T(8,128)(2,1)} collective-permute-done((bf16[512,1024]{1,0:T(8,128)(2,1)}, bf16[512,1024]{1,0:T(8,128)(2,1)}, u32[]{:S(2)}, u32[]{:S(2)}) %collective-permute-start.86) | collective-permute-done | bytes 1048608 | tf_op jit(solution)/shard_map/ppermute | solution.py:77
  432.0 5.6 %assemble_turned.1 = (f32[1024,256]{1,0:T(8,128)}, f32[1024,256]{1,0:T(8,128)}, f32[1024,256]{1,0:T(8,128)}, f32[256,1024]{1,0:T(8,128)}) custom-call(s32[1]{0:T(128)} %bitcast.33.place, s32[10]{0:T(128)S(1)} %pad_add_fusion.info, bf16[512,1024]{1,0:T(8,128)(2,1)} %pad_maximum_fusion.7.own_ref, bf16[512,1024]{1,0:T(8,128)(2,1)} %collective-permute-done.86.other_ref), custom_call_target="tpu_custom_call" | custom-call | bytes 6291456 | tf_op jit(solution)/shard_map/assemble_turned/pallas_call | solution.py:276
  (479 shorter events, 101.1 us)
Async XLA Ops:
  2.1 13.7 %collective-permute-start = (bf16[1024,256]{1,0:T(8,128)(2,1)S(1)}, bf16[1024,256]{1,0:T(8,128)(2,1)S(1)}, u32[]{:S(2)}, u32[]{:S(2)}) collective-permute-start(bf16[1024,256]{1,0:T(8,128)(2,1)S(1)} %get-tuple-element.361.refs_0_.refs_8_), channel_id=1, source_target_pairs={{0,2},{1,3},{2,0},{3,1},{4,6},{5,7},{6,4},{7,5},{8,10},{9,11},{10,... | collective-permute-start | bytes 1572872 | tf_op jit(solution)/shard_map/ppermute | solution.py:77
  17.4 13.4 %collective-permute-start.3 = (bf16[256,512]{1,0:T(8,128)(2,1)S(1)}, bf16[256,512]{1,0:T(8,128)(2,1)S(1)}, u32[]{:S(2)}, u32[]{:S(2)}) collective-permute-start(bf16[256,512]{1,0:T(8,128)(2,1)S(1)} %get-tuple-element.378), channel_id=1, source_target_pairs={{0,2},{1,3},{2,0},{3,1},{4,6},{5,7},{6,4},{7,5},{8,10},{9,11},{10,... | collective-permute-start | bytes 786440 | tf_op jit(solution)/shard_map/ppermute | solution.py:77
  19.0 18.0 %collective-permute-start.4 = (bf16[1024,256]{1,0:T(8,128)(2,1)S(1)}, bf16[1024,256]{1,0:T(8,128)(2,1)}, u32[]{:S(2)}, u32[]{:S(2)}) collective-permute-start(bf16[1024,256]{1,0:T(8,128)(2,1)S(1)} %get-tuple-element.380.refs_0_.refs_8_.refs_4_), channel_id=1, source_target_pairs={{0,2},{1,3},{2,0},{3,1},{4,6},{5,7},{6,4},{7,5},{8,10},{9,11},{10,... | collective-permute-start | bytes 1572872 | tf_op jit(solution)/shard_map/ppermute | solution.py:77
  37.5 23.2 %collective-permute-start.10 = (bf16[2,512,256]{2,1,0:T(8,128)(2,1)}, bf16[2,512,256]{2,1,0:T(8,128)(2,1)S(1)}, u32[]{:S(2)}, u32[]{:S(2)}) collective-permute-start(bf16[2,512,256]{2,1,0:T(8,128)(2,1)} %copy-done.75), channel_id=1, source_target_pairs={{0,2},{1,3},{2,0},{3,1},{4,6},{5,7},{6,4},{7,5},{8,10},{9,11},{10,... | collective-permute-start | bytes 1572872 | tf_op jit(solution)/shard_map/ppermute | solution.py:77
  39.1 21.6 %collective-permute-start.9 = (bf16[512,256]{1,0:T(8,128)(2,1)}, bf16[512,256]{1,0:T(8,128)(2,1)S(1)}, u32[]{:S(2)}, u32[]{:S(2)}) collective-permute-start(bf16[512,256]{1,0:T(8,128)(2,1)} %copy-done.76), channel_id=1, source_target_pairs={{0,1},{1,0},{2,3},{3,2},{4,5},{5,4},{6,7},{7,6},{8,9},{9,8},{10,11... | collective-permute-start | bytes 786440 | tf_op jit(solution)/shard_map/ppermute | solution.py:77
  39.1 21.6 %collective-permute-start.11 = (bf16[256,512]{1,0:T(8,128)(2,1)}, bf16[256,512]{1,0:T(8,128)(2,1)S(1)}, u32[]{:S(2)}, u32[]{:S(2)}) collective-permute-start(bf16[256,512]{1,0:T(8,128)(2,1)} %copy-done.113), channel_id=1, source_target_pairs={{0,4},{4,0},{8,12},{12,8},{16,20},{20,16},{24,28},{28,24},{1,5},{5... | collective-permute-start | bytes 786440 | tf_op jit(solution)/shard_map/ppermute | solution.py:77
  40.6 20.1 %collective-permute-start.8 = (bf16[2,256,256]{2,1,0:T(8,128)(2,1)}, bf16[2,256,256]{2,1,0:T(8,128)(2,1)S(1)}, u32[]{:S(2)}, u32[]{:S(2)}) collective-permute-start(bf16[2,256,256]{2,1,0:T(8,128)(2,1)} %get-tuple-element.404), channel_id=1, source_target_pairs={{0,2},{1,3},{2,0},{3,1},{4,6},{5,7},{6,4},{7,5},{8,10},{9,11},{10,... | collective-permute-start | bytes 786440 | tf_op jit(solution)/shard_map/ppermute | solution.py:77
  41.1 19.1 %collective-permute-start.7 = (bf16[256,256]{1,0:T(8,128)(2,1)}, bf16[256,256]{1,0:T(8,128)(2,1)S(1)}, u32[]{:S(2)}, u32[]{:S(2)}) collective-permute-start(bf16[256,256]{1,0:T(8,128)(2,1)} %get-tuple-element.403), channel_id=1, source_target_pairs={{0,1},{1,0},{2,3},{3,2},{4,5},{5,4},{6,7},{7,6},{8,9},{9,8},{10,11... | collective-permute-start | bytes 393224 | tf_op jit(solution)/shard_map/ppermute | solution.py:77
  61.0 8.9 %collective-permute-start.16 = (bf16[2,256,256]{2,1,0:T(8,128)(2,1)}, bf16[2,256,256]{2,1,0:T(8,128)(2,1)S(1)}, u32[]{:S(2)}, u32[]{:S(2)}) collective-permute-start(bf16[2,256,256]{2,1,0:T(8,128)(2,1)} %get-tuple-element.424), channel_id=1, source_target_pairs={{0,2},{1,3},{2,0},{3,1},{4,6},{5,7},{6,4},{7,5},{8,10},{9,11},{10,... | collective-permute-start | bytes 786440 | tf_op jit(solution)/shard_map/ppermute | solution.py:77
  69.9 13.5 %collective-permute-start.18 = (bf16[256,1024]{1,0:T(8,128)(2,1)S(1)}, bf16[256,1024]{1,0:T(8,128)(2,1)S(1)}, u32[]{:S(2)}, u32[]{:S(2)}) collective-permute-start(bf16[256,1024]{1,0:T(8,128)(2,1)S(1)} %get-tuple-element.438.refs_0_), channel_id=1, source_target_pairs={{0,2},{1,3},{2,0},{3,1},{4,6},{5,7},{6,4},{7,5},{8,10},{9,11},{10,... | collective-permute-start | bytes 1572872 | tf_op jit(solution)/shard_map/ppermute | solution.py:77
  83.9 13.8 %collective-permute-start.21 = (bf16[256,1024]{1,0:T(8,128)(2,1)S(1)}, bf16[256,1024]{1,0:T(8,128)(2,1)S(1)}, u32[]{:S(2)}, u32[]{:S(2)}) collective-permute-start(bf16[256,1024]{1,0:T(8,128)(2,1)S(1)} %get-tuple-element.453.refs_0_), channel_id=1, source_target_pairs={{0,2},{1,3},{2,0},{3,1},{4,6},{5,7},{6,4},{7,5},{8,10},{9,11},{10,... | collective-permute-start | bytes 1572872 | tf_op jit(solution)/shard_map/ppermute | solution.py:77
  98.3 13.9 %collective-permute-start.25 = (bf16[256,1024]{1,0:T(8,128)(2,1)S(1)}, bf16[256,1024]{1,0:T(8,128)(2,1)S(1)}, u32[]{:S(2)}, u32[]{:S(2)}) collective-permute-start(bf16[256,1024]{1,0:T(8,128)(2,1)S(1)} %get-tuple-element.463), channel_id=1, source_target_pairs={{0,1},{1,0},{2,3},{3,2},{4,5},{5,4},{6,7},{7,6},{8,9},{9,8},{10,11... | collective-permute-start | bytes 1572872 | tf_op jit(solution)/shard_map/ppermute | solution.py:77
  99.9 14.0 %collective-permute-start.26 = (bf16[256,1024]{1,0:T(8,128)(2,1)S(1)}, bf16[256,1024]{1,0:T(8,128)(2,1)S(1)}, u32[]{:S(2)}, u32[]{:S(2)}) collective-permute-start(bf16[256,1024]{1,0:T(8,128)(2,1)S(1)} %add_convert_fusion.14), channel_id=1, source_target_pairs={{0,2},{1,3},{2,0},{3,1},{4,6},{5,7},{6,4},{7,5},{8,10},{9,11},{10,... | collective-permute-start | bytes 1572872 | tf_op jit(solution)/shard_map/ppermute | solution.py:77
  113.9 6.9 %collective-permute-start.28 = (bf16[256,1024]{1,0:T(8,128)(2,1)S(1)}, bf16[256,1024]{1,0:T(8,128)(2,1)S(1)}, u32[]{:S(2)}, u32[]{:S(2)}) collective-permute-start(bf16[256,1024]{1,0:T(8,128)(2,1)S(1)} %get-tuple-element.478), channel_id=1, source_target_pairs={{0,1},{1,0},{2,3},{3,2},{4,5},{5,4},{6,7},{7,6},{8,9},{9,8},{10,11... | collective-permute-start | bytes 1572872 | tf_op jit(solution)/shard_map/ppermute | solution.py:77
  113.9 6.9 %collective-permute-start.29 = (bf16[256,1024]{1,0:T(8,128)(2,1)S(1)}, bf16[256,1024]{1,0:T(8,128)(2,1)S(1)}, u32[]{:S(2)}, u32[]{:S(2)}) collective-permute-start(bf16[256,1024]{1,0:T(8,128)(2,1)S(1)} %get-tuple-element.479), channel_id=1, source_target_pairs={{0,1},{1,0},{2,3},{3,2},{4,5},{5,4},{6,7},{7,6},{8,9},{9,8},{10,11... | collective-permute-start | bytes 1572872 | tf_op jit(solution)/shard_map/ppermute | solution.py:77
  120.9 14.0 %collective-permute-start.31 = (bf16[256,1024]{1,0:T(8,128)(2,1)S(1)}, bf16[256,1024]{1,0:T(8,128)(2,1)S(1)}, u32[]{:S(2)}, u32[]{:S(2)}) collective-permute-start(bf16[256,1024]{1,0:T(8,128)(2,1)S(1)} %get-tuple-element.485.refs_0_), channel_id=1, source_target_pairs={{0,2},{1,3},{2,0},{3,1},{4,6},{5,7},{6,4},{7,5},{8,10},{9,11},{10,... | collective-permute-start | bytes 1572872 | tf_op jit(solution)/shard_map/ppermute | solution.py:77
  122.5 14.2 %collective-permute-start.30 = (bf16[256,1024]{1,0:T(8,128)(2,1)S(1)}, bf16[256,1024]{1,0:T(8,128)(2,1)S(1)}, u32[]{:S(2)}, u32[]{:S(2)}) collective-permute-start(bf16[256,1024]{1,0:T(8,128)(2,1)S(1)} %get-tuple-element.485.refs_0_), channel_id=1, source_target_pairs={{0,1},{1,0},{2,3},{3,2},{4,5},{5,4},{6,7},{7,6},{8,9},{9,8},{10,11... | collective-permute-start | bytes 1572872 | tf_op jit(solution)/shard_map/ppermute | solution.py:77
  135.1 15.9 %collective-permute-start.33 = (bf16[256,1024]{1,0:T(8,128)(2,1)S(1)}, bf16[256,1024]{1,0:T(8,128)(2,1)S(1)}, u32[]{:S(2)}, u32[]{:S(2)}) collective-permute-start(bf16[256,1024]{1,0:T(8,128)(2,1)S(1)} %add_convert_fusion.13), channel_id=1, source_target_pairs={{0,2},{1,3},{2,0},{3,1},{4,6},{5,7},{6,4},{7,5},{8,10},{9,11},{10,... | collective-permute-start | bytes 1572872 | tf_op jit(solution)/shard_map/ppermute | solution.py:77
  157.0 14.3 %collective-permute-start.36 = (bf16[256,1024]{1,0:T(8,128)(2,1)}, bf16[256,1024]{1,0:T(8,128)(2,1)S(1)}, u32[]{:S(2)}, u32[]{:S(2)}) collective-permute-start(bf16[256,1024]{1,0:T(8,128)(2,1)} %get-tuple-element.530.refs_0_), channel_id=1, source_target_pairs={{0,2},{1,3},{2,0},{3,1},{4,6},{5,7},{6,4},{7,5},{8,10},{9,11},{10,... | collective-permute-start | bytes 1572872 | tf_op jit(solution)/shard_map/ppermute | solution.py:77
  173.7 19.2 %collective-permute-start.39 = (bf16[256,1024]{1,0:T(8,128)(2,1)S(1)}, bf16[256,1024]{1,0:T(8,128)(2,1)S(1)}, u32[]{:S(2)}, u32[]{:S(2)}) collective-permute-start(bf16[256,1024]{1,0:T(8,128)(2,1)S(1)} %add_convert_fusion.12), channel_id=1, source_target_pairs={{0,2},{1,3},{2,0},{3,1},{4,6},{5,7},{6,4},{7,5},{8,10},{9,11},{10,... | collective-permute-start | bytes 1572872 | tf_op jit(solution)/shard_map/ppermute | solution.py:77
  179.4 24.9 %collective-permute-start.40 = (bf16[512,1024]{1,0:T(8,128)(2,1)S(1)}, bf16[512,1024]{1,0:T(8,128)(2,1)S(1)}, u32[]{:S(2)}, u32[]{:S(2)}) collective-permute-start(bf16[512,1024]{1,0:T(8,128)(2,1)S(1)} %constant_dynamic-slice_fusion.10), channel_id=1, source_target_pairs={{0,4},{4,0},{8,12},{12,8},{16,20},{20,16},{24,28},{28,24},{1,5},{5... | collective-permute-start | bytes 3145736 | tf_op jit(solution)/shard_map/ppermute | solution.py:77
  204.8 12.7 %collective-permute-start.44 = (bf16[256,1024]{1,0:T(8,128)(2,1)S(1)}, bf16[256,1024]{1,0:T(8,128)(2,1)S(1)}, u32[]{:S(2)}, u32[]{:S(2)}) collective-permute-start(bf16[256,1024]{1,0:T(8,128)(2,1)S(1)} %constant_dynamic-slice_fusion.9), channel_id=1, source_target_pairs={{0,8},{4,12},{8,0},{12,4},{16,24},{20,28},{24,16},{28,20},{1,9},{5... | collective-permute-start | bytes 1572872 | tf_op jit(solution)/shard_map/ppermute | solution.py:77
  205.5 12.4 %collective-permute-start.43 = (bf16[256,1024]{1,0:T(8,128)(2,1)S(1)}, bf16[256,1024]{1,0:T(8,128)(2,1)S(1)}, u32[]{:S(2)}, u32[]{:S(2)}) collective-permute-start(bf16[256,1024]{1,0:T(8,128)(2,1)S(1)} %add_convert_fusion.11), channel_id=1, source_target_pairs={{0,2},{1,3},{2,0},{3,1},{4,6},{5,7},{6,4},{7,5},{8,10},{9,11},{10,... | collective-permute-start | bytes 1572872 | tf_op jit(solution)/shard_map/ppermute | solution.py:77
  206.9 27.5 %collective-permute-start.48 = (bf16[512,1024]{1,0:T(8,128)(2,1)S(1)}, bf16[512,1024]{1,0:T(8,128)(2,1)S(1)}, u32[]{:S(2)}, u32[]{:S(2)}) collective-permute-start(bf16[512,1024]{1,0:T(8,128)(2,1)S(1)} %constant_dynamic-slice_fusion.8), channel_id=1, source_target_pairs={{0,4},{4,0},{8,12},{12,8},{16,20},{20,16},{24,28},{28,24},{1,5},{5... | collective-permute-start | bytes 3145736 | tf_op jit(solution)/shard_map/ppermute | solution.py:77
  218.0 9.0 %collective-permute-start.46 = (bf16[2,256,256]{2,1,0:T(8,128)(2,1)S(1)}, bf16[2,256,256]{2,1,0:T(8,128)(2,1)S(1)}, u32[]{:S(2)}, u32[]{:S(2)}) collective-permute-start(bf16[2,256,256]{2,1,0:T(8,128)(2,1)S(1)} %get-tuple-element.589), channel_id=1, source_target_pairs={{0,2},{1,3},{2,0},{3,1},{4,6},{5,7},{6,4},{7,5},{8,10},{9,11},{10,... | collective-permute-start | bytes 786440 | tf_op jit(solution)/shard_map/ppermute | solution.py:77
  219.6 7.3 %collective-permute-start.45 = (bf16[256,256]{1,0:T(8,128)(2,1)S(1)}, bf16[256,256]{1,0:T(8,128)(2,1)S(1)}, u32[]{:S(2)}, u32[]{:S(2)}) collective-permute-start(bf16[256,256]{1,0:T(8,128)(2,1)S(1)} %get-tuple-element.588), channel_id=1, source_target_pairs={{0,1},{1,0},{2,3},{3,2},{4,5},{5,4},{6,7},{7,6},{8,9},{9,8},{10,11... | collective-permute-start | bytes 393224 | tf_op jit(solution)/shard_map/ppermute | solution.py:77
  219.9 14.5 %collective-permute-start.47 = (bf16[128,1024]{1,0:T(8,128)(2,1)S(1)}, bf16[128,1024]{1,0:T(8,128)(2,1)S(1)}, u32[]{:S(2)}, u32[]{:S(2)}) collective-permute-start(bf16[128,1024]{1,0:T(8,128)(2,1)S(1)} %constant_dynamic-slice_fusion.7), channel_id=1, source_target_pairs={{0,16},{4,20},{8,24},{12,28},{16,0},{20,4},{24,8},{28,12},{1,17},{... | collective-permute-start | bytes 786440 | tf_op jit(solution)/shard_map/ppermute | solution.py:77
  227.0 8.5 %collective-permute-start.50 = (bf16[2,256,256]{2,1,0:T(8,128)(2,1)S(1)}, bf16[2,256,256]{2,1,0:T(8,128)(2,1)S(1)}, u32[]{:S(2)}, u32[]{:S(2)}) collective-permute-start(bf16[2,256,256]{2,1,0:T(8,128)(2,1)S(1)} %get-tuple-element.593), channel_id=1, source_target_pairs={{0,2},{1,3},{2,0},{3,1},{4,6},{5,7},{6,4},{7,5},{8,10},{9,11},{10,... | collective-permute-start | bytes 786440 | tf_op jit(solution)/shard_map/ppermute | solution.py:77
  227.4 7.0 %collective-permute-start.49 = (bf16[256,256]{1,0:T(8,128)(2,1)S(1)}, bf16[256,256]{1,0:T(8,128)(2,1)S(1)}, u32[]{:S(2)}, u32[]{:S(2)}) collective-permute-start(bf16[256,256]{1,0:T(8,128)(2,1)S(1)} %get-tuple-element.592), channel_id=1, source_target_pairs={{0,1},{1,0},{2,3},{3,2},{4,5},{5,4},{6,7},{7,6},{8,9},{9,8},{10,11... | collective-permute-start | bytes 393224 | tf_op jit(solution)/shard_map/ppermute | solution.py:77
  227.4 11.3 %collective-permute-start.51 = (bf16[256,256]{1,0:T(8,128)(2,1)S(1)}, bf16[256,256]{1,0:T(8,128)(2,1)S(1)}, u32[]{:S(2)}, u32[]{:S(2)}) collective-permute-start(bf16[256,256]{1,0:T(8,128)(2,1)S(1)} %get-tuple-element.722), channel_id=1, source_target_pairs={{0,1},{1,0},{2,3},{3,2},{4,5},{5,4},{6,7},{7,6},{8,9},{9,8},{10,11... | collective-permute-start | bytes 393224 | tf_op jit(solution)/shard_map/ppermute | solution.py:77
  235.9 21.7 %collective-permute-start.55 = (bf16[272,1024]{1,0:T(8,128)(2,1)S(1)}, bf16[272,1024]{1,0:T(8,128)(2,1)S(1)}, u32[]{:S(2)}, u32[]{:S(2)}) collective-permute-start(bf16[272,1024]{1,0:T(8,128)(2,1)S(1)} %get-tuple-element.732), channel_id=1, source_target_pairs={{0,1},{1,0},{2,3},{3,2},{4,5},{5,4},{6,7},{7,6},{8,9},{9,8},{10,11... | collective-permute-start | bytes 1671176 | tf_op jit(solution)/shard_map/ppermute | solution.py:77
  236.0 21.7 %collective-permute-start.56 = (bf16[272,1024]{1,0:T(8,128)(2,1)S(1)}, bf16[272,1024]{1,0:T(8,128)(2,1)S(1)}, u32[]{:S(2)}, u32[]{:S(2)}) collective-permute-start(bf16[272,1024]{1,0:T(8,128)(2,1)S(1)} %get-tuple-element.731), channel_id=1, source_target_pairs={{0,1},{1,0},{2,3},{3,2},{4,5},{5,4},{6,7},{7,6},{8,9},{9,8},{10,11... | collective-permute-start | bytes 1671176 | tf_op jit(solution)/shard_map/ppermute | solution.py:77
  237.1 20.5 %collective-permute-start.54 = (bf16[256,1024]{1,0:T(8,128)(2,1)S(1)}, bf16[256,1024]{1,0:T(8,128)(2,1)S(1)}, u32[]{:S(2)}, u32[]{:S(2)}) collective-permute-start(bf16[256,1024]{1,0:T(8,128)(2,1)S(1)} %constant_dynamic-slice_fusion.6), channel_id=1, source_target_pairs={{0,8},{4,12},{8,0},{12,4},{16,24},{20,28},{24,16},{28,20},{1,9},{5... | collective-permute-start | bytes 1572872 | tf_op jit(solution)/shard_map/ppermute | solution.py:77
  238.7 18.9 %collective-permute-start.53 = (bf16[128,1024]{1,0:T(8,128)(2,1)S(1)}, bf16[128,1024]{1,0:T(8,128)(2,1)S(1)}, u32[]{:S(2)}, u32[]{:S(2)}) collective-permute-start(bf16[128,1024]{1,0:T(8,128)(2,1)S(1)} %add_convert_fusion.19), channel_id=1, source_target_pairs={{0,16},{4,20},{8,24},{12,28},{16,0},{20,4},{24,8},{28,12},{1,17},{... | collective-permute-start | bytes 786440 | tf_op jit(solution)/shard_map/ppermute | solution.py:77
  239.9 26.4 %collective-permute-start.57 = (bf16[512,1024]{1,0:T(8,128)(2,1)S(1)}, bf16[512,1024]{1,0:T(8,128)(2,1)S(1)}, u32[]{:S(2)}, u32[]{:S(2)}) collective-permute-start(bf16[512,1024]{1,0:T(8,128)(2,1)S(1)} %constant_dynamic-slice_fusion.5), channel_id=1, source_target_pairs={{0,4},{4,0},{8,12},{12,8},{16,20},{20,16},{24,28},{28,24},{1,5},{5... | collective-permute-start | bytes 3145736 | tf_op jit(solution)/shard_map/ppermute | solution.py:77
  257.9 26.9 %collective-permute-start.61 = (bf16[272,1024]{1,0:T(8,128)(2,1)S(1)}, bf16[272,1024]{1,0:T(8,128)(2,1)S(1)}, u32[]{:S(2)}, u32[]{:S(2)}) collective-permute-start(bf16[272,1024]{1,0:T(8,128)(2,1)S(1)} %add_convert_fusion.7), channel_id=1, source_target_pairs={{0,2},{1,3},{2,0},{3,1},{4,6},{5,7},{6,4},{7,5},{8,10},{9,11},{10,... | collective-permute-start | bytes 1671176 | tf_op jit(solution)/shard_map/ppermute | solution.py:77
  258.5 26.2 %collective-permute-start.59 = (bf16[128,1024]{1,0:T(8,128)(2,1)S(1)}, bf16[128,1024]{1,0:T(8,128)(2,1)S(1)}, u32[]{:S(2)}, u32[]{:S(2)}) collective-permute-start(bf16[128,1024]{1,0:T(8,128)(2,1)S(1)} %constant_dynamic-slice_fusion.4), channel_id=1, source_target_pairs={{0,16},{4,20},{8,24},{12,28},{16,0},{20,4},{24,8},{28,12},{1,17},{... | collective-permute-start | bytes 786440 | tf_op jit(solution)/shard_map/ppermute | solution.py:77
  260.4 24.4 %collective-permute-start.58 = (bf16[256,1024]{1,0:T(8,128)(2,1)S(1)}, bf16[256,1024]{1,0:T(8,128)(2,1)S(1)}, u32[]{:S(2)}, u32[]{:S(2)}) collective-permute-start(bf16[256,1024]{1,0:T(8,128)(2,1)S(1)} %pad_maximum_fusion.8), channel_id=1, source_target_pairs={{0,8},{4,12},{8,0},{12,4},{16,24},{20,28},{24,16},{28,20},{1,9},{5... | collective-permute-start | bytes 1572872 | tf_op jit(solution)/shard_map/ppermute | solution.py:77
  267.3 17.5 %collective-permute-start.60 = (bf16[192,1024]{1,0:T(8,128)(2,1)S(1)}, bf16[192,1024]{1,0:T(8,128)(2,1)S(1)}, u32[]{:S(2)}, u32[]{:S(2)}) collective-permute-start(bf16[192,1024]{1,0:T(8,128)(2,1)S(1)} %constant_dynamic-slice_fusion.2), channel_id=1, source_target_pairs={{0,4},{4,0},{8,12},{12,8},{16,20},{20,16},{24,28},{28,24},{1,5},{5... | collective-permute-start | bytes 1179656 | tf_op jit(solution)/shard_map/ppermute | solution.py:77
  267.9 25.1 %collective-permute-start.62 = (bf16[256,1024]{1,0:T(8,128)(2,1)S(1)}, bf16[256,1024]{1,0:T(8,128)(2,1)S(1)}, u32[]{:S(2)}, u32[]{:S(2)}) collective-permute-start(bf16[256,1024]{1,0:T(8,128)(2,1)S(1)} %constant_dynamic-slice_fusion.3), channel_id=1, source_target_pairs={{0,8},{4,12},{8,0},{12,4},{16,24},{20,28},{24,16},{28,20},{1,9},{5... | collective-permute-start | bytes 1572872 | tf_op jit(solution)/shard_map/ppermute | solution.py:77
  284.9 25.3 %collective-permute-start.65 = (bf16[512,1024]{1,0:T(8,128)(2,1)S(1)}, bf16[512,1024]{1,0:T(8,128)(2,1)S(1)}, u32[]{:S(2)}, u32[]{:S(2)}) collective-permute-start(bf16[512,1024]{1,0:T(8,128)(2,1)S(1)} %pad_maximum_fusion.4.own_ref), channel_id=1, source_target_pairs={{0,4},{4,0},{8,12},{12,8},{16,20},{20,16},{24,28},{28,24},{1,5},{5... | collective-permute-start | bytes 3145736 | tf_op jit(solution)/shard_map/ppermute | solution.py:77
  285.7 21.5 %collective-permute-start.63 = (bf16[128,1024]{1,0:T(8,128)(2,1)S(1)}, bf16[128,1024]{1,0:T(8,128)(2,1)S(1)}, u32[]{:S(2)}, u32[]{:S(2)}) collective-permute-start(bf16[128,1024]{1,0:T(8,128)(2,1)S(1)} %add_convert_fusion.18), channel_id=1, source_target_pairs={{0,16},{4,20},{8,24},{12,28},{16,0},{20,4},{24,8},{28,12},{1,17},{... | collective-permute-start | bytes 786440 | tf_op jit(solution)/shard_map/ppermute | solution.py:77
  293.1 17.1 %collective-permute-start.67 = (bf16[2,512,256]{2,1,0:T(8,128)(2,1)S(1)}, bf16[2,512,256]{2,1,0:T(8,128)(2,1)S(1)}, u32[]{:S(2)}, u32[]{:S(2)}) collective-permute-start(bf16[2,512,256]{2,1,0:T(8,128)(2,1)S(1)} %copy-done.108), channel_id=1, source_target_pairs={{0,2},{1,3},{2,0},{3,1},{4,6},{5,7},{6,4},{7,5},{8,10},{9,11},{10,... | collective-permute-start | bytes 1572872 | tf_op jit(solution)/shard_map/ppermute | solution.py:77
  294.8 12.3 %collective-permute-start.66 = (bf16[512,256]{1,0:T(8,128)(2,1)S(1)}, bf16[512,256]{1,0:T(8,128)(2,1)S(1)}, u32[]{:S(2)}, u32[]{:S(2)}) collective-permute-start(bf16[512,256]{1,0:T(8,128)(2,1)S(1)} %copy-done.112), channel_id=1, source_target_pairs={{0,1},{1,0},{2,3},{3,2},{4,5},{5,4},{6,7},{7,6},{8,9},{9,8},{10,11... | collective-permute-start | bytes 786440 | tf_op jit(solution)/shard_map/ppermute | solution.py:77
  295.1 15.1 %collective-permute-start.64 = (bf16[128,1024]{1,0:T(8,128)(2,1)S(1)}, bf16[128,1024]{1,0:T(8,128)(2,1)S(1)}, u32[]{:S(2)}, u32[]{:S(2)}) collective-permute-start(bf16[128,1024]{1,0:T(8,128)(2,1)S(1)} %constant_dynamic-slice_fusion.1), channel_id=1, source_target_pairs={{0,16},{4,20},{8,24},{12,28},{16,0},{20,4},{24,8},{28,12},{1,17},{... | collective-permute-start | bytes 786440 | tf_op jit(solution)/shard_map/ppermute | solution.py:77
  311.4 27.3 %collective-permute-start.72 = (bf16[2,1024,256]{2,1,0:T(8,128)(2,1)}, bf16[2,1024,256]{2,1,0:T(8,128)(2,1)}, u32[]{:S(2)}, u32[]{:S(2)}) collective-permute-start(bf16[2,1024,256]{2,1,0:T(8,128)(2,1)} %get-tuple-element.657), channel_id=1, source_target_pairs={{0,1},{1,0},{2,3},{3,2},{4,5},{5,4},{6,7},{7,6},{8,9},{9,8},{10,11... | collective-permute-start | bytes 3145736 | tf_op jit(solution)/shard_map/ppermute | solution.py:77
  313.7 21.6 %collective-permute-start.73 = (f32[5,1024]{1,0:T(8,128)S(1)}, f32[5,1024]{1,0:T(8,128)S(1)}, u32[]{:S(2)}, u32[]{:S(2)}) collective-permute-start(f32[5,1024]{1,0:T(8,128)S(1)} %select_maximum_fusion), channel_id=1, source_target_pairs={{0,4},{4,0},{8,12},{12,8},{16,20},{20,16},{24,28},{28,24},{1,5},{5... | collective-permute-start | bytes 61448 | tf_op jit(solution)/shard_map/ppermute | solution.py:77
  314.7 20.7 %collective-permute-start.69 = (bf16[320,1024]{1,0:T(8,128)(2,1)}, bf16[320,1024]{1,0:T(8,128)(2,1)S(1)}, u32[]{:S(2)}, u32[]{:S(2)}) collective-permute-start(bf16[320,1024]{1,0:T(8,128)(2,1)} %fusion.4), channel_id=1, source_target_pairs={{0,4},{4,0},{8,12},{12,8},{16,20},{20,16},{24,28},{28,24},{1,5},{5... | collective-permute-start | bytes 1966088 | tf_op jit(solution)/shard_map/ppermute | solution.py:77
  316.7 22.0 %collective-permute-start.70 = (bf16[256,1024]{1,0:T(8,128)(2,1)S(1)}, bf16[256,1024]{1,0:T(8,128)(2,1)S(1)}, u32[]{:S(2)}, u32[]{:S(2)}) collective-permute-start(bf16[256,1024]{1,0:T(8,128)(2,1)S(1)} %pad_maximum_fusion.9), channel_id=1, source_target_pairs={{0,8},{4,12},{8,0},{12,4},{16,24},{20,28},{24,16},{28,20},{1,9},{5... | collective-permute-start | bytes 1572872 | tf_op jit(solution)/shard_map/ppermute | solution.py:77
  321.1 17.6 %collective-permute-start.71 = (bf16[128,1024]{1,0:T(8,128)(2,1)S(1)}, bf16[128,1024]{1,0:T(8,128)(2,1)S(1)}, u32[]{:S(2)}, u32[]{:S(2)}) collective-permute-start(bf16[128,1024]{1,0:T(8,128)(2,1)S(1)} %add_convert_fusion.17), channel_id=1, source_target_pairs={{0,16},{4,20},{8,24},{12,28},{16,0},{20,4},{24,8},{28,12},{1,17},{... | collective-permute-start | bytes 786440 | tf_op jit(solution)/shard_map/ppermute | solution.py:77
  341.1 28.1 %collective-permute-start.77 = (bf16[512,1024]{1,0:T(8,128)(2,1)S(1)}, bf16[512,1024]{1,0:T(8,128)(2,1)S(1)}, u32[]{:S(2)}, u32[]{:S(2)}) collective-permute-start(bf16[512,1024]{1,0:T(8,128)(2,1)S(1)} %pad_maximum_fusion.5.own_ref), channel_id=1, source_target_pairs={{0,4},{4,0},{8,12},{12,8},{16,20},{20,16},{24,28},{28,24},{1,5},{5... | collective-permute-start | bytes 3145736 | tf_op jit(solution)/shard_map/ppermute | solution.py:77
  342.4 26.8 %collective-permute-start.78 = (bf16[256,1024]{1,0:T(8,128)(2,1)}, bf16[256,1024]{1,0:T(8,128)(2,1)}, u32[]{:S(2)}, u32[]{:S(2)}) collective-permute-start(bf16[256,1024]{1,0:T(8,128)(2,1)} %pad_maximum_fusion.10), channel_id=1, source_target_pairs={{0,8},{4,12},{8,0},{12,4},{16,24},{20,28},{24,16},{28,20},{1,9},{5... | collective-permute-start | bytes 1572872 | tf_op jit(solution)/shard_map/ppermute | solution.py:77
  343.5 22.5 %collective-permute-start.74 = (bf16[128,1024]{1,0:T(8,128)(2,1)}, bf16[128,1024]{1,0:T(8,128)(2,1)S(1)}, u32[]{:S(2)}, u32[]{:S(2)}) collective-permute-start(bf16[128,1024]{1,0:T(8,128)(2,1)} %get-tuple-element.712), channel_id=1, source_target_pairs={{0,8},{4,12},{8,0},{12,4},{16,24},{20,28},{24,16},{28,20},{1,9},{5... | collective-permute-start | bytes 786440 | tf_op jit(solution)/shard_map/ppermute | solution.py:77
  344.4 24.8 %collective-permute-start.75 = (bf16[128,1024]{1,0:T(8,128)(2,1)}, bf16[128,1024]{1,0:T(8,128)(2,1)}, u32[]{:S(2)}, u32[]{:S(2)}) collective-permute-start(bf16[128,1024]{1,0:T(8,128)(2,1)} %get-tuple-element.713), channel_id=1, source_target_pairs={{0,16},{4,20},{8,24},{12,28},{16,0},{20,4},{24,8},{28,12},{1,17},{... | collective-permute-start | bytes 786440 | tf_op jit(solution)/shard_map/ppermute | solution.py:77
  345.8 23.4 %collective-permute-start.76 = (bf16[128,1024]{1,0:T(8,128)(2,1)}, bf16[128,1024]{1,0:T(8,128)(2,1)}, u32[]{:S(2)}, u32[]{:S(2)}) collective-permute-start(bf16[128,1024]{1,0:T(8,128)(2,1)} %get-tuple-element.711), channel_id=1, source_target_pairs={{0,24},{4,28},{8,16},{12,20},{16,8},{20,12},{24,0},{28,4},{1,25},{... | collective-permute-start | bytes 786440 | tf_op jit(solution)/shard_map/ppermute | solution.py:77
  372.0 31.3 %collective-permute-start.82 = (bf16[512,1024]{1,0:T(8,128)(2,1)S(1)}, bf16[512,1024]{1,0:T(8,128)(2,1)S(1)}, u32[]{:S(2)}, u32[]{:S(2)}) collective-permute-start(bf16[512,1024]{1,0:T(8,128)(2,1)S(1)} %pad_maximum_fusion.6.own_ref), channel_id=1, source_target_pairs={{0,4},{4,0},{8,12},{12,8},{16,20},{20,16},{24,28},{28,24},{1,5},{5... | collective-permute-start | bytes 3145736 | tf_op jit(solution)/shard_map/ppermute | solution.py:77
  374.4 10.1 %collective-permute-start.83 = (bf16[1024,256]{1,0:T(8,128)(2,1)S(1)}, bf16[1024,256]{1,0:T(8,128)(2,1)S(1)}, u32[]{:S(2)}, u32[]{:S(2)}) collective-permute-start(bf16[1024,256]{1,0:T(8,128)(2,1)S(1)} %fusion.2), channel_id=1, source_target_pairs={{0,2},{1,3},{2,0},{3,1},{4,6},{5,7},{6,4},{7,5},{8,10},{9,11},{10,... | collective-permute-start | bytes 1572872 | tf_op jit(solution)/shard_map/ppermute | solution.py:77
  376.0 14.0 %collective-permute-start.79 = (bf16[128,1024]{1,0:T(8,128)(2,1)S(1)}, bf16[128,1024]{1,0:T(8,128)(2,1)S(1)}, u32[]{:S(2)}, u32[]{:S(2)}) collective-permute-start(bf16[128,1024]{1,0:T(8,128)(2,1)S(1)} %add_convert_fusion.16), channel_id=1, source_target_pairs={{0,8},{4,12},{8,0},{12,4},{16,24},{20,28},{24,16},{28,20},{1,9},{5... | collective-permute-start | bytes 786440 | tf_op jit(solution)/shard_map/ppermute | solution.py:77
  381.2 17.9 %collective-permute-start.80 = (bf16[128,1024]{1,0:T(8,128)(2,1)S(1)}, bf16[128,1024]{1,0:T(8,128)(2,1)S(1)}, u32[]{:S(2)}, u32[]{:S(2)}) collective-permute-start(bf16[128,1024]{1,0:T(8,128)(2,1)S(1)} %add_convert_fusion.16), channel_id=1, source_target_pairs={{0,16},{4,20},{8,24},{12,28},{16,0},{20,4},{24,8},{28,12},{1,17},{... | collective-permute-start | bytes 786440 | tf_op jit(solution)/shard_map/ppermute | solution.py:77
  382.1 21.3 %collective-permute-start.81 = (bf16[128,1024]{1,0:T(8,128)(2,1)S(1)}, bf16[128,1024]{1,0:T(8,128)(2,1)S(1)}, u32[]{:S(2)}, u32[]{:S(2)}) collective-permute-start(bf16[128,1024]{1,0:T(8,128)(2,1)S(1)} %add_convert_fusion.16), channel_id=1, source_target_pairs={{0,24},{4,28},{8,16},{12,20},{16,8},{20,12},{24,0},{28,4},{1,25},{... | collective-permute-start | bytes 786440 | tf_op jit(solution)/shard_map/ppermute | solution.py:77
  405.4 13.0 %collective-permute-start.84 = (bf16[2,1024,256]{2,1,0:T(8,128)(2,1)}, bf16[2,1024,256]{2,1,0:T(8,128)(2,1)}, u32[]{:S(2)}, u32[]{:S(2)}) collective-permute-start(bf16[2,1024,256]{2,1,0:T(8,128)(2,1)} %get-tuple-element.687), channel_id=1, source_target_pairs={{0,1},{1,0},{2,3},{3,2},{4,5},{5,4},{6,7},{7,6},{8,9},{9,8},{10,11... | collective-permute-start | bytes 3145736 | tf_op jit(solution)/shard_map/ppermute | solution.py:77
  406.6 25.4 %collective-permute-start.86 = (bf16[512,1024]{1,0:T(8,128)(2,1)}, bf16[512,1024]{1,0:T(8,128)(2,1)}, u32[]{:S(2)}, u32[]{:S(2)}) collective-permute-start(bf16[512,1024]{1,0:T(8,128)(2,1)} %pad_maximum_fusion.7.own_ref), channel_id=1, source_target_pairs={{0,4},{4,0},{8,12},{12,8},{16,20},{20,16},{24,28},{28,24},{1,5},{5... | collective-permute-start | bytes 3145736 | tf_op jit(solution)/shard_map/ppermute | solution.py:77
  407.7 8.5 %collective-permute-start.87 = (f32[5,1024]{1,0:T(8,128)S(1)}, f32[5,1024]{1,0:T(8,128)S(1)}, u32[]{:S(2)}, u32[]{:S(2)}) collective-permute-start(f32[5,1024]{1,0:T(8,128)S(1)} %fusion.21), channel_id=1, source_target_pairs={{0,8},{4,12},{8,0},{12,4},{16,24},{20,28},{24,16},{28,20},{1,9},{5... | collective-permute-start | bytes 61448 | tf_op jit(solution)/shard_map/ppermute | solution.py:77
  419.5 18.1 %collective-permute-start.85 = (bf16[1024,256]{1,0:T(8,128)(2,1)S(1)}, bf16[1024,256]{1,0:T(8,128)(2,1)S(1)}, u32[]{:S(2)}, u32[]{:S(2)}) collective-permute-start(bf16[1024,256]{1,0:T(8,128)(2,1)S(1)} %fusion), channel_id=1, source_target_pairs={{0,2},{1,3},{2,0},{3,1},{4,6},{5,7},{6,4},{7,5},{8,10},{9,11},{10,... | collective-permute-start | bytes 1572872 | tf_op jit(solution)/shard_map/ppermute | solution.py:77
  (153 other events, 1189.9 us)

commit v2 on v1

--- a/solution.py
+++ b/solution.py
@@ -269,9 +269,10 @@
                     lanes = slice(g * width + offset, g * width + offset + count)
                     for e in range(n_head):
                         at = pl.ds(pl.multiple_of((info[0] ^ e) * share, share), share)
-                        out[at, lanes] = room[row : row + count, e * share : (e + 1) * share].T
+                        block = room[row : row + count, e * share : (e + 1) * share]
+                        out[at, lanes] = block.T.astype(F32)
         for row, offset, count in segments(3 * cols, cols, ranges):
-            o_out[offset : offset + count, :] = room[row : row + count, :]
+            o_out[offset : offset + count, :] = room[row : row + count, :].astype(F32)
 
     return pl.pallas_call(
         body,
@@ -280,7 +281,7 @@
             grid=(1,),
             in_specs=[whole((rows, model))] * 2,
             out_specs=[whole((model, cols))] * 3 + [whole((cols, model))],
-            scratch_shapes=[pltpu.VMEM((2 * rows, model), F32)],
+            scratch_shapes=[pltpu.VMEM((2 * rows, model), BF16)],
         ),
         out_shape=[shape((model, cols), F32)] * 3 + [shape((cols, model), F32)],
         compiler_params=params(32),
@@ -460,7 +461,7 @@
         whole((cols, 1)),
         by_lane(1),
     ]
-    operands = [*x_pieces, w_t, cosine, sine, gain, starts]
+    operands = [*x_pieces, held(w_t), held(cosine), held(sine), gain, starts]
     aliases = {}
     if chunk:
         aliases = {1 + len(operands) + i: i for i in range(9)}
@@ -963,7 +964,7 @@
     model = dz_pieces[0].shape[1]
     count, hidden = u.shape
     rows = count // n_head
-    tile = min(256, hidden // 2)
+    tile = hidden // 2
     by_col = lambda height: pl.BlockSpec((height, tile), lambda n: (0, n))
     anywhere = pl.BlockSpec(memory_space=pl.ANY)
     outs = pl.pallas_call(
@@ -1061,10 +1062,10 @@
     d_refs, (w_ref, direct_ref), out_refs = refs[:pairs], refs[pairs : pairs + 2], refs[pairs + 2 :]
     me = info[0]
     block = pl.program_id(0)
-    d_all = jnp.concatenate([r[...] for r in d_refs], axis=0).T
+    d_all = jnp.concatenate([r[...] for r in d_refs], axis=0)
     for e in range(n_head):
         at = pl.ds(pl.multiple_of((me ^ e) * share, share), share)
-        term = dot(d_all, w_ref[:, at])
+        term = dot(d_all, w_ref[:, at], 0, 0)
 
         ref = out_refs[n_head // 2].at[e // 2] if e % 2 else out_refs[e // 2]
 
@@ -1094,12 +1095,12 @@
             out_specs=[pl.BlockSpec((rows, share), lambda i, info: (i, 0))] * (n_head // 2)
             + [pl.BlockSpec((n_head // 2, rows, share), lambda i, info: (0, i, 0))],
         ),
-        out_shape=[shape((chunk_len, share), BF16)] * (n_head // 2)
-        + [shape((n_head // 2, chunk_len, share), BF16)],
+        out_shape=[kept_shape((chunk_len, share), BF16)] * (n_head // 2)
+        + [kept_shape((n_head // 2, chunk_len, share), BF16)],
         compiler_params=params(32),
         cost_estimate=cost(2.0 * chunk_len * model * rows3, 8e6),
         name="spread",
-    )(info, *d_all, w_t, direct)
+    )(info, *(held(d) for d in d_all), held(w_t), held(direct))
 
 
 def settle(own, pieces, info):

time: 449 us -> 450 us (level); the launches traced: 441 us -> 447 us
  Pallas kernels: 183 us -> 202 us
  local copies, waits for them, and re-layouts: 24.5 us -> 19.4 us
  starting transfers between devices: 77.2 us -> 72.7 us
    pallas_call x2, Pallas kernels: 27.1 us -> 38.6 us  [unfeed(): pl.pallas_call(functools.partial(unfeed_kernel, n_head, n_in, rows), grid...]
    unnamed x256 -> x196, local copies, waits for them, and re-layouts: 16.9 us -> 11.7 us
    ppermute x89, starting transfers between devices: 77.2 us -> 72.7 us  [swap(): return lax.ppermute(value, axis, [(i, i ^ mask) for i in range(size)])]
  transfers between devices with their start and end apart: 89 -> 89, of which waited for: 28 -> 29; matrix products, arithmetic and copies ran while one was open for 9% -> 8% of each run, Pallas kernels for 41% -> 45%
where the time goes in v2:
time: 450 us; the launch traced here: 447 us
  Pallas kernels  202 us (45%)
  waiting for transfers between devices  109 us (24%)
  starting transfers between devices  72.7 us (16%)
  other arithmetic  28.9 us (6%)
  local copies, waits for them, and re-layouts  19.4 us (4%)
  matrix products  12 us (3%)
    ppermute x89, waiting for transfers between devices, swap(): return lax.ppermute(value, axis, [(i, i ^ mask) for i in range(size)])  109 us
    ppermute x89, starting transfers between devices, swap(): return lax.ppermute(value, axis, [(i, i ^ mask) for i in range(size)])  72.7 us
    pallas_call x2, Pallas kernels, unfeed(): pl.pallas_call(functools.partial(unfeed_kernel, n_head, n_in, rows), grid...  38.6 us
    pallas_call x2, Pallas kernels, unattend(): pl.pallas_call(functools.partial(unattend_kernel, n_head, chunks, row_len...  35.6 us
    pallas_call x2, Pallas kernels, attend_chunk(): pl.pallas_call(body, grid_spec=pltpu.PrefetchScalarGridSpec(num_scalar_pr...  30 us
    pallas_call x2, Pallas kernels, feed(): pl.pallas_call(functools.partial(feed_kernel, n_head, rows), grid=(hidden...  21.3 us
    pallas_call x2, Pallas kernels, spread(): pl.pallas_call(functools.partial(spread_kernel, n_head, share, len(d_all)...  18.9 us
    dot_general x4, matrix products, dot(): lax.dot_general(left, right, (((left_dim,), (right_dim,)), ((), ())), pre...  12 us
  transfers between devices with their start and end apart: 89, of which 29 were waited for; matrix products, arithmetic and copies ran while one was open for 8% of the time, Pallas kernels for 45%

profile of v2, /device:TPU:8, one launch (start us, length us, event | category | flops | bytes accessed | tf_op | source)
XLA Modules:
  0.0 447.3 jit_solution(15928049754080152120)
XLA Ops:
  2.1 1.6 collective-permute-start
  4.4 3.3 subtract_convert_fusion
  14.0 1.8 collective-permute-done.refs_2_.refs_10_
  16.4 1.8 multiply_sine_fusion
  20.3 12.7 %attend.2 = (bf16[4,2048,64]{2,1,0:T(8,128)(2,1)}, bf16[4,80,2048]{2,1,0:T(8,128)(2,1)}, bf16[4,2048,64]{2,1,0:T(8,128)(2,1)}, bf16[256,2048]{1,0:T(8,128)(2,1)}...) custom-call(s32[10]{0:T(128)S(1)} %pad_add_fusion.info, ...), custom_call_target="tpu_custom_call" | custom-call | flops 8000000000 | bytes 8000000 | tf_op jit(solution)/shard_map/attend/pallas_call | solution.py:473
  33.0 4.7 %collective-permute-done.4.refs_2_.refs_10_.refs_6_ = bf16[1024,256]{1,0:T(8,128)(2,1)} collective-permute-done((bf16[1024,256]{1,0:T(8,128)(2,1)S(1)}, bf16[1024,256]{1,0:T(8,128)(2,1)}, u32[]{:S(2)}, u32[]{:S(2)}) %collective-permute-start.4) | collective-permute-done | bytes 524320 | tf_op jit(solution)/shard_map/ppermute | solution.py:77
  38.3 1.6 collective-permute-start.10
  41.9 17.3 %attend.3 = (bf16[4,2048,64]{2,1,0:T(8,128)(2,1)}, bf16[4,80,2048]{2,1,0:T(8,128)(2,1)}, bf16[4,2048,64]{2,1,0:T(8,128)(2,1)}, bf16[256,2048]{1,0:T(8,128)(2,1)}...) custom-call(s32[10]{0:T(128)S(1)} %pad_add_fusion.info, ...), custom_call_target="tpu_custom_call", output_to_operand_aliasing={{0}: (10, {}), {1}: (11, {}), {2}: (12, {}), {3}: (13, {}),... | custom-call | flops 8000000000 | bytes 8000000 | tf_op jit(solution)/shard_map/attend/pallas_call | solution.py:473
  63.1 3.0 project.2
  66.1 2.8 collective-permute-done.16
  71.9 4.0 project.3
  75.9 6.5 %collective-permute-done.18.refs_2_ = bf16[256,1024]{1,0:T(8,128)(2,1)S(1)} collective-permute-done((bf16[256,1024]{1,0:T(8,128)(2,1)S(1)}, bf16[256,1024]{1,0:T(8,128)(2,1)S(1)}, u32[]{:S(2)}, u32[]{:S(2)}) %collective-permute-start.18) | collective-permute-done | bytes 524320 | tf_op jit(solution)/shard_map/ppermute | solution.py:77
  85.1 10.7 %feed.2 = (bf16[1024,1024]{1,0:T(8,128)(2,1)}, bf16[1024,1024]{1,0:T(8,128)(2,1)}, bf16[1024,1024]{1,0:T(8,128)(2,1)}, bf16[1024,1024]{1,0:T(8,128)(2,1)}, bf16[...) custom-call(bf16[256,1024]{1,0:T(8,128)(2,1)S(1)} %get-tuple-element, ...), custom_call_target="tpu_custom_call" | custom-call | flops 6442450944 | bytes 20000000 | tf_op jit(solution)/shard_map/feed/pallas_call | solution.py:736
  98.9 1.6 collective-permute-start.26
  100.5 10.6 %feed.3 = (bf16[1024,1024]{1,0:T(8,128)(2,1)}, bf16[1024,1024]{1,0:T(8,128)(2,1)}, bf16[1024,1024]{1,0:T(8,128)(2,1)}, bf16[1024,1024]{1,0:T(8,128)(2,1)}, bf16[...) custom-call(bf16[256,1024]{1,0:T(8,128)(2,1)S(1)} %get-tuple-element, ...), custom_call_target="tpu_custom_call" | custom-call | flops 6442450944 | bytes 20000000 | tf_op jit(solution)/shard_map/feed/pallas_call | solution.py:736
  111.1 1.8 collective-permute-done.26.refs_2_
  113.5 2.4 collective-permute-done.27.refs_6_
  116.0 3.9 middle.2
  119.9 1.6 collective-permute-start.31
  121.4 12.4 %collective-permute-done.31.refs_2_ = bf16[256,1024]{1,0:T(8,128)(2,1)S(1)} collective-permute-done((bf16[256,1024]{1,0:T(8,128)(2,1)S(1)}, bf16[256,1024]{1,0:T(8,128)(2,1)S(1)}, u32[]{:S(2)}, u32[]{:S(2)}) %collective-permute-start.31) | collective-permute-done | bytes 524320 | tf_op jit(solution)/shard_map/ppermute | solution.py:77
  134.1 1.6 collective-permute-start.33
  135.8 25.4 %unfeed.2 = (bf16[1024,1024]{1,0:T(8,128)(2,1)}, bf16[1024,1024]{1,0:T(8,128)(2,1)}, f32[1,1024]{1,0:T(1,128)S(1)}, f32[1,1024]{1,0:T(1,128)S(1)}, bf16[256,1024...) custom-call(bf16[256,1024]{1,0:T(8,128)(2,1)S(1)} %get-tuple-element, ...), custom_call_target="tpu_custom_call" | custom-call | flops 6442450944 | bytes 20000000 | tf_op jit(solution)/shard_map/unfeed/pallas_call | solution.py:970
  161.8 4.4 middle.3
  168.5 10.7 %weigh_feed.1 = (bf16[1024,1024]{1,0:T(8,128)(2,1)}, bf16[1024,1024]{1,0:T(8,128)(2,1)}, bf16[1024,1024]{1,0:T(8,128)(2,1)}) custom-call(bf16[1024,1024]{1,0:T(8,128)(2,1)S(1)} %copy-done.53, bf16[1024,1024]{1,0:T(8,128)(2,1)S(1)} %copy-done.54, bf16[1024,1024]{1,0:T(8,128)(2,1)} %get-tuple-element.518.z_ref, bf16[1024,1024]{1,0:T(8,128)(2,1)} %get-tuple-element.500.u_ref, ...), custom_call_target="tpu_custom_call" | custom-call | flops 6442450944 | bytes 20000000 | tf_op jit(solution)/shard_map/weigh_feed/pallas_call | solution.py:865
  179.1 2.2 collective-permute-done.36.refs_2_
  186.0 2.4 add_convert_fusion.2
  189.7 13.2 %unfeed.3 = (bf16[1024,1024]{1,0:T(8,128)(2,1)}, bf16[1024,1024]{1,0:T(8,128)(2,1)}, f32[1,1024]{1,0:T(1,128)S(1)}, f32[1,1024]{1,0:T(1,128)S(1)}, bf16[256,1024...) custom-call(bf16[1024,1024]{1,0:T(8,128)(2,1)S(1)} %join.1.refs_0_, ...), custom_call_target="tpu_custom_call" | custom-call | flops 6442450944 | bytes 20000000 | tf_op jit(solution)/shard_map/unfeed/pallas_call | solution.py:970
  203.6 4.6 %add_convert_fusion.1 = bf16[1024,1024]{1,0:T(8,128)(2,1)S(1)} fusion(bf16[1024,1024]{1,0:T(8,128)(2,1)} %get-tuple-element.549, bf16[1024,1024]{1,0:T(8,128)(2,1)S(1)} %copy-done.93, bf16[1024,1024]{1,0:T(8,128)(2,1)} %get-tuple-element.550), kind=kOutput, calls=%fused_computation.1 | convolution fusion | flops 2150629376 | bytes 8388608 | tf_op jit(solution)/shard_map/dot_general | solution.py:25
  208.2 5.4 %collective-permute-done.40 = bf16[512,1024]{1,0:T(8,128)(2,1)S(1)} collective-permute-done((bf16[512,1024]{1,0:T(8,128)(2,1)S(1)}, bf16[512,1024]{1,0:T(8,128)(2,1)S(1)}, u32[]{:S(2)}, u32[]{:S(2)}) %collective-permute-start.40) | collective-permute-done | bytes 1048608 | tf_op jit(solution)/shard_map/ppermute | solution.py:77
  217.0 2.5 add_convert_fusion
  219.5 4.4 unproject.2
  223.9 3.2 collective-permute-done.44
  229.3 2.6 collective-permute-start.47
  231.9 4.4 unproject.3
  237.6 2.5 convolution_convert_fusion
  240.2 3.4 collective-permute-done.47
  250.0 17.8 %unattend.2 = (bf16[3,128,2048]{2,1,0:T(8,128)(2,1)}, f32[128,1]{1,0:T(8,128)S(1)}) custom-call(s32[10]{0:T(128)S(1)} %pad_add_fusion.info, bf16[256,256]{1,0:T(8,128)(2,1)S(1)} %get-tuple-element.624.refs_0_, bf16[256,256]{1,0:T(8,128)(2,1)S(1)} %collective-permute-done.45.refs_1_, bf16[256,256]{1,0:T(8,128)(2,1)S(1)} %get-tuple-element.723.refs_2_, ...), custom_call_target="tpu_custom_call" | custom-call | flops 22000001024 | bytes 6000000 | tf_op jit(solution)/shard_map/unattend/pallas_call | solution.py:601
  269.8 1.8 collective-permute-start.58
  271.6 3.0 weigh.2
  277.4 17.8 %unattend.3 = (bf16[3,128,2048]{2,1,0:T(8,128)(2,1)}, f32[128,1]{1,0:T(8,128)S(1)}) custom-call(s32[10]{0:T(128)S(1)} %pad_add_fusion.info, bf16[256,256]{1,0:T(8,128)(2,1)S(1)} %get-tuple-element.624.refs_0_, bf16[256,256]{1,0:T(8,128)(2,1)S(1)} %collective-permute-done.45.refs_1_, bf16[256,256]{1,0:T(8,128)(2,1)S(1)} %get-tuple-element.723.refs_2_, ...), custom_call_target="tpu_custom_call" | custom-call | flops 22000001024 | bytes 6000000 | tf_op jit(solution)/shard_map/unattend/pallas_call | solution.py:601
  297.6 3.3 weigh.3
  303.5 3.5 collective-permute-start.64
  308.4 9.6 %spread.2 = (bf16[1024,256]{1,0:T(8,128)(2,1)}, bf16[1024,256]{1,0:T(8,128)(2,1)}, bf16[2,1024,256]{2,1,0:T(8,128)(2,1)}) custom-call(s32[10]{0:T(128)S(1)} %pad_add_fusion.info, bf16[384,2048]{1,0:T(8,128)(2,1)} %bitcast.76, bf16[384,2048]{1,0:T(8,128)(2,1)} %bitcast.79, bf16[768,1024]{1,0:T(8,128)(2,1)} %copy-done.48, f32[256,1024]{1,0:T(8,128)} %get-tuple-element.637.refs_3_), custom_call_target="tpu_custom_call" | custom-call | flops 1610612736 | bytes 8000000 | tf_op jit(solution)/shard_map/spread/pallas_call | solution.py:1085
  321.7 2.0 collective-permute-start.69
  324.8 2.2 collective-permute-start.70
  329.4 9.4 %spread.3 = (bf16[1024,256]{1,0:T(8,128)(2,1)}, bf16[1024,256]{1,0:T(8,128)(2,1)}, bf16[2,1024,256]{2,1,0:T(8,128)(2,1)}) custom-call(s32[10]{0:T(128)S(1)} %pad_add_fusion.info, bf16[384,2048]{1,0:T(8,128)(2,1)} %bitcast.77, bf16[384,2048]{1,0:T(8,128)(2,1)} %bitcast.80, bf16[768,1024]{1,0:T(8,128)(2,1)} %copy-done.48, f32[256,1024]{1,0:T(8,128)} %get-tuple-element.653.refs_3_), custom_call_target="tpu_custom_call" | custom-call | flops 1610612736 | bytes 8000000 | tf_op jit(solution)/shard_map/spread/pallas_call | solution.py:1085
  339.4 5.3 %collective-permute-done.71 = bf16[128,1024]{1,0:T(8,128)(2,1)S(1)} collective-permute-done((bf16[128,1024]{1,0:T(8,128)(2,1)S(1)}, bf16[128,1024]{1,0:T(8,128)(2,1)S(1)}, u32[]{:S(2)}, u32[]{:S(2)}) %collective-permute-start.71) | collective-permute-done | bytes 262176 | tf_op jit(solution)/shard_map/ppermute | solution.py:77
  351.8 1.7 collective-permute-start.75
  354.3 19.0 %collective-permute-done.74 = bf16[128,1024]{1,0:T(8,128)(2,1)} collective-permute-done((bf16[128,1024]{1,0:T(8,128)(2,1)}, bf16[128,1024]{1,0:T(8,128)(2,1)}, u32[]{:S(2)}, u32[]{:S(2)}) %collective-permute-start.74) | collective-permute-done | bytes 262176 | tf_op jit(solution)/shard_map/ppermute | solution.py:77
  373.3 3.1 collective-permute-done.75
  376.4 1.8 add_convert_fusion.16
  379.4 1.7 collective-permute-start.82
  383.6 5.2 %collective-permute-start.79 = (bf16[128,1024]{1,0:T(8,128)(2,1)S(1)}, bf16[128,1024]{1,0:T(8,128)(2,1)S(1)}, u32[]{:S(2)}, u32[]{:S(2)}) collective-permute-start(bf16[128,1024]{1,0:T(8,128)(2,1)S(1)} %add_convert_fusion.16), channel_id=1, source_target_pairs={{0,8},{4,12},{8,0},{12,4},{16,24},{20,28},{24,16},{28,20},{1,9},{5... | collective-permute-start | bytes 786440 | tf_op jit(solution)/shard_map/ppermute | solution.py:77
  390.3 1.9 slice_bitcast_fusion.2
  392.1 5.4 %collective-permute-done.79 = bf16[128,1024]{1,0:T(8,128)(2,1)S(1)} collective-permute-done((bf16[128,1024]{1,0:T(8,128)(2,1)S(1)}, bf16[128,1024]{1,0:T(8,128)(2,1)S(1)}, u32[]{:S(2)}, u32[]{:S(2)}) %collective-permute-start.79) | collective-permute-done | bytes 262176 | tf_op jit(solution)/shard_map/ppermute | solution.py:77
  397.6 8.7 %collective-permute-done.80 = bf16[128,1024]{1,0:T(8,128)(2,1)S(1)} collective-permute-done((bf16[128,1024]{1,0:T(8,128)(2,1)S(1)}, bf16[128,1024]{1,0:T(8,128)(2,1)S(1)}, u32[]{:S(2)}, u32[]{:S(2)}) %collective-permute-start.80) | collective-permute-done | bytes 262176 | tf_op jit(solution)/shard_map/ppermute | solution.py:77
  406.3 4.7 %collective-permute-done.81 = bf16[128,1024]{1,0:T(8,128)(2,1)S(1)} collective-permute-done((bf16[128,1024]{1,0:T(8,128)(2,1)S(1)}, bf16[128,1024]{1,0:T(8,128)(2,1)S(1)}, u32[]{:S(2)}, u32[]{:S(2)}) %collective-permute-start.81) | collective-permute-done | bytes 262176 | tf_op jit(solution)/shard_map/ppermute | solution.py:77
  416.6 2.3 assemble.5
  418.9 2.5 settle.1
  421.4 2.3 assemble.3
  423.8 2.1 collective-permute-start.88
  428.2 2.3 assemble.4
  432.3 7.3 %collective-permute-done.86.other_ref = bf16[512,1024]{1,0:T(8,128)(2,1)} collective-permute-done((bf16[512,1024]{1,0:T(8,128)(2,1)}, bf16[512,1024]{1,0:T(8,128)(2,1)}, u32[]{:S(2)}, u32[]{:S(2)}) %collective-permute-start.86) | collective-permute-done | bytes 1048608 | tf_op jit(solution)/shard_map/ppermute | solution.py:77
  439.6 4.8 %assemble_turned.1 = (f32[1024,256]{1,0:T(8,128)}, f32[1024,256]{1,0:T(8,128)}, f32[1024,256]{1,0:T(8,128)}, f32[256,1024]{1,0:T(8,128)}) custom-call(s32[1]{0:T(128)} %bitcast.33.place, s32[10]{0:T(128)S(1)} %pad_add_fusion.info, bf16[512,1024]{1,0:T(8,128)(2,1)} %pad_maximum_fusion.7.own_ref, bf16[512,1024]{1,0:T(8,128)(2,1)} %collective-permute-done.86.other_ref), custom_call_target="tpu_custom_call" | custom-call | bytes 6291456 | tf_op jit(solution)/shard_map/assemble_turned/pallas_call | solution.py:277
  (419 shorter events, 92.7 us)
Async XLA Ops:
  2.1 13.7 %collective-permute-start = (bf16[1024,256]{1,0:T(8,128)(2,1)S(1)}, bf16[1024,256]{1,0:T(8,128)(2,1)S(1)}, u32[]{:S(2)}, u32[]{:S(2)}) collective-permute-start(bf16[1024,256]{1,0:T(8,128)(2,1)S(1)} %get-tuple-element.361.refs_0_.refs_8_), channel_id=1, source_target_pairs={{0,2},{1,3},{2,0},{3,1},{4,6},{5,7},{6,4},{7,5},{8,10},{9,11},{10,... | collective-permute-start | bytes 1572872 | tf_op jit(solution)/shard_map/ppermute | solution.py:77
  18.2 14.8 %collective-permute-start.3 = (bf16[256,512]{1,0:T(8,128)(2,1)S(1)}, bf16[256,512]{1,0:T(8,128)(2,1)S(1)}, u32[]{:S(2)}, u32[]{:S(2)}) collective-permute-start(bf16[256,512]{1,0:T(8,128)(2,1)S(1)} %get-tuple-element.378), channel_id=1, source_target_pairs={{0,2},{1,3},{2,0},{3,1},{4,6},{5,7},{6,4},{7,5},{8,10},{9,11},{10,... | collective-permute-start | bytes 786440 | tf_op jit(solution)/shard_map/ppermute | solution.py:77
  19.7 18.0 %collective-permute-start.4 = (bf16[1024,256]{1,0:T(8,128)(2,1)S(1)}, bf16[1024,256]{1,0:T(8,128)(2,1)}, u32[]{:S(2)}, u32[]{:S(2)}) collective-permute-start(bf16[1024,256]{1,0:T(8,128)(2,1)S(1)} %get-tuple-element.380.refs_0_.refs_8_.refs_4_), channel_id=1, source_target_pairs={{0,2},{1,3},{2,0},{3,1},{4,6},{5,7},{6,4},{7,5},{8,10},{9,11},{10,... | collective-permute-start | bytes 1572872 | tf_op jit(solution)/shard_map/ppermute | solution.py:77
  38.3 21.5 %collective-permute-start.10 = (bf16[2,512,256]{2,1,0:T(8,128)(2,1)}, bf16[2,512,256]{2,1,0:T(8,128)(2,1)S(1)}, u32[]{:S(2)}, u32[]{:S(2)}) collective-permute-start(bf16[2,512,256]{2,1,0:T(8,128)(2,1)} %copy-done.49), channel_id=1, source_target_pairs={{0,2},{1,3},{2,0},{3,1},{4,6},{5,7},{6,4},{7,5},{8,10},{9,11},{10,... | collective-permute-start | bytes 1572872 | tf_op jit(solution)/shard_map/ppermute | solution.py:77
  39.9 19.9 %collective-permute-start.9 = (bf16[512,256]{1,0:T(8,128)(2,1)}, bf16[512,256]{1,0:T(8,128)(2,1)S(1)}, u32[]{:S(2)}, u32[]{:S(2)}) collective-permute-start(bf16[512,256]{1,0:T(8,128)(2,1)} %copy-done.50), channel_id=1, source_target_pairs={{0,1},{1,0},{2,3},{3,2},{4,5},{5,4},{6,7},{7,6},{8,9},{9,8},{10,11... | collective-permute-start | bytes 786440 | tf_op jit(solution)/shard_map/ppermute | solution.py:77
  39.9 19.9 %collective-permute-start.11 = (bf16[256,512]{1,0:T(8,128)(2,1)}, bf16[256,512]{1,0:T(8,128)(2,1)S(1)}, u32[]{:S(2)}, u32[]{:S(2)}) collective-permute-start(bf16[256,512]{1,0:T(8,128)(2,1)} %copy-done.88), channel_id=1, source_target_pairs={{0,4},{4,0},{8,12},{12,8},{16,20},{20,16},{24,28},{28,24},{1,5},{5... | collective-permute-start | bytes 786440 | tf_op jit(solution)/shard_map/ppermute | solution.py:77
  41.4 18.4 %collective-permute-start.8 = (bf16[2,256,256]{2,1,0:T(8,128)(2,1)}, bf16[2,256,256]{2,1,0:T(8,128)(2,1)S(1)}, u32[]{:S(2)}, u32[]{:S(2)}) collective-permute-start(bf16[2,256,256]{2,1,0:T(8,128)(2,1)} %get-tuple-element.404), channel_id=1, source_target_pairs={{0,2},{1,3},{2,0},{3,1},{4,6},{5,7},{6,4},{7,5},{8,10},{9,11},{10,... | collective-permute-start | bytes 786440 | tf_op jit(solution)/shard_map/ppermute | solution.py:77
  41.9 17.3 %collective-permute-start.7 = (bf16[256,256]{1,0:T(8,128)(2,1)}, bf16[256,256]{1,0:T(8,128)(2,1)S(1)}, u32[]{:S(2)}, u32[]{:S(2)}) collective-permute-start(bf16[256,256]{1,0:T(8,128)(2,1)} %get-tuple-element.403), channel_id=1, source_target_pairs={{0,1},{1,0},{2,3},{3,2},{4,5},{5,4},{6,7},{7,6},{8,9},{9,8},{10,11... | collective-permute-start | bytes 393224 | tf_op jit(solution)/shard_map/ppermute | solution.py:77
  60.0 8.9 %collective-permute-start.16 = (bf16[2,256,256]{2,1,0:T(8,128)(2,1)}, bf16[2,256,256]{2,1,0:T(8,128)(2,1)S(1)}, u32[]{:S(2)}, u32[]{:S(2)}) collective-permute-start(bf16[2,256,256]{2,1,0:T(8,128)(2,1)} %get-tuple-element.424), channel_id=1, source_target_pairs={{0,2},{1,3},{2,0},{3,1},{4,6},{5,7},{6,4},{7,5},{8,10},{9,11},{10,... | collective-permute-start | bytes 786440 | tf_op jit(solution)/shard_map/ppermute | solution.py:77
  68.9 13.5 %collective-permute-start.18 = (bf16[256,1024]{1,0:T(8,128)(2,1)S(1)}, bf16[256,1024]{1,0:T(8,128)(2,1)S(1)}, u32[]{:S(2)}, u32[]{:S(2)}) collective-permute-start(bf16[256,1024]{1,0:T(8,128)(2,1)S(1)} %get-tuple-element.438.refs_0_), channel_id=1, source_target_pairs={{0,2},{1,3},{2,0},{3,1},{4,6},{5,7},{6,4},{7,5},{8,10},{9,11},{10,... | collective-permute-start | bytes 1572872 | tf_op jit(solution)/shard_map/ppermute | solution.py:77
  82.9 13.8 %collective-permute-start.21 = (bf16[256,1024]{1,0:T(8,128)(2,1)S(1)}, bf16[256,1024]{1,0:T(8,128)(2,1)S(1)}, u32[]{:S(2)}, u32[]{:S(2)}) collective-permute-start(bf16[256,1024]{1,0:T(8,128)(2,1)S(1)} %get-tuple-element.453.refs_0_), channel_id=1, source_target_pairs={{0,2},{1,3},{2,0},{3,1},{4,6},{5,7},{6,4},{7,5},{8,10},{9,11},{10,... | collective-permute-start | bytes 1572872 | tf_op jit(solution)/shard_map/ppermute | solution.py:77
  97.3 13.8 %collective-permute-start.25 = (bf16[256,1024]{1,0:T(8,128)(2,1)S(1)}, bf16[256,1024]{1,0:T(8,128)(2,1)S(1)}, u32[]{:S(2)}, u32[]{:S(2)}) collective-permute-start(bf16[256,1024]{1,0:T(8,128)(2,1)S(1)} %get-tuple-element.463), channel_id=1, source_target_pairs={{0,1},{1,0},{2,3},{3,2},{4,5},{5,4},{6,7},{7,6},{8,9},{9,8},{10,11... | collective-permute-start | bytes 1572872 | tf_op jit(solution)/shard_map/ppermute | solution.py:77
  98.9 14.0 %collective-permute-start.26 = (bf16[256,1024]{1,0:T(8,128)(2,1)S(1)}, bf16[256,1024]{1,0:T(8,128)(2,1)S(1)}, u32[]{:S(2)}, u32[]{:S(2)}) collective-permute-start(bf16[256,1024]{1,0:T(8,128)(2,1)S(1)} %add_convert_fusion.14), channel_id=1, source_target_pairs={{0,2},{1,3},{2,0},{3,1},{4,6},{5,7},{6,4},{7,5},{8,10},{9,11},{10,... | collective-permute-start | bytes 1572872 | tf_op jit(solution)/shard_map/ppermute | solution.py:77
  112.9 6.9 %collective-permute-start.28 = (bf16[256,1024]{1,0:T(8,128)(2,1)S(1)}, bf16[256,1024]{1,0:T(8,128)(2,1)S(1)}, u32[]{:S(2)}, u32[]{:S(2)}) collective-permute-start(bf16[256,1024]{1,0:T(8,128)(2,1)S(1)} %get-tuple-element.478), channel_id=1, source_target_pairs={{0,1},{1,0},{2,3},{3,2},{4,5},{5,4},{6,7},{7,6},{8,9},{9,8},{10,11... | collective-permute-start | bytes 1572872 | tf_op jit(solution)/shard_map/ppermute | solution.py:77
  112.9 6.9 %collective-permute-start.29 = (bf16[256,1024]{1,0:T(8,128)(2,1)S(1)}, bf16[256,1024]{1,0:T(8,128)(2,1)S(1)}, u32[]{:S(2)}, u32[]{:S(2)}) collective-permute-start(bf16[256,1024]{1,0:T(8,128)(2,1)S(1)} %get-tuple-element.479), channel_id=1, source_target_pairs={{0,1},{1,0},{2,3},{3,2},{4,5},{5,4},{6,7},{7,6},{8,9},{9,8},{10,11... | collective-permute-start | bytes 1572872 | tf_op jit(solution)/shard_map/ppermute | solution.py:77
  119.9 14.0 %collective-permute-start.31 = (bf16[256,1024]{1,0:T(8,128)(2,1)S(1)}, bf16[256,1024]{1,0:T(8,128)(2,1)S(1)}, u32[]{:S(2)}, u32[]{:S(2)}) collective-permute-start(bf16[256,1024]{1,0:T(8,128)(2,1)S(1)} %get-tuple-element.485.refs_0_), channel_id=1, source_target_pairs={{0,2},{1,3},{2,0},{3,1},{4,6},{5,7},{6,4},{7,5},{8,10},{9,11},{10,... | collective-permute-start | bytes 1572872 | tf_op jit(solution)/shard_map/ppermute | solution.py:77
  121.4 14.2 %collective-permute-start.30 = (bf16[256,1024]{1,0:T(8,128)(2,1)S(1)}, bf16[256,1024]{1,0:T(8,128)(2,1)S(1)}, u32[]{:S(2)}, u32[]{:S(2)}) collective-permute-start(bf16[256,1024]{1,0:T(8,128)(2,1)S(1)} %get-tuple-element.485.refs_0_), channel_id=1, source_target_pairs={{0,1},{1,0},{2,3},{3,2},{4,5},{5,4},{6,7},{7,6},{8,9},{9,8},{10,11... | collective-permute-start | bytes 1572872 | tf_op jit(solution)/shard_map/ppermute | solution.py:77
  134.1 27.1 %collective-permute-start.33 = (bf16[256,1024]{1,0:T(8,128)(2,1)S(1)}, bf16[256,1024]{1,0:T(8,128)(2,1)S(1)}, u32[]{:S(2)}, u32[]{:S(2)}) collective-permute-start(bf16[256,1024]{1,0:T(8,128)(2,1)S(1)} %add_convert_fusion.13), channel_id=1, source_target_pairs={{0,2},{1,3},{2,0},{3,1},{4,6},{5,7},{6,4},{7,5},{8,10},{9,11},{10,... | collective-permute-start | bytes 1572872 | tf_op jit(solution)/shard_map/ppermute | solution.py:77
  167.1 14.3 %collective-permute-start.36 = (bf16[256,1024]{1,0:T(8,128)(2,1)}, bf16[256,1024]{1,0:T(8,128)(2,1)S(1)}, u32[]{:S(2)}, u32[]{:S(2)}) collective-permute-start(bf16[256,1024]{1,0:T(8,128)(2,1)} %get-tuple-element.530.refs_0_), channel_id=1, source_target_pairs={{0,2},{1,3},{2,0},{3,1},{4,6},{5,7},{6,4},{7,5},{8,10},{9,11},{10,... | collective-permute-start | bytes 1572872 | tf_op jit(solution)/shard_map/ppermute | solution.py:77
  183.1 19.8 %collective-permute-start.39 = (bf16[256,1024]{1,0:T(8,128)(2,1)S(1)}, bf16[256,1024]{1,0:T(8,128)(2,1)S(1)}, u32[]{:S(2)}, u32[]{:S(2)}) collective-permute-start(bf16[256,1024]{1,0:T(8,128)(2,1)S(1)} %add_convert_fusion.12), channel_id=1, source_target_pairs={{0,2},{1,3},{2,0},{3,1},{4,6},{5,7},{6,4},{7,5},{8,10},{9,11},{10,... | collective-permute-start | bytes 1572872 | tf_op jit(solution)/shard_map/ppermute | solution.py:77
  188.5 25.1 %collective-permute-start.40 = (bf16[512,1024]{1,0:T(8,128)(2,1)S(1)}, bf16[512,1024]{1,0:T(8,128)(2,1)S(1)}, u32[]{:S(2)}, u32[]{:S(2)}) collective-permute-start(bf16[512,1024]{1,0:T(8,128)(2,1)S(1)} %constant_dynamic-slice_fusion.10), channel_id=1, source_target_pairs={{0,4},{4,0},{8,12},{12,8},{16,20},{20,16},{24,28},{28,24},{1,5},{5... | collective-permute-start | bytes 3145736 | tf_op jit(solution)/shard_map/ppermute | solution.py:77
  214.1 13.0 %collective-permute-start.44 = (bf16[256,1024]{1,0:T(8,128)(2,1)S(1)}, bf16[256,1024]{1,0:T(8,128)(2,1)S(1)}, u32[]{:S(2)}, u32[]{:S(2)}) collective-permute-start(bf16[256,1024]{1,0:T(8,128)(2,1)S(1)} %constant_dynamic-slice_fusion.9), channel_id=1, source_target_pairs={{0,8},{4,12},{8,0},{12,4},{16,24},{20,28},{24,16},{28,20},{1,9},{5... | collective-permute-start | bytes 1572872 | tf_op jit(solution)/shard_map/ppermute | solution.py:77
  214.9 12.7 %collective-permute-start.43 = (bf16[256,1024]{1,0:T(8,128)(2,1)S(1)}, bf16[256,1024]{1,0:T(8,128)(2,1)S(1)}, u32[]{:S(2)}, u32[]{:S(2)}) collective-permute-start(bf16[256,1024]{1,0:T(8,128)(2,1)S(1)} %add_convert_fusion.11), channel_id=1, source_target_pairs={{0,2},{1,3},{2,0},{3,1},{4,6},{5,7},{6,4},{7,5},{8,10},{9,11},{10,... | collective-permute-start | bytes 1572872 | tf_op jit(solution)/shard_map/ppermute | solution.py:77
  216.3 27.3 %collective-permute-start.48 = (bf16[512,1024]{1,0:T(8,128)(2,1)S(1)}, bf16[512,1024]{1,0:T(8,128)(2,1)S(1)}, u32[]{:S(2)}, u32[]{:S(2)}) collective-permute-start(bf16[512,1024]{1,0:T(8,128)(2,1)S(1)} %constant_dynamic-slice_fusion.8), channel_id=1, source_target_pairs={{0,4},{4,0},{8,12},{12,8},{16,20},{20,16},{24,28},{28,24},{1,5},{5... | collective-permute-start | bytes 3145736 | tf_op jit(solution)/shard_map/ppermute | solution.py:77
  227.6 8.7 %collective-permute-start.46 = (bf16[2,256,256]{2,1,0:T(8,128)(2,1)S(1)}, bf16[2,256,256]{2,1,0:T(8,128)(2,1)S(1)}, u32[]{:S(2)}, u32[]{:S(2)}) collective-permute-start(bf16[2,256,256]{2,1,0:T(8,128)(2,1)S(1)} %get-tuple-element.589), channel_id=1, source_target_pairs={{0,2},{1,3},{2,0},{3,1},{4,6},{5,7},{6,4},{7,5},{8,10},{9,11},{10,... | collective-permute-start | bytes 786440 | tf_op jit(solution)/shard_map/ppermute | solution.py:77
  229.1 7.3 %collective-permute-start.45 = (bf16[256,256]{1,0:T(8,128)(2,1)S(1)}, bf16[256,256]{1,0:T(8,128)(2,1)S(1)}, u32[]{:S(2)}, u32[]{:S(2)}) collective-permute-start(bf16[256,256]{1,0:T(8,128)(2,1)S(1)} %get-tuple-element.588), channel_id=1, source_target_pairs={{0,1},{1,0},{2,3},{3,2},{4,5},{5,4},{6,7},{7,6},{8,9},{9,8},{10,11... | collective-permute-start | bytes 393224 | tf_op jit(solution)/shard_map/ppermute | solution.py:77
  229.3 14.2 %collective-permute-start.47 = (bf16[128,1024]{1,0:T(8,128)(2,1)S(1)}, bf16[128,1024]{1,0:T(8,128)(2,1)S(1)}, u32[]{:S(2)}, u32[]{:S(2)}) collective-permute-start(bf16[128,1024]{1,0:T(8,128)(2,1)S(1)} %constant_dynamic-slice_fusion.7), channel_id=1, source_target_pairs={{0,16},{4,20},{8,24},{12,28},{16,0},{20,4},{24,8},{28,12},{1,17},{... | collective-permute-start | bytes 786440 | tf_op jit(solution)/shard_map/ppermute | solution.py:77
  236.4 8.5 %collective-permute-start.50 = (bf16[2,256,256]{2,1,0:T(8,128)(2,1)S(1)}, bf16[2,256,256]{2,1,0:T(8,128)(2,1)S(1)}, u32[]{:S(2)}, u32[]{:S(2)}) collective-permute-start(bf16[2,256,256]{2,1,0:T(8,128)(2,1)S(1)} %get-tuple-element.593), channel_id=1, source_target_pairs={{0,2},{1,3},{2,0},{3,1},{4,6},{5,7},{6,4},{7,5},{8,10},{9,11},{10,... | collective-permute-start | bytes 786440 | tf_op jit(solution)/shard_map/ppermute | solution.py:77
  237.0 11.0 %collective-permute-start.51 = (bf16[256,256]{1,0:T(8,128)(2,1)S(1)}, bf16[256,256]{1,0:T(8,128)(2,1)S(1)}, u32[]{:S(2)}, u32[]{:S(2)}) collective-permute-start(bf16[256,256]{1,0:T(8,128)(2,1)S(1)} %get-tuple-element.722), channel_id=1, source_target_pairs={{0,1},{1,0},{2,3},{3,2},{4,5},{5,4},{6,7},{7,6},{8,9},{9,8},{10,11... | collective-permute-start | bytes 393224 | tf_op jit(solution)/shard_map/ppermute | solution.py:77
  245.2 22.5 %collective-permute-start.55 = (bf16[272,1024]{1,0:T(8,128)(2,1)S(1)}, bf16[272,1024]{1,0:T(8,128)(2,1)S(1)}, u32[]{:S(2)}, u32[]{:S(2)}) collective-permute-start(bf16[272,1024]{1,0:T(8,128)(2,1)S(1)} %get-tuple-element.732), channel_id=1, source_target_pairs={{0,1},{1,0},{2,3},{3,2},{4,5},{5,4},{6,7},{7,6},{8,9},{9,8},{10,11... | collective-permute-start | bytes 1671176 | tf_op jit(solution)/shard_map/ppermute | solution.py:77
  245.3 22.5 %collective-permute-start.56 = (bf16[272,1024]{1,0:T(8,128)(2,1)S(1)}, bf16[272,1024]{1,0:T(8,128)(2,1)S(1)}, u32[]{:S(2)}, u32[]{:S(2)}) collective-permute-start(bf16[272,1024]{1,0:T(8,128)(2,1)S(1)} %get-tuple-element.731), channel_id=1, source_target_pairs={{0,1},{1,0},{2,3},{3,2},{4,5},{5,4},{6,7},{7,6},{8,9},{9,8},{10,11... | collective-permute-start | bytes 1671176 | tf_op jit(solution)/shard_map/ppermute | solution.py:77
  246.5 21.2 %collective-permute-start.54 = (bf16[256,1024]{1,0:T(8,128)(2,1)S(1)}, bf16[256,1024]{1,0:T(8,128)(2,1)S(1)}, u32[]{:S(2)}, u32[]{:S(2)}) collective-permute-start(bf16[256,1024]{1,0:T(8,128)(2,1)S(1)} %constant_dynamic-slice_fusion.6), channel_id=1, source_target_pairs={{0,8},{4,12},{8,0},{12,4},{16,24},{20,28},{24,16},{28,20},{1,9},{5... | collective-permute-start | bytes 1572872 | tf_op jit(solution)/shard_map/ppermute | solution.py:77
  248.1 19.7 %collective-permute-start.53 = (bf16[128,1024]{1,0:T(8,128)(2,1)S(1)}, bf16[128,1024]{1,0:T(8,128)(2,1)S(1)}, u32[]{:S(2)}, u32[]{:S(2)}) collective-permute-start(bf16[128,1024]{1,0:T(8,128)(2,1)S(1)} %add_convert_fusion.19), channel_id=1, source_target_pairs={{0,16},{4,20},{8,24},{12,28},{16,0},{20,4},{24,8},{28,12},{1,17},{... | collective-permute-start | bytes 786440 | tf_op jit(solution)/shard_map/ppermute | solution.py:77
  249.0 25.6 %collective-permute-start.57 = (bf16[512,1024]{1,0:T(8,128)(2,1)S(1)}, bf16[512,1024]{1,0:T(8,128)(2,1)S(1)}, u32[]{:S(2)}, u32[]{:S(2)}) collective-permute-start(bf16[512,1024]{1,0:T(8,128)(2,1)S(1)} %constant_dynamic-slice_fusion.5), channel_id=1, source_target_pairs={{0,4},{4,0},{8,12},{12,8},{16,20},{20,16},{24,28},{28,24},{1,5},{5... | collective-permute-start | bytes 3145736 | tf_op jit(solution)/shard_map/ppermute | solution.py:77
  268.0 27.2 %collective-permute-start.61 = (bf16[272,1024]{1,0:T(8,128)(2,1)S(1)}, bf16[272,1024]{1,0:T(8,128)(2,1)S(1)}, u32[]{:S(2)}, u32[]{:S(2)}) collective-permute-start(bf16[272,1024]{1,0:T(8,128)(2,1)S(1)} %add_convert_fusion.7), channel_id=1, source_target_pairs={{0,2},{1,3},{2,0},{3,1},{4,6},{5,7},{6,4},{7,5},{8,10},{9,11},{10,... | collective-permute-start | bytes 1671176 | tf_op jit(solution)/shard_map/ppermute | solution.py:77
  269.5 25.7 %collective-permute-start.59 = (bf16[128,1024]{1,0:T(8,128)(2,1)S(1)}, bf16[128,1024]{1,0:T(8,128)(2,1)S(1)}, u32[]{:S(2)}, u32[]{:S(2)}) collective-permute-start(bf16[128,1024]{1,0:T(8,128)(2,1)S(1)} %constant_dynamic-slice_fusion.4), channel_id=1, source_target_pairs={{0,16},{4,20},{8,24},{12,28},{16,0},{20,4},{24,8},{28,12},{1,17},{... | collective-permute-start | bytes 786440 | tf_op jit(solution)/shard_map/ppermute | solution.py:77
  269.8 25.4 %collective-permute-start.58 = (bf16[256,1024]{1,0:T(8,128)(2,1)S(1)}, bf16[256,1024]{1,0:T(8,128)(2,1)S(1)}, u32[]{:S(2)}, u32[]{:S(2)}) collective-permute-start(bf16[256,1024]{1,0:T(8,128)(2,1)S(1)} %pad_maximum_fusion.8), channel_id=1, source_target_pairs={{0,8},{4,12},{8,0},{12,4},{16,24},{20,28},{24,16},{28,20},{1,9},{5... | collective-permute-start | bytes 1572872 | tf_op jit(solution)/shard_map/ppermute | solution.py:77
  275.6 19.6 %collective-permute-start.60 = (bf16[192,1024]{1,0:T(8,128)(2,1)S(1)}, bf16[192,1024]{1,0:T(8,128)(2,1)S(1)}, u32[]{:S(2)}, u32[]{:S(2)}) collective-permute-start(bf16[192,1024]{1,0:T(8,128)(2,1)S(1)} %constant_dynamic-slice_fusion.2), channel_id=1, source_target_pairs={{0,4},{4,0},{8,12},{12,8},{16,20},{20,16},{24,28},{28,24},{1,5},{5... | collective-permute-start | bytes 1179656 | tf_op jit(solution)/shard_map/ppermute | solution.py:77
  276.1 26.0 %collective-permute-start.62 = (bf16[256,1024]{1,0:T(8,128)(2,1)S(1)}, bf16[256,1024]{1,0:T(8,128)(2,1)S(1)}, u32[]{:S(2)}, u32[]{:S(2)}) collective-permute-start(bf16[256,1024]{1,0:T(8,128)(2,1)S(1)} %constant_dynamic-slice_fusion.3), channel_id=1, source_target_pairs={{0,8},{4,12},{8,0},{12,4},{16,24},{20,28},{24,16},{28,20},{1,9},{5... | collective-permute-start | bytes 1572872 | tf_op jit(solution)/shard_map/ppermute | solution.py:77
  295.3 23.6 %collective-permute-start.65 = (bf16[512,1024]{1,0:T(8,128)(2,1)S(1)}, bf16[512,1024]{1,0:T(8,128)(2,1)S(1)}, u32[]{:S(2)}, u32[]{:S(2)}) collective-permute-start(bf16[512,1024]{1,0:T(8,128)(2,1)S(1)} %pad_maximum_fusion.4.own_ref), channel_id=1, source_target_pairs={{0,4},{4,0},{8,12},{12,8},{16,20},{20,16},{24,28},{28,24},{1,5},{5... | collective-permute-start | bytes 3145736 | tf_op jit(solution)/shard_map/ppermute | solution.py:77
  295.7 22.3 %collective-permute-start.63 = (bf16[128,1024]{1,0:T(8,128)(2,1)S(1)}, bf16[128,1024]{1,0:T(8,128)(2,1)}, u32[]{:S(2)}, u32[]{:S(2)}) collective-permute-start(bf16[128,1024]{1,0:T(8,128)(2,1)S(1)} %add_convert_fusion.18), channel_id=1, source_target_pairs={{0,16},{4,20},{8,24},{12,28},{16,0},{20,4},{24,8},{28,12},{1,17},{... | collective-permute-start | bytes 786440 | tf_op jit(solution)/shard_map/ppermute | solution.py:77
  302.1 16.6 %collective-permute-start.67 = (bf16[2,512,256]{2,1,0:T(8,128)(2,1)S(1)}, bf16[2,512,256]{2,1,0:T(8,128)(2,1)S(1)}, u32[]{:S(2)}, u32[]{:S(2)}) collective-permute-start(bf16[2,512,256]{2,1,0:T(8,128)(2,1)S(1)} %copy-done.83), channel_id=1, source_target_pairs={{0,2},{1,3},{2,0},{3,1},{4,6},{5,7},{6,4},{7,5},{8,10},{9,11},{10,... | collective-permute-start | bytes 1572872 | tf_op jit(solution)/shard_map/ppermute | solution.py:77
  303.2 14.8 %collective-permute-start.66 = (bf16[512,256]{1,0:T(8,128)(2,1)S(1)}, bf16[512,256]{1,0:T(8,128)(2,1)S(1)}, u32[]{:S(2)}, u32[]{:S(2)}) collective-permute-start(bf16[512,256]{1,0:T(8,128)(2,1)S(1)} %copy-done.87), channel_id=1, source_target_pairs={{0,1},{1,0},{2,3},{3,2},{4,5},{5,4},{6,7},{7,6},{8,9},{9,8},{10,11... | collective-permute-start | bytes 786440 | tf_op jit(solution)/shard_map/ppermute | solution.py:77
  303.5 15.3 %collective-permute-start.64 = (bf16[128,1024]{1,0:T(8,128)(2,1)S(1)}, bf16[128,1024]{1,0:T(8,128)(2,1)S(1)}, u32[]{:S(2)}, u32[]{:S(2)}) collective-permute-start(bf16[128,1024]{1,0:T(8,128)(2,1)S(1)} %constant_dynamic-slice_fusion.1), channel_id=1, source_target_pairs={{0,16},{4,20},{8,24},{12,28},{16,0},{20,4},{24,8},{28,12},{1,17},{... | collective-permute-start | bytes 786440 | tf_op jit(solution)/shard_map/ppermute | solution.py:77
  320.4 24.3 %collective-permute-start.72 = (bf16[2,1024,256]{2,1,0:T(8,128)(2,1)}, bf16[2,1024,256]{2,1,0:T(8,128)(2,1)}, u32[]{:S(2)}, u32[]{:S(2)}) collective-permute-start(bf16[2,1024,256]{2,1,0:T(8,128)(2,1)} %get-tuple-element.657), channel_id=1, source_target_pairs={{0,1},{1,0},{2,3},{3,2},{4,5},{5,4},{6,7},{7,6},{8,9},{9,8},{10,11... | collective-permute-start | bytes 3145736 | tf_op jit(solution)/shard_map/ppermute | solution.py:77
  321.7 17.1 %collective-permute-start.73 = (f32[5,1024]{1,0:T(8,128)S(1)}, f32[5,1024]{1,0:T(8,128)S(1)}, u32[]{:S(2)}, u32[]{:S(2)}) collective-permute-start(f32[5,1024]{1,0:T(8,128)S(1)} %select_maximum_fusion), channel_id=1, source_target_pairs={{0,4},{4,0},{8,12},{12,8},{16,20},{20,16},{24,28},{28,24},{1,5},{5... | collective-permute-start | bytes 61448 | tf_op jit(solution)/shard_map/ppermute | solution.py:77
  321.7 17.6 %collective-permute-start.69 = (bf16[320,1024]{1,0:T(8,128)(2,1)}, bf16[320,1024]{1,0:T(8,128)(2,1)S(1)}, u32[]{:S(2)}, u32[]{:S(2)}) collective-permute-start(bf16[320,1024]{1,0:T(8,128)(2,1)} %fusion.4), channel_id=1, source_target_pairs={{0,4},{4,0},{8,12},{12,8},{16,20},{20,16},{24,28},{28,24},{1,5},{5... | collective-permute-start | bytes 1966088 | tf_op jit(solution)/shard_map/ppermute | solution.py:77
  324.8 19.9 %collective-permute-start.70 = (bf16[256,1024]{1,0:T(8,128)(2,1)S(1)}, bf16[256,1024]{1,0:T(8,128)(2,1)S(1)}, u32[]{:S(2)}, u32[]{:S(2)}) collective-permute-start(bf16[256,1024]{1,0:T(8,128)(2,1)S(1)} %pad_maximum_fusion.9), channel_id=1, source_target_pairs={{0,8},{4,12},{8,0},{12,4},{16,24},{20,28},{24,16},{28,20},{1,9},{5... | collective-permute-start | bytes 1572872 | tf_op jit(solution)/shard_map/ppermute | solution.py:77
  328.0 16.7 %collective-permute-start.71 = (bf16[128,1024]{1,0:T(8,128)(2,1)S(1)}, bf16[128,1024]{1,0:T(8,128)(2,1)S(1)}, u32[]{:S(2)}, u32[]{:S(2)}) collective-permute-start(bf16[128,1024]{1,0:T(8,128)(2,1)S(1)} %add_convert_fusion.17), channel_id=1, source_target_pairs={{0,16},{4,20},{8,24},{12,28},{16,0},{20,4},{24,8},{28,12},{1,17},{... | collective-permute-start | bytes 786440 | tf_op jit(solution)/shard_map/ppermute | solution.py:77
  348.0 28.4 %collective-permute-start.77 = (bf16[512,1024]{1,0:T(8,128)(2,1)S(1)}, bf16[512,1024]{1,0:T(8,128)(2,1)S(1)}, u32[]{:S(2)}, u32[]{:S(2)}) collective-permute-start(bf16[512,1024]{1,0:T(8,128)(2,1)S(1)} %pad_maximum_fusion.5.own_ref), channel_id=1, source_target_pairs={{0,4},{4,0},{8,12},{12,8},{16,20},{20,16},{24,28},{28,24},{1,5},{5... | collective-permute-start | bytes 3145736 | tf_op jit(solution)/shard_map/ppermute | solution.py:77
  349.8 26.6 %collective-permute-start.78 = (bf16[256,1024]{1,0:T(8,128)(2,1)}, bf16[256,1024]{1,0:T(8,128)(2,1)}, u32[]{:S(2)}, u32[]{:S(2)}) collective-permute-start(bf16[256,1024]{1,0:T(8,128)(2,1)} %pad_maximum_fusion.10), channel_id=1, source_target_pairs={{0,8},{4,12},{8,0},{12,4},{16,24},{20,28},{24,16},{28,20},{1,9},{5... | collective-permute-start | bytes 1572872 | tf_op jit(solution)/shard_map/ppermute | solution.py:77
  350.8 22.5 %collective-permute-start.74 = (bf16[128,1024]{1,0:T(8,128)(2,1)}, bf16[128,1024]{1,0:T(8,128)(2,1)}, u32[]{:S(2)}, u32[]{:S(2)}) collective-permute-start(bf16[128,1024]{1,0:T(8,128)(2,1)} %get-tuple-element.712), channel_id=1, source_target_pairs={{0,8},{4,12},{8,0},{12,4},{16,24},{20,28},{24,16},{28,20},{1,9},{5... | collective-permute-start | bytes 786440 | tf_op jit(solution)/shard_map/ppermute | solution.py:77
  351.8 24.6 %collective-permute-start.75 = (bf16[128,1024]{1,0:T(8,128)(2,1)}, bf16[128,1024]{1,0:T(8,128)(2,1)}, u32[]{:S(2)}, u32[]{:S(2)}) collective-permute-start(bf16[128,1024]{1,0:T(8,128)(2,1)} %get-tuple-element.713), channel_id=1, source_target_pairs={{0,16},{4,20},{8,24},{12,28},{16,0},{20,4},{24,8},{28,12},{1,17},{... | collective-permute-start | bytes 786440 | tf_op jit(solution)/shard_map/ppermute | solution.py:77
  353.5 22.9 %collective-permute-start.76 = (bf16[128,1024]{1,0:T(8,128)(2,1)}, bf16[128,1024]{1,0:T(8,128)(2,1)}, u32[]{:S(2)}, u32[]{:S(2)}) collective-permute-start(bf16[128,1024]{1,0:T(8,128)(2,1)} %get-tuple-element.711), channel_id=1, source_target_pairs={{0,24},{4,28},{8,16},{12,20},{16,8},{20,12},{24,0},{28,4},{1,25},{... | collective-permute-start | bytes 786440 | tf_op jit(solution)/shard_map/ppermute | solution.py:77
  379.4 31.6 %collective-permute-start.82 = (bf16[512,1024]{1,0:T(8,128)(2,1)S(1)}, bf16[512,1024]{1,0:T(8,128)(2,1)S(1)}, u32[]{:S(2)}, u32[]{:S(2)}) collective-permute-start(bf16[512,1024]{1,0:T(8,128)(2,1)S(1)} %pad_maximum_fusion.6.own_ref), channel_id=1, source_target_pairs={{0,4},{4,0},{8,12},{12,8},{16,20},{20,16},{24,28},{28,24},{1,5},{5... | collective-permute-start | bytes 3145736 | tf_op jit(solution)/shard_map/ppermute | solution.py:77
  382.3 9.8 %collective-permute-start.83 = (bf16[1024,256]{1,0:T(8,128)(2,1)S(1)}, bf16[1024,256]{1,0:T(8,128)(2,1)S(1)}, u32[]{:S(2)}, u32[]{:S(2)}) collective-permute-start(bf16[1024,256]{1,0:T(8,128)(2,1)S(1)} %fusion.2), channel_id=1, source_target_pairs={{0,2},{1,3},{2,0},{3,1},{4,6},{5,7},{6,4},{7,5},{8,10},{9,11},{10,... | collective-permute-start | bytes 1572872 | tf_op jit(solution)/shard_map/ppermute | solution.py:77
  383.6 14.0 %collective-permute-start.79 = (bf16[128,1024]{1,0:T(8,128)(2,1)S(1)}, bf16[128,1024]{1,0:T(8,128)(2,1)S(1)}, u32[]{:S(2)}, u32[]{:S(2)}) collective-permute-start(bf16[128,1024]{1,0:T(8,128)(2,1)S(1)} %add_convert_fusion.16), channel_id=1, source_target_pairs={{0,8},{4,12},{8,0},{12,4},{16,24},{20,28},{24,16},{28,20},{1,9},{5... | collective-permute-start | bytes 786440 | tf_op jit(solution)/shard_map/ppermute | solution.py:77
  388.8 17.5 %collective-permute-start.80 = (bf16[128,1024]{1,0:T(8,128)(2,1)S(1)}, bf16[128,1024]{1,0:T(8,128)(2,1)S(1)}, u32[]{:S(2)}, u32[]{:S(2)}) collective-permute-start(bf16[128,1024]{1,0:T(8,128)(2,1)S(1)} %add_convert_fusion.16), channel_id=1, source_target_pairs={{0,16},{4,20},{8,24},{12,28},{16,0},{20,4},{24,8},{28,12},{1,17},{... | collective-permute-start | bytes 786440 | tf_op jit(solution)/shard_map/ppermute | solution.py:77
  388.9 22.1 %collective-permute-start.81 = (bf16[128,1024]{1,0:T(8,128)(2,1)S(1)}, bf16[128,1024]{1,0:T(8,128)(2,1)S(1)}, u32[]{:S(2)}, u32[]{:S(2)}) collective-permute-start(bf16[128,1024]{1,0:T(8,128)(2,1)S(1)} %add_convert_fusion.16), channel_id=1, source_target_pairs={{0,24},{4,28},{8,16},{12,20},{16,8},{20,12},{24,0},{28,4},{1,25},{... | collective-permute-start | bytes 786440 | tf_op jit(solution)/shard_map/ppermute | solution.py:77
  413.0 12.8 %collective-permute-start.84 = (bf16[2,1024,256]{2,1,0:T(8,128)(2,1)}, bf16[2,1024,256]{2,1,0:T(8,128)(2,1)}, u32[]{:S(2)}, u32[]{:S(2)}) collective-permute-start(bf16[2,1024,256]{2,1,0:T(8,128)(2,1)} %get-tuple-element.687), channel_id=1, source_target_pairs={{0,1},{1,0},{2,3},{3,2},{4,5},{5,4},{6,7},{7,6},{8,9},{9,8},{10,11... | collective-permute-start | bytes 3145736 | tf_op jit(solution)/shard_map/ppermute | solution.py:77
  414.3 25.4 %collective-permute-start.86 = (bf16[512,1024]{1,0:T(8,128)(2,1)}, bf16[512,1024]{1,0:T(8,128)(2,1)}, u32[]{:S(2)}, u32[]{:S(2)}) collective-permute-start(bf16[512,1024]{1,0:T(8,128)(2,1)} %pad_maximum_fusion.7.own_ref), channel_id=1, source_target_pairs={{0,4},{4,0},{8,12},{12,8},{16,20},{20,16},{24,28},{28,24},{1,5},{5... | collective-permute-start | bytes 3145736 | tf_op jit(solution)/shard_map/ppermute | solution.py:77
  415.3 8.5 %collective-permute-start.87 = (f32[5,1024]{1,0:T(8,128)S(1)}, f32[5,1024]{1,0:T(8,128)S(1)}, u32[]{:S(2)}, u32[]{:S(2)}) collective-permute-start(f32[5,1024]{1,0:T(8,128)S(1)} %fusion.21), channel_id=1, source_target_pairs={{0,8},{4,12},{8,0},{12,4},{16,24},{20,28},{24,16},{28,20},{1,9},{5... | collective-permute-start | bytes 61448 | tf_op jit(solution)/shard_map/ppermute | solution.py:77
  423.8 6.7 %collective-permute-start.88 = (f32[5,1024]{1,0:T(8,128)S(1)}, f32[5,1024]{1,0:T(8,128)S(1)}, u32[]{:S(2)}, u32[]{:S(2)}) collective-permute-start(f32[5,1024]{1,0:T(8,128)S(1)} %add.262), channel_id=1, source_target_pairs={{0,16},{4,20},{8,24},{12,28},{16,0},{20,4},{24,8},{28,12},{1,17},{... | collective-permute-start | bytes 61448 | tf_op jit(solution)/shard_map/ppermute | solution.py:77
  427.0 17.4 %collective-permute-start.85 = (bf16[1024,256]{1,0:T(8,128)(2,1)S(1)}, bf16[1024,256]{1,0:T(8,128)(2,1)S(1)}, u32[]{:S(2)}, u32[]{:S(2)}) collective-permute-start(bf16[1024,256]{1,0:T(8,128)(2,1)S(1)} %fusion), channel_id=1, source_target_pairs={{0,2},{1,3},{2,0},{3,1},{4,6},{5,7},{6,4},{7,5},{8,10},{9,11},{10,... | collective-permute-start | bytes 1572872 | tf_op jit(solution)/shard_map/ppermute | solution.py:77
  (123 other events, 970.6 us)

commit v3 on v2

--- a/solution.py
+++ b/solution.py
@@ -354,19 +354,16 @@
         old_k, old_v = refs.pop(0), refs.pop(0)
         refs = refs[7:]
     k_ref, ve_ref, v_ref, kt_ref, qt_ref, ot_ref, inv_ref, qf_ref, kf_ref, o_ref = refs[:10]
-    near_ref, far_ref, raw, acc = refs[10:]
+    near_ref, far_ref, raw, acc, joined = refs[10:]
     me, length = info[0], info[1]
     cols = heads * HD
     pair = min(2, heads)
     for e in range(n_head):
         first = pl.multiple_of((me ^ e) * share, share)
-        for third in range(3):
-            rows = slice(third * cols, (third + 1) * cols)
-            term = dot(w_ref[rows, pl.ds(first, share)], x_refs[e][...], 1, 1)
-            if e == 0:
-                raw[rows, :] = term
-            else:
-                raw[rows, :] += term
+        joined[:, pl.ds(first, share)] = x_refs[e][...]
+    for third in range(3):
+        rows = slice(third * cols, (third + 1) * cols)
+        raw[rows, :] = dot(w_ref[rows, :], joined[...], 1, 1)
 
     def raw_row(part, h):
         return ((h // pair * 3 + part) * pair + h % pair) * HD
@@ -495,6 +492,7 @@
             scratch_shapes=[
                 pltpu.VMEM((3 * cols, chunk_len), F32),
                 pltpu.VMEM((heads, VALUE_ROWS, QUERIES), F32),
+                pltpu.VMEM((chunk_len, model), BF16),
             ],
         ),
         out_shape=[

time: 450 us -> 452 us (level)
  Pallas kernels: 202 us -> 192 us
  starting transfers between devices: 72.7 us -> 79.7 us
    pallas_call x2, Pallas kernels: 35.6 us -> 28.2 us  [unattend(): pl.pallas_call(functools.partial(unattend_kernel, n_head, chunks, row_len...]
    ppermute x89, starting transfers between devices: 72.7 us -> 79.7 us  [swap(): return lax.ppermute(value, axis, [(i, i ^ mask) for i in range(size)])]
  transfers between devices with their start and end apart: 89 -> 89, of which waited for: 29 -> 31; matrix products, arithmetic and copies ran while one was open for 8% -> 8% of each run, Pallas kernels for 45% -> 43%
where the time goes in v3:
time: 452 us; the launch traced here: 447 us
  Pallas kernels  192 us (42%)
  waiting for transfers between devices  113 us (25%)
  starting transfers between devices  79.7 us (18%)
  other arithmetic  28.9 us (6%)
  local copies, waits for them, and re-layouts  19.1 us (4%)
  matrix products  12 us (3%)
    ppermute x89, waiting for transfers between devices, swap(): return lax.ppermute(value, axis, [(i, i ^ mask) for i in range(size)])  113 us
    ppermute x89, starting transfers between devices, swap(): return lax.ppermute(value, axis, [(i, i ^ mask) for i in range(size)])  79.7 us
    pallas_call x2, Pallas kernels, unfeed(): pl.pallas_call(functools.partial(unfeed_kernel, n_head, n_in, rows), grid...  38.6 us
    pallas_call x2, Pallas kernels, unattend(): pl.pallas_call(functools.partial(unattend_kernel, n_head, chunks, row_len...  28.2 us
    pallas_call x2, Pallas kernels, attend_chunk(): pl.pallas_call(body, grid_spec=pltpu.PrefetchScalarGridSpec(num_scalar_pr...  26.9 us
    pallas_call x2, Pallas kernels, feed(): pl.pallas_call(functools.partial(feed_kernel, n_head, rows), grid=(hidden...  21.3 us
    pallas_call x2, Pallas kernels, spread(): pl.pallas_call(functools.partial(spread_kernel, n_head, share, len(d_all)...  18.9 us
    dot_general x4, matrix products, dot(): lax.dot_general(left, right, (((left_dim,), (right_dim,)), ((), ())), pre...  12 us
  transfers between devices with their start and end apart: 89, of which 31 were waited for; matrix products, arithmetic and copies ran while one was open for 8% of the time, Pallas kernels for 43%

profile of v3, /device:TPU:8, one launch (start us, length us, event | category | flops | bytes accessed | tf_op | source)
XLA Modules:
  0.0 447.1 jit_solution(346135770238707829)
XLA Ops:
  4.4 3.3 subtract_convert_fusion
  14.0 1.8 collective-permute-done.refs_2_.refs_10_
  16.4 1.8 multiply_sine_fusion
  20.3 12.7 %attend.2 = (bf16[4,2048,64]{2,1,0:T(8,128)(2,1)}, bf16[4,80,2048]{2,1,0:T(8,128)(2,1)}, bf16[4,2048,64]{2,1,0:T(8,128)(2,1)}, bf16[256,2048]{1,0:T(8,128)(2,1)}...) custom-call(s32[10]{0:T(128)S(1)} %pad_add_fusion.info, ...), custom_call_target="tpu_custom_call" | custom-call | flops 8000000000 | bytes 8000000 | tf_op jit(solution)/shard_map/attend/pallas_call | solution.py:470
  33.0 4.7 %collective-permute-done.4.refs_2_.refs_10_.refs_6_ = bf16[1024,256]{1,0:T(8,128)(2,1)} collective-permute-done((bf16[1024,256]{1,0:T(8,128)(2,1)S(1)}, bf16[1024,256]{1,0:T(8,128)(2,1)}, u32[]{:S(2)}, u32[]{:S(2)}) %collective-permute-start.4) | collective-permute-done | bytes 524320 | tf_op jit(solution)/shard_map/ppermute | solution.py:77
  41.9 14.2 %attend.3 = (bf16[4,2048,64]{2,1,0:T(8,128)(2,1)}, bf16[4,80,2048]{2,1,0:T(8,128)(2,1)}, bf16[4,2048,64]{2,1,0:T(8,128)(2,1)}, bf16[256,2048]{1,0:T(8,128)(2,1)}...) custom-call(s32[10]{0:T(128)S(1)} %pad_add_fusion.info, ...), custom_call_target="tpu_custom_call", output_to_operand_aliasing={{0}: (10, {}), {1}: (11, {}), {2}: (12, {}), {3}: (13, {}),... | custom-call | flops 8000000000 | bytes 8000000 | tf_op jit(solution)/shard_map/attend/pallas_call | solution.py:470
  61.3 3.0 project.2
  64.4 2.8 collective-permute-done.16
  70.2 4.0 project.3
  74.2 6.5 %collective-permute-done.18.refs_2_ = bf16[256,1024]{1,0:T(8,128)(2,1)S(1)} collective-permute-done((bf16[256,1024]{1,0:T(8,128)(2,1)S(1)}, bf16[256,1024]{1,0:T(8,128)(2,1)S(1)}, u32[]{:S(2)}, u32[]{:S(2)}) %collective-permute-start.18) | collective-permute-done | bytes 524320 | tf_op jit(solution)/shard_map/ppermute | solution.py:77
  83.3 10.7 %feed.2 = (bf16[1024,1024]{1,0:T(8,128)(2,1)}, bf16[1024,1024]{1,0:T(8,128)(2,1)}, bf16[1024,1024]{1,0:T(8,128)(2,1)}, bf16[1024,1024]{1,0:T(8,128)(2,1)}, bf16[...) custom-call(bf16[256,1024]{1,0:T(8,128)(2,1)S(1)} %get-tuple-element, ...), custom_call_target="tpu_custom_call" | custom-call | flops 6442450944 | bytes 20000000 | tf_op jit(solution)/shard_map/feed/pallas_call | solution.py:734
  98.7 10.6 %feed.3 = (bf16[1024,1024]{1,0:T(8,128)(2,1)}, bf16[1024,1024]{1,0:T(8,128)(2,1)}, bf16[1024,1024]{1,0:T(8,128)(2,1)}, bf16[1024,1024]{1,0:T(8,128)(2,1)}, bf16[...) custom-call(bf16[256,1024]{1,0:T(8,128)(2,1)S(1)} %get-tuple-element, ...), custom_call_target="tpu_custom_call" | custom-call | flops 6442450944 | bytes 20000000 | tf_op jit(solution)/shard_map/feed/pallas_call | solution.py:734
  109.4 1.8 collective-permute-done.26.refs_2_
  111.8 2.4 collective-permute-done.27.refs_6_
  114.2 3.9 middle.2
  119.7 12.4 %collective-permute-done.31.refs_2_ = bf16[256,1024]{1,0:T(8,128)(2,1)S(1)} collective-permute-done((bf16[256,1024]{1,0:T(8,128)(2,1)S(1)}, bf16[256,1024]{1,0:T(8,128)(2,1)S(1)}, u32[]{:S(2)}, u32[]{:S(2)}) %collective-permute-start.31) | collective-permute-done | bytes 524320 | tf_op jit(solution)/shard_map/ppermute | solution.py:77
  134.1 25.4 %unfeed.2 = (bf16[1024,1024]{1,0:T(8,128)(2,1)}, bf16[1024,1024]{1,0:T(8,128)(2,1)}, f32[1,1024]{1,0:T(1,128)S(1)}, f32[1,1024]{1,0:T(1,128)S(1)}, bf16[256,1024...) custom-call(bf16[256,1024]{1,0:T(8,128)(2,1)S(1)} %get-tuple-element, ...), custom_call_target="tpu_custom_call" | custom-call | flops 6442450944 | bytes 20000000 | tf_op jit(solution)/shard_map/unfeed/pallas_call | solution.py:968
  160.1 4.4 middle.3
  166.7 10.7 %weigh_feed.1 = (bf16[1024,1024]{1,0:T(8,128)(2,1)}, bf16[1024,1024]{1,0:T(8,128)(2,1)}, bf16[1024,1024]{1,0:T(8,128)(2,1)}) custom-call(bf16[1024,1024]{1,0:T(8,128)(2,1)S(1)} %copy-done.53, bf16[1024,1024]{1,0:T(8,128)(2,1)S(1)} %copy-done.54, bf16[1024,1024]{1,0:T(8,128)(2,1)} %get-tuple-element.518.z_ref, bf16[1024,1024]{1,0:T(8,128)(2,1)} %get-tuple-element.500.u_ref, ...), custom_call_target="tpu_custom_call" | custom-call | flops 6442450944 | bytes 20000000 | tf_op jit(solution)/shard_map/weigh_feed/pallas_call | solution.py:863
  177.4 2.2 collective-permute-done.36.refs_2_
  184.3 2.4 add_convert_fusion.2
  186.8 3.0 collective-permute-start.40
  189.8 13.2 %unfeed.3 = (bf16[1024,1024]{1,0:T(8,128)(2,1)}, bf16[1024,1024]{1,0:T(8,128)(2,1)}, f32[1,1024]{1,0:T(1,128)S(1)}, f32[1,1024]{1,0:T(1,128)S(1)}, bf16[256,1024...) custom-call(bf16[1024,1024]{1,0:T(8,128)(2,1)S(1)} %join.1.refs_0_, ...), custom_call_target="tpu_custom_call" | custom-call | flops 6442450944 | bytes 20000000 | tf_op jit(solution)/shard_map/unfeed/pallas_call | solution.py:968
  203.6 4.6 %add_convert_fusion.1 = bf16[1024,1024]{1,0:T(8,128)(2,1)S(1)} fusion(bf16[1024,1024]{1,0:T(8,128)(2,1)} %get-tuple-element.549, bf16[1024,1024]{1,0:T(8,128)(2,1)S(1)} %copy-done.93, bf16[1024,1024]{1,0:T(8,128)(2,1)} %get-tuple-element.550), kind=kOutput, calls=%fused_computation.1 | convolution fusion | flops 2150629376 | bytes 8388608 | tf_op jit(solution)/shard_map/dot_general | solution.py:25
  208.2 4.9 %collective-permute-done.40 = bf16[512,1024]{1,0:T(8,128)(2,1)S(1)} collective-permute-done((bf16[512,1024]{1,0:T(8,128)(2,1)S(1)}, bf16[512,1024]{1,0:T(8,128)(2,1)S(1)}, u32[]{:S(2)}, u32[]{:S(2)}) %collective-permute-start.40) | collective-permute-done | bytes 1048608 | tf_op jit(solution)/shard_map/ppermute | solution.py:77
  216.6 2.5 add_convert_fusion
  219.1 4.4 unproject.2
  223.5 3.6 collective-permute-done.44
  229.3 2.7 collective-permute-start.47
  232.0 4.4 unproject.3
  237.6 2.5 convolution_convert_fusion
  240.2 3.6 collective-permute-done.47
  250.0 14.1 %unattend.2 = (bf16[3,128,2048]{2,1,0:T(8,128)(2,1)}, f32[128,1]{1,0:T(8,128)S(1)}) custom-call(s32[10]{0:T(128)S(1)} %pad_add_fusion.info, bf16[256,256]{1,0:T(8,128)(2,1)S(1)} %get-tuple-element.624.refs_0_, bf16[256,256]{1,0:T(8,128)(2,1)S(1)} %collective-permute-done.45.refs_1_, bf16[256,256]{1,0:T(8,128)(2,1)S(1)} %get-tuple-element.723.refs_2_, ...), custom_call_target="tpu_custom_call" | custom-call | flops 22000001024 | bytes 6000000 | tf_op jit(solution)/shard_map/unattend/pallas_call | solution.py:599
  264.1 3.0 collective-permute-done.53
  268.2 1.8 collective-permute-start.59
  270.0 1.9 collective-permute-start.58
  272.0 3.0 weigh.2
  277.6 14.1 %unattend.3 = (bf16[3,128,2048]{2,1,0:T(8,128)(2,1)}, f32[128,1]{1,0:T(8,128)S(1)}) custom-call(s32[10]{0:T(128)S(1)} %pad_add_fusion.info, bf16[256,256]{1,0:T(8,128)(2,1)S(1)} %get-tuple-element.624.refs_0_, bf16[256,256]{1,0:T(8,128)(2,1)S(1)} %collective-permute-done.45.refs_1_, bf16[256,256]{1,0:T(8,128)(2,1)S(1)} %get-tuple-element.723.refs_2_, ...), custom_call_target="tpu_custom_call" | custom-call | flops 22000001024 | bytes 6000000 | tf_op jit(solution)/shard_map/unattend/pallas_call | solution.py:599
  291.8 3.2 collective-permute-start.65
  296.8 3.2 weigh.3
  300.0 1.9 collective-permute-done.62
  303.2 4.8 %collective-permute-start.64 = (bf16[128,1024]{1,0:T(8,128)(2,1)S(1)}, bf16[128,1024]{1,0:T(8,128)(2,1)S(1)}, u32[]{:S(2)}, u32[]{:S(2)}) collective-permute-start(bf16[128,1024]{1,0:T(8,128)(2,1)S(1)} %constant_dynamic-slice_fusion.1), channel_id=1, source_target_pairs={{0,16},{4,20},{8,24},{12,28},{16,0},{20,4},{24,8},{28,12},{1,17},{... | collective-permute-start | bytes 786440 | tf_op jit(solution)/shard_map/ppermute | solution.py:77
  309.5 9.6 %spread.2 = (bf16[1024,256]{1,0:T(8,128)(2,1)}, bf16[1024,256]{1,0:T(8,128)(2,1)}, bf16[2,1024,256]{2,1,0:T(8,128)(2,1)}) custom-call(s32[10]{0:T(128)S(1)} %pad_add_fusion.info, bf16[384,2048]{1,0:T(8,128)(2,1)} %bitcast.76, bf16[384,2048]{1,0:T(8,128)(2,1)} %bitcast.79, bf16[768,1024]{1,0:T(8,128)(2,1)} %copy-done.48, f32[256,1024]{1,0:T(8,128)} %get-tuple-element.637.refs_3_), custom_call_target="tpu_custom_call" | custom-call | flops 1610612736 | bytes 8000000 | tf_op jit(solution)/shard_map/spread/pallas_call | solution.py:1083
  322.8 2.0 collective-permute-start.69
  330.5 9.4 %spread.3 = (bf16[1024,256]{1,0:T(8,128)(2,1)}, bf16[1024,256]{1,0:T(8,128)(2,1)}, bf16[2,1024,256]{2,1,0:T(8,128)(2,1)}) custom-call(s32[10]{0:T(128)S(1)} %pad_add_fusion.info, bf16[384,2048]{1,0:T(8,128)(2,1)} %bitcast.77, bf16[384,2048]{1,0:T(8,128)(2,1)} %bitcast.80, bf16[768,1024]{1,0:T(8,128)(2,1)} %copy-done.48, f32[256,1024]{1,0:T(8,128)} %get-tuple-element.653.refs_3_), custom_call_target="tpu_custom_call" | custom-call | flops 1610612736 | bytes 8000000 | tf_op jit(solution)/shard_map/spread/pallas_call | solution.py:1083
  340.4 5.3 %collective-permute-done.71 = bf16[128,1024]{1,0:T(8,128)(2,1)S(1)} collective-permute-done((bf16[128,1024]{1,0:T(8,128)(2,1)S(1)}, bf16[128,1024]{1,0:T(8,128)(2,1)S(1)}, u32[]{:S(2)}, u32[]{:S(2)}) %collective-permute-start.71) | collective-permute-done | bytes 262176 | tf_op jit(solution)/shard_map/ppermute | solution.py:77
  350.3 1.8 collective-permute-start.78
  352.4 1.7 collective-permute-start.75
  355.7 19.0 %collective-permute-done.74 = bf16[128,1024]{1,0:T(8,128)(2,1)} collective-permute-done((bf16[128,1024]{1,0:T(8,128)(2,1)}, bf16[128,1024]{1,0:T(8,128)(2,1)}, u32[]{:S(2)}, u32[]{:S(2)}) %collective-permute-start.74) | collective-permute-done | bytes 262176 | tf_op jit(solution)/shard_map/ppermute | solution.py:77
  374.7 3.1 collective-permute-done.75
  377.8 1.8 add_convert_fusion.16
  383.6 5.0 %collective-permute-start.79 = (bf16[128,1024]{1,0:T(8,128)(2,1)S(1)}, bf16[128,1024]{1,0:T(8,128)(2,1)S(1)}, u32[]{:S(2)}, u32[]{:S(2)}) collective-permute-start(bf16[128,1024]{1,0:T(8,128)(2,1)S(1)} %add_convert_fusion.16), channel_id=1, source_target_pairs={{0,8},{4,12},{8,0},{12,4},{16,24},{20,28},{24,16},{28,20},{1,9},{5... | collective-permute-start | bytes 786440 | tf_op jit(solution)/shard_map/ppermute | solution.py:77
  390.1 1.9 slice_bitcast_fusion.2
  392.3 4.8 %collective-permute-done.79 = bf16[128,1024]{1,0:T(8,128)(2,1)S(1)} collective-permute-done((bf16[128,1024]{1,0:T(8,128)(2,1)S(1)}, bf16[128,1024]{1,0:T(8,128)(2,1)S(1)}, u32[]{:S(2)}, u32[]{:S(2)}) %collective-permute-start.79) | collective-permute-done | bytes 262176 | tf_op jit(solution)/shard_map/ppermute | solution.py:77
  397.1 9.3 %collective-permute-done.80 = bf16[128,1024]{1,0:T(8,128)(2,1)S(1)} collective-permute-done((bf16[128,1024]{1,0:T(8,128)(2,1)S(1)}, bf16[128,1024]{1,0:T(8,128)(2,1)S(1)}, u32[]{:S(2)}, u32[]{:S(2)}) %collective-permute-start.80) | collective-permute-done | bytes 262176 | tf_op jit(solution)/shard_map/ppermute | solution.py:77
  406.4 4.4 collective-permute-done.81
  414.1 1.7 collective-permute-start.86
  417.1 2.3 assemble.5
  419.4 2.5 settle.1
  422.0 2.3 assemble.3
  424.3 2.1 collective-permute-start.88
  429.1 2.3 assemble.4
  433.3 6.2 %collective-permute-done.86.other_ref = bf16[512,1024]{1,0:T(8,128)(2,1)} collective-permute-done((bf16[512,1024]{1,0:T(8,128)(2,1)}, bf16[512,1024]{1,0:T(8,128)(2,1)}, u32[]{:S(2)}, u32[]{:S(2)}) %collective-permute-start.86) | collective-permute-done | bytes 1048608 | tf_op jit(solution)/shard_map/ppermute | solution.py:77
  439.5 4.8 %assemble_turned.1 = (f32[1024,256]{1,0:T(8,128)}, f32[1024,256]{1,0:T(8,128)}, f32[1024,256]{1,0:T(8,128)}, f32[256,1024]{1,0:T(8,128)}) custom-call(s32[1]{0:T(128)} %bitcast.33.place, s32[10]{0:T(128)S(1)} %pad_add_fusion.info, bf16[512,1024]{1,0:T(8,128)(2,1)} %pad_maximum_fusion.7.own_ref, bf16[512,1024]{1,0:T(8,128)(2,1)} %collective-permute-done.86.other_ref), custom_call_target="tpu_custom_call" | custom-call | bytes 6291456 | tf_op jit(solution)/shard_map/assemble_turned/pallas_call | solution.py:277
  (419 shorter events, 98.6 us)
Async XLA Ops:
  2.1 13.7 %collective-permute-start = (bf16[1024,256]{1,0:T(8,128)(2,1)S(1)}, bf16[1024,256]{1,0:T(8,128)(2,1)S(1)}, u32[]{:S(2)}, u32[]{:S(2)}) collective-permute-start(bf16[1024,256]{1,0:T(8,128)(2,1)S(1)} %get-tuple-element.361.refs_0_.refs_8_), channel_id=1, source_target_pairs={{0,2},{1,3},{2,0},{3,1},{4,6},{5,7},{6,4},{7,5},{8,10},{9,11},{10,... | collective-permute-start | bytes 1572872 | tf_op jit(solution)/shard_map/ppermute | solution.py:77
  18.2 14.8 %collective-permute-start.3 = (bf16[256,512]{1,0:T(8,128)(2,1)S(1)}, bf16[256,512]{1,0:T(8,128)(2,1)S(1)}, u32[]{:S(2)}, u32[]{:S(2)}) collective-permute-start(bf16[256,512]{1,0:T(8,128)(2,1)S(1)} %get-tuple-element.378), channel_id=1, source_target_pairs={{0,2},{1,3},{2,0},{3,1},{4,6},{5,7},{6,4},{7,5},{8,10},{9,11},{10,... | collective-permute-start | bytes 786440 | tf_op jit(solution)/shard_map/ppermute | solution.py:77
  19.7 18.0 %collective-permute-start.4 = (bf16[1024,256]{1,0:T(8,128)(2,1)S(1)}, bf16[1024,256]{1,0:T(8,128)(2,1)}, u32[]{:S(2)}, u32[]{:S(2)}) collective-permute-start(bf16[1024,256]{1,0:T(8,128)(2,1)S(1)} %get-tuple-element.380.refs_0_.refs_8_.refs_4_), channel_id=1, source_target_pairs={{0,2},{1,3},{2,0},{3,1},{4,6},{5,7},{6,4},{7,5},{8,10},{9,11},{10,... | collective-permute-start | bytes 1572872 | tf_op jit(solution)/shard_map/ppermute | solution.py:77
  38.3 19.7 %collective-permute-start.10 = (bf16[2,512,256]{2,1,0:T(8,128)(2,1)}, bf16[2,512,256]{2,1,0:T(8,128)(2,1)S(1)}, u32[]{:S(2)}, u32[]{:S(2)}) collective-permute-start(bf16[2,512,256]{2,1,0:T(8,128)(2,1)} %copy-done.49), channel_id=1, source_target_pairs={{0,2},{1,3},{2,0},{3,1},{4,6},{5,7},{6,4},{7,5},{8,10},{9,11},{10,... | collective-permute-start | bytes 1572872 | tf_op jit(solution)/shard_map/ppermute | solution.py:77
  39.9 16.8 %collective-permute-start.9 = (bf16[512,256]{1,0:T(8,128)(2,1)}, bf16[512,256]{1,0:T(8,128)(2,1)S(1)}, u32[]{:S(2)}, u32[]{:S(2)}) collective-permute-start(bf16[512,256]{1,0:T(8,128)(2,1)} %copy-done.50), channel_id=1, source_target_pairs={{0,1},{1,0},{2,3},{3,2},{4,5},{5,4},{6,7},{7,6},{8,9},{9,8},{10,11... | collective-permute-start | bytes 786440 | tf_op jit(solution)/shard_map/ppermute | solution.py:77
  39.9 16.8 %collective-permute-start.11 = (bf16[256,512]{1,0:T(8,128)(2,1)}, bf16[256,512]{1,0:T(8,128)(2,1)S(1)}, u32[]{:S(2)}, u32[]{:S(2)}) collective-permute-start(bf16[256,512]{1,0:T(8,128)(2,1)} %copy-done.88), channel_id=1, source_target_pairs={{0,4},{4,0},{8,12},{12,8},{16,20},{20,16},{24,28},{28,24},{1,5},{5... | collective-permute-start | bytes 786440 | tf_op jit(solution)/shard_map/ppermute | solution.py:77
  41.4 16.6 %collective-permute-start.8 = (bf16[2,256,256]{2,1,0:T(8,128)(2,1)}, bf16[2,256,256]{2,1,0:T(8,128)(2,1)S(1)}, u32[]{:S(2)}, u32[]{:S(2)}) collective-permute-start(bf16[2,256,256]{2,1,0:T(8,128)(2,1)} %get-tuple-element.404), channel_id=1, source_target_pairs={{0,2},{1,3},{2,0},{3,1},{4,6},{5,7},{6,4},{7,5},{8,10},{9,11},{10,... | collective-permute-start | bytes 786440 | tf_op jit(solution)/shard_map/ppermute | solution.py:77
  41.9 14.2 %collective-permute-start.7 = (bf16[256,256]{1,0:T(8,128)(2,1)}, bf16[256,256]{1,0:T(8,128)(2,1)S(1)}, u32[]{:S(2)}, u32[]{:S(2)}) collective-permute-start(bf16[256,256]{1,0:T(8,128)(2,1)} %get-tuple-element.403), channel_id=1, source_target_pairs={{0,1},{1,0},{2,3},{3,2},{4,5},{5,4},{6,7},{7,6},{8,9},{9,8},{10,11... | collective-permute-start | bytes 393224 | tf_op jit(solution)/shard_map/ppermute | solution.py:77
  58.2 8.9 %collective-permute-start.16 = (bf16[2,256,256]{2,1,0:T(8,128)(2,1)}, bf16[2,256,256]{2,1,0:T(8,128)(2,1)S(1)}, u32[]{:S(2)}, u32[]{:S(2)}) collective-permute-start(bf16[2,256,256]{2,1,0:T(8,128)(2,1)} %get-tuple-element.424), channel_id=1, source_target_pairs={{0,2},{1,3},{2,0},{3,1},{4,6},{5,7},{6,4},{7,5},{8,10},{9,11},{10,... | collective-permute-start | bytes 786440 | tf_op jit(solution)/shard_map/ppermute | solution.py:77
  67.2 13.5 %collective-permute-start.18 = (bf16[256,1024]{1,0:T(8,128)(2,1)S(1)}, bf16[256,1024]{1,0:T(8,128)(2,1)S(1)}, u32[]{:S(2)}, u32[]{:S(2)}) collective-permute-start(bf16[256,1024]{1,0:T(8,128)(2,1)S(1)} %get-tuple-element.438.refs_0_), channel_id=1, source_target_pairs={{0,2},{1,3},{2,0},{3,1},{4,6},{5,7},{6,4},{7,5},{8,10},{9,11},{10,... | collective-permute-start | bytes 1572872 | tf_op jit(solution)/shard_map/ppermute | solution.py:77
  81.2 13.8 %collective-permute-start.21 = (bf16[256,1024]{1,0:T(8,128)(2,1)S(1)}, bf16[256,1024]{1,0:T(8,128)(2,1)S(1)}, u32[]{:S(2)}, u32[]{:S(2)}) collective-permute-start(bf16[256,1024]{1,0:T(8,128)(2,1)S(1)} %get-tuple-element.453.refs_0_), channel_id=1, source_target_pairs={{0,2},{1,3},{2,0},{3,1},{4,6},{5,7},{6,4},{7,5},{8,10},{9,11},{10,... | collective-permute-start | bytes 1572872 | tf_op jit(solution)/shard_map/ppermute | solution.py:77
  95.5 13.8 %collective-permute-start.25 = (bf16[256,1024]{1,0:T(8,128)(2,1)S(1)}, bf16[256,1024]{1,0:T(8,128)(2,1)S(1)}, u32[]{:S(2)}, u32[]{:S(2)}) collective-permute-start(bf16[256,1024]{1,0:T(8,128)(2,1)S(1)} %get-tuple-element.463), channel_id=1, source_target_pairs={{0,1},{1,0},{2,3},{3,2},{4,5},{5,4},{6,7},{7,6},{8,9},{9,8},{10,11... | collective-permute-start | bytes 1572872 | tf_op jit(solution)/shard_map/ppermute | solution.py:77
  97.1 14.0 %collective-permute-start.26 = (bf16[256,1024]{1,0:T(8,128)(2,1)S(1)}, bf16[256,1024]{1,0:T(8,128)(2,1)S(1)}, u32[]{:S(2)}, u32[]{:S(2)}) collective-permute-start(bf16[256,1024]{1,0:T(8,128)(2,1)S(1)} %add_convert_fusion.14), channel_id=1, source_target_pairs={{0,2},{1,3},{2,0},{3,1},{4,6},{5,7},{6,4},{7,5},{8,10},{9,11},{10,... | collective-permute-start | bytes 1572872 | tf_op jit(solution)/shard_map/ppermute | solution.py:77
  111.2 6.9 %collective-permute-start.28 = (bf16[256,1024]{1,0:T(8,128)(2,1)S(1)}, bf16[256,1024]{1,0:T(8,128)(2,1)S(1)}, u32[]{:S(2)}, u32[]{:S(2)}) collective-permute-start(bf16[256,1024]{1,0:T(8,128)(2,1)S(1)} %get-tuple-element.478), channel_id=1, source_target_pairs={{0,1},{1,0},{2,3},{3,2},{4,5},{5,4},{6,7},{7,6},{8,9},{9,8},{10,11... | collective-permute-start | bytes 1572872 | tf_op jit(solution)/shard_map/ppermute | solution.py:77
  111.2 6.9 %collective-permute-start.29 = (bf16[256,1024]{1,0:T(8,128)(2,1)S(1)}, bf16[256,1024]{1,0:T(8,128)(2,1)S(1)}, u32[]{:S(2)}, u32[]{:S(2)}) collective-permute-start(bf16[256,1024]{1,0:T(8,128)(2,1)S(1)} %get-tuple-element.479), channel_id=1, source_target_pairs={{0,1},{1,0},{2,3},{3,2},{4,5},{5,4},{6,7},{7,6},{8,9},{9,8},{10,11... | collective-permute-start | bytes 1572872 | tf_op jit(solution)/shard_map/ppermute | solution.py:77
  118.1 14.0 %collective-permute-start.31 = (bf16[256,1024]{1,0:T(8,128)(2,1)S(1)}, bf16[256,1024]{1,0:T(8,128)(2,1)S(1)}, u32[]{:S(2)}, u32[]{:S(2)}) collective-permute-start(bf16[256,1024]{1,0:T(8,128)(2,1)S(1)} %get-tuple-element.485.refs_0_), channel_id=1, source_target_pairs={{0,2},{1,3},{2,0},{3,1},{4,6},{5,7},{6,4},{7,5},{8,10},{9,11},{10,... | collective-permute-start | bytes 1572872 | tf_op jit(solution)/shard_map/ppermute | solution.py:77
  119.7 14.2 %collective-permute-start.30 = (bf16[256,1024]{1,0:T(8,128)(2,1)S(1)}, bf16[256,1024]{1,0:T(8,128)(2,1)S(1)}, u32[]{:S(2)}, u32[]{:S(2)}) collective-permute-start(bf16[256,1024]{1,0:T(8,128)(2,1)S(1)} %get-tuple-element.485.refs_0_), channel_id=1, source_target_pairs={{0,1},{1,0},{2,3},{3,2},{4,5},{5,4},{6,7},{7,6},{8,9},{9,8},{10,11... | collective-permute-start | bytes 1572872 | tf_op jit(solution)/shard_map/ppermute | solution.py:77
  132.3 27.1 %collective-permute-start.33 = (bf16[256,1024]{1,0:T(8,128)(2,1)S(1)}, bf16[256,1024]{1,0:T(8,128)(2,1)S(1)}, u32[]{:S(2)}, u32[]{:S(2)}) collective-permute-start(bf16[256,1024]{1,0:T(8,128)(2,1)S(1)} %add_convert_fusion.13), channel_id=1, source_target_pairs={{0,2},{1,3},{2,0},{3,1},{4,6},{5,7},{6,4},{7,5},{8,10},{9,11},{10,... | collective-permute-start | bytes 1572872 | tf_op jit(solution)/shard_map/ppermute | solution.py:77
  165.3 14.3 %collective-permute-start.36 = (bf16[256,1024]{1,0:T(8,128)(2,1)}, bf16[256,1024]{1,0:T(8,128)(2,1)S(1)}, u32[]{:S(2)}, u32[]{:S(2)}) collective-permute-start(bf16[256,1024]{1,0:T(8,128)(2,1)} %get-tuple-element.530.refs_0_), channel_id=1, source_target_pairs={{0,2},{1,3},{2,0},{3,1},{4,6},{5,7},{6,4},{7,5},{8,10},{9,11},{10,... | collective-permute-start | bytes 1572872 | tf_op jit(solution)/shard_map/ppermute | solution.py:77
  181.4 21.6 %collective-permute-start.39 = (bf16[256,1024]{1,0:T(8,128)(2,1)S(1)}, bf16[256,1024]{1,0:T(8,128)(2,1)S(1)}, u32[]{:S(2)}, u32[]{:S(2)}) collective-permute-start(bf16[256,1024]{1,0:T(8,128)(2,1)S(1)} %add_convert_fusion.12), channel_id=1, source_target_pairs={{0,2},{1,3},{2,0},{3,1},{4,6},{5,7},{6,4},{7,5},{8,10},{9,11},{10,... | collective-permute-start | bytes 1572872 | tf_op jit(solution)/shard_map/ppermute | solution.py:77
  186.8 26.4 %collective-permute-start.40 = (bf16[512,1024]{1,0:T(8,128)(2,1)S(1)}, bf16[512,1024]{1,0:T(8,128)(2,1)S(1)}, u32[]{:S(2)}, u32[]{:S(2)}) collective-permute-start(bf16[512,1024]{1,0:T(8,128)(2,1)S(1)} %constant_dynamic-slice_fusion.10), channel_id=1, source_target_pairs={{0,4},{4,0},{8,12},{12,8},{16,20},{20,16},{24,28},{28,24},{1,5},{5... | collective-permute-start | bytes 3145736 | tf_op jit(solution)/shard_map/ppermute | solution.py:77
  213.7 13.4 %collective-permute-start.44 = (bf16[256,1024]{1,0:T(8,128)(2,1)S(1)}, bf16[256,1024]{1,0:T(8,128)(2,1)S(1)}, u32[]{:S(2)}, u32[]{:S(2)}) collective-permute-start(bf16[256,1024]{1,0:T(8,128)(2,1)S(1)} %constant_dynamic-slice_fusion.9), channel_id=1, source_target_pairs={{0,8},{4,12},{8,0},{12,4},{16,24},{20,28},{24,16},{28,20},{1,9},{5... | collective-permute-start | bytes 1572872 | tf_op jit(solution)/shard_map/ppermute | solution.py:77
  214.9 12.7 %collective-permute-start.43 = (bf16[256,1024]{1,0:T(8,128)(2,1)S(1)}, bf16[256,1024]{1,0:T(8,128)(2,1)S(1)}, u32[]{:S(2)}, u32[]{:S(2)}) collective-permute-start(bf16[256,1024]{1,0:T(8,128)(2,1)S(1)} %add_convert_fusion.11), channel_id=1, source_target_pairs={{0,2},{1,3},{2,0},{3,1},{4,6},{5,7},{6,4},{7,5},{8,10},{9,11},{10,... | collective-permute-start | bytes 1572872 | tf_op jit(solution)/shard_map/ppermute | solution.py:77
  216.3 27.6 %collective-permute-start.48 = (bf16[512,1024]{1,0:T(8,128)(2,1)S(1)}, bf16[512,1024]{1,0:T(8,128)(2,1)S(1)}, u32[]{:S(2)}, u32[]{:S(2)}) collective-permute-start(bf16[512,1024]{1,0:T(8,128)(2,1)S(1)} %constant_dynamic-slice_fusion.8), channel_id=1, source_target_pairs={{0,4},{4,0},{8,12},{12,8},{16,20},{20,16},{24,28},{28,24},{1,5},{5... | collective-permute-start | bytes 3145736 | tf_op jit(solution)/shard_map/ppermute | solution.py:77
  227.6 8.8 %collective-permute-start.46 = (bf16[2,256,256]{2,1,0:T(8,128)(2,1)S(1)}, bf16[2,256,256]{2,1,0:T(8,128)(2,1)S(1)}, u32[]{:S(2)}, u32[]{:S(2)}) collective-permute-start(bf16[2,256,256]{2,1,0:T(8,128)(2,1)S(1)} %get-tuple-element.589), channel_id=1, source_target_pairs={{0,2},{1,3},{2,0},{3,1},{4,6},{5,7},{6,4},{7,5},{8,10},{9,11},{10,... | collective-permute-start | bytes 786440 | tf_op jit(solution)/shard_map/ppermute | solution.py:77
  229.1 7.3 %collective-permute-start.45 = (bf16[256,256]{1,0:T(8,128)(2,1)S(1)}, bf16[256,256]{1,0:T(8,128)(2,1)S(1)}, u32[]{:S(2)}, u32[]{:S(2)}) collective-permute-start(bf16[256,256]{1,0:T(8,128)(2,1)S(1)} %get-tuple-element.588), channel_id=1, source_target_pairs={{0,1},{1,0},{2,3},{3,2},{4,5},{5,4},{6,7},{7,6},{8,9},{9,8},{10,11... | collective-permute-start | bytes 393224 | tf_op jit(solution)/shard_map/ppermute | solution.py:77
  229.3 14.5 %collective-permute-start.47 = (bf16[128,1024]{1,0:T(8,128)(2,1)S(1)}, bf16[128,1024]{1,0:T(8,128)(2,1)S(1)}, u32[]{:S(2)}, u32[]{:S(2)}) collective-permute-start(bf16[128,1024]{1,0:T(8,128)(2,1)S(1)} %constant_dynamic-slice_fusion.7), channel_id=1, source_target_pairs={{0,16},{4,20},{8,24},{12,28},{16,0},{20,4},{24,8},{28,12},{1,17},{... | collective-permute-start | bytes 786440 | tf_op jit(solution)/shard_map/ppermute | solution.py:77
  236.4 8.5 %collective-permute-start.50 = (bf16[2,256,256]{2,1,0:T(8,128)(2,1)S(1)}, bf16[2,256,256]{2,1,0:T(8,128)(2,1)S(1)}, u32[]{:S(2)}, u32[]{:S(2)}) collective-permute-start(bf16[2,256,256]{2,1,0:T(8,128)(2,1)S(1)} %get-tuple-element.593), channel_id=1, source_target_pairs={{0,2},{1,3},{2,0},{3,1},{4,6},{5,7},{6,4},{7,5},{8,10},{9,11},{10,... | collective-permute-start | bytes 786440 | tf_op jit(solution)/shard_map/ppermute | solution.py:77
  237.1 11.4 %collective-permute-start.51 = (bf16[256,256]{1,0:T(8,128)(2,1)S(1)}, bf16[256,256]{1,0:T(8,128)(2,1)S(1)}, u32[]{:S(2)}, u32[]{:S(2)}) collective-permute-start(bf16[256,256]{1,0:T(8,128)(2,1)S(1)} %get-tuple-element.722), channel_id=1, source_target_pairs={{0,1},{1,0},{2,3},{3,2},{4,5},{5,4},{6,7},{7,6},{8,9},{9,8},{10,11... | collective-permute-start | bytes 393224 | tf_op jit(solution)/shard_map/ppermute | solution.py:77
  245.3 21.8 %collective-permute-start.55 = (bf16[272,1024]{1,0:T(8,128)(2,1)S(1)}, bf16[272,1024]{1,0:T(8,128)(2,1)S(1)}, u32[]{:S(2)}, u32[]{:S(2)}) collective-permute-start(bf16[272,1024]{1,0:T(8,128)(2,1)S(1)} %get-tuple-element.732), channel_id=1, source_target_pairs={{0,1},{1,0},{2,3},{3,2},{4,5},{5,4},{6,7},{7,6},{8,9},{9,8},{10,11... | collective-permute-start | bytes 1671176 | tf_op jit(solution)/shard_map/ppermute | solution.py:77
  245.3 21.7 %collective-permute-start.56 = (bf16[272,1024]{1,0:T(8,128)(2,1)S(1)}, bf16[272,1024]{1,0:T(8,128)(2,1)S(1)}, u32[]{:S(2)}, u32[]{:S(2)}) collective-permute-start(bf16[272,1024]{1,0:T(8,128)(2,1)S(1)} %get-tuple-element.731), channel_id=1, source_target_pairs={{0,1},{1,0},{2,3},{3,2},{4,5},{5,4},{6,7},{7,6},{8,9},{9,8},{10,11... | collective-permute-start | bytes 1671176 | tf_op jit(solution)/shard_map/ppermute | solution.py:77
  246.5 20.5 %collective-permute-start.54 = (bf16[256,1024]{1,0:T(8,128)(2,1)S(1)}, bf16[256,1024]{1,0:T(8,128)(2,1)S(1)}, u32[]{:S(2)}, u32[]{:S(2)}) collective-permute-start(bf16[256,1024]{1,0:T(8,128)(2,1)S(1)} %constant_dynamic-slice_fusion.6), channel_id=1, source_target_pairs={{0,8},{4,12},{8,0},{12,4},{16,24},{20,28},{24,16},{28,20},{1,9},{5... | collective-permute-start | bytes 1572872 | tf_op jit(solution)/shard_map/ppermute | solution.py:77
  248.5 18.6 %collective-permute-start.53 = (bf16[128,1024]{1,0:T(8,128)(2,1)S(1)}, bf16[128,1024]{1,0:T(8,128)(2,1)S(1)}, u32[]{:S(2)}, u32[]{:S(2)}) collective-permute-start(bf16[128,1024]{1,0:T(8,128)(2,1)S(1)} %add_convert_fusion.19), channel_id=1, source_target_pairs={{0,16},{4,20},{8,24},{12,28},{16,0},{20,4},{24,8},{28,12},{1,17},{... | collective-permute-start | bytes 786440 | tf_op jit(solution)/shard_map/ppermute | solution.py:77
  249.3 25.7 %collective-permute-start.57 = (bf16[512,1024]{1,0:T(8,128)(2,1)S(1)}, bf16[512,1024]{1,0:T(8,128)(2,1)S(1)}, u32[]{:S(2)}, u32[]{:S(2)}) collective-permute-start(bf16[512,1024]{1,0:T(8,128)(2,1)S(1)} %constant_dynamic-slice_fusion.5), channel_id=1, source_target_pairs={{0,4},{4,0},{8,12},{12,8},{16,20},{20,16},{24,28},{28,24},{1,5},{5... | collective-permute-start | bytes 3145736 | tf_op jit(solution)/shard_map/ppermute | solution.py:77
  267.3 24.4 %collective-permute-start.61 = (bf16[272,1024]{1,0:T(8,128)(2,1)S(1)}, bf16[272,1024]{1,0:T(8,128)(2,1)S(1)}, u32[]{:S(2)}, u32[]{:S(2)}) collective-permute-start(bf16[272,1024]{1,0:T(8,128)(2,1)S(1)} %add_convert_fusion.7), channel_id=1, source_target_pairs={{0,2},{1,3},{2,0},{3,1},{4,6},{5,7},{6,4},{7,5},{8,10},{9,11},{10,... | collective-permute-start | bytes 1671176 | tf_op jit(solution)/shard_map/ppermute | solution.py:77
  268.2 23.5 %collective-permute-start.59 = (bf16[128,1024]{1,0:T(8,128)(2,1)S(1)}, bf16[128,1024]{1,0:T(8,128)(2,1)S(1)}, u32[]{:S(2)}, u32[]{:S(2)}) collective-permute-start(bf16[128,1024]{1,0:T(8,128)(2,1)S(1)} %constant_dynamic-slice_fusion.4), channel_id=1, source_target_pairs={{0,16},{4,20},{8,24},{12,28},{16,0},{20,4},{24,8},{28,12},{1,17},{... | collective-permute-start | bytes 786440 | tf_op jit(solution)/shard_map/ppermute | solution.py:77
  270.0 21.6 %collective-permute-start.58 = (bf16[256,1024]{1,0:T(8,128)(2,1)S(1)}, bf16[256,1024]{1,0:T(8,128)(2,1)S(1)}, u32[]{:S(2)}, u32[]{:S(2)}) collective-permute-start(bf16[256,1024]{1,0:T(8,128)(2,1)S(1)} %pad_maximum_fusion.8), channel_id=1, source_target_pairs={{0,8},{4,12},{8,0},{12,4},{16,24},{20,28},{24,16},{28,20},{1,9},{5... | collective-permute-start | bytes 1572872 | tf_op jit(solution)/shard_map/ppermute | solution.py:77
  275.9 15.7 %collective-permute-start.60 = (bf16[192,1024]{1,0:T(8,128)(2,1)S(1)}, bf16[192,1024]{1,0:T(8,128)(2,1)S(1)}, u32[]{:S(2)}, u32[]{:S(2)}) collective-permute-start(bf16[192,1024]{1,0:T(8,128)(2,1)S(1)} %constant_dynamic-slice_fusion.2), channel_id=1, source_target_pairs={{0,4},{4,0},{8,12},{12,8},{16,20},{20,16},{24,28},{28,24},{1,5},{5... | collective-permute-start | bytes 1179656 | tf_op jit(solution)/shard_map/ppermute | solution.py:77
  276.2 25.7 %collective-permute-start.62 = (bf16[256,1024]{1,0:T(8,128)(2,1)S(1)}, bf16[256,1024]{1,0:T(8,128)(2,1)S(1)}, u32[]{:S(2)}, u32[]{:S(2)}) collective-permute-start(bf16[256,1024]{1,0:T(8,128)(2,1)S(1)} %constant_dynamic-slice_fusion.3), channel_id=1, source_target_pairs={{0,8},{4,12},{8,0},{12,4},{16,24},{20,28},{24,16},{28,20},{1,9},{5... | collective-permute-start | bytes 1572872 | tf_op jit(solution)/shard_map/ppermute | solution.py:77
  291.8 28.0 %collective-permute-start.65 = (bf16[512,1024]{1,0:T(8,128)(2,1)S(1)}, bf16[512,1024]{1,0:T(8,128)(2,1)S(1)}, u32[]{:S(2)}, u32[]{:S(2)}) collective-permute-start(bf16[512,1024]{1,0:T(8,128)(2,1)S(1)} %pad_maximum_fusion.4.own_ref), channel_id=1, source_target_pairs={{0,4},{4,0},{8,12},{12,8},{16,20},{20,16},{24,28},{28,24},{1,5},{5... | collective-permute-start | bytes 3145736 | tf_op jit(solution)/shard_map/ppermute | solution.py:77
  295.1 24.0 %collective-permute-start.63 = (bf16[128,1024]{1,0:T(8,128)(2,1)S(1)}, bf16[128,1024]{1,0:T(8,128)(2,1)}, u32[]{:S(2)}, u32[]{:S(2)}) collective-permute-start(bf16[128,1024]{1,0:T(8,128)(2,1)S(1)} %add_convert_fusion.18), channel_id=1, source_target_pairs={{0,16},{4,20},{8,24},{12,28},{16,0},{20,4},{24,8},{28,12},{1,17},{... | collective-permute-start | bytes 786440 | tf_op jit(solution)/shard_map/ppermute | solution.py:77
  301.9 17.9 %collective-permute-start.67 = (bf16[2,512,256]{2,1,0:T(8,128)(2,1)S(1)}, bf16[2,512,256]{2,1,0:T(8,128)(2,1)S(1)}, u32[]{:S(2)}, u32[]{:S(2)}) collective-permute-start(bf16[2,512,256]{2,1,0:T(8,128)(2,1)S(1)} %copy-done.83), channel_id=1, source_target_pairs={{0,2},{1,3},{2,0},{3,1},{4,6},{5,7},{6,4},{7,5},{8,10},{9,11},{10,... | collective-permute-start | bytes 1572872 | tf_op jit(solution)/shard_map/ppermute | solution.py:77
  303.0 16.1 %collective-permute-start.66 = (bf16[512,256]{1,0:T(8,128)(2,1)S(1)}, bf16[512,256]{1,0:T(8,128)(2,1)S(1)}, u32[]{:S(2)}, u32[]{:S(2)}) collective-permute-start(bf16[512,256]{1,0:T(8,128)(2,1)S(1)} %copy-done.87), channel_id=1, source_target_pairs={{0,1},{1,0},{2,3},{3,2},{4,5},{5,4},{6,7},{7,6},{8,9},{9,8},{10,11... | collective-permute-start | bytes 786440 | tf_op jit(solution)/shard_map/ppermute | solution.py:77
  303.2 16.6 %collective-permute-start.64 = (bf16[128,1024]{1,0:T(8,128)(2,1)S(1)}, bf16[128,1024]{1,0:T(8,128)(2,1)S(1)}, u32[]{:S(2)}, u32[]{:S(2)}) collective-permute-start(bf16[128,1024]{1,0:T(8,128)(2,1)S(1)} %constant_dynamic-slice_fusion.1), channel_id=1, source_target_pairs={{0,16},{4,20},{8,24},{12,28},{16,0},{20,4},{24,8},{28,12},{1,17},{... | collective-permute-start | bytes 786440 | tf_op jit(solution)/shard_map/ppermute | solution.py:77
  321.5 24.3 %collective-permute-start.72 = (bf16[2,1024,256]{2,1,0:T(8,128)(2,1)}, bf16[2,1024,256]{2,1,0:T(8,128)(2,1)}, u32[]{:S(2)}, u32[]{:S(2)}) collective-permute-start(bf16[2,1024,256]{2,1,0:T(8,128)(2,1)} %get-tuple-element.657), channel_id=1, source_target_pairs={{0,1},{1,0},{2,3},{3,2},{4,5},{5,4},{6,7},{7,6},{8,9},{9,8},{10,11... | collective-permute-start | bytes 3145736 | tf_op jit(solution)/shard_map/ppermute | solution.py:77
  322.7 17.1 %collective-permute-start.73 = (f32[5,1024]{1,0:T(8,128)S(1)}, f32[5,1024]{1,0:T(8,128)S(1)}, u32[]{:S(2)}, u32[]{:S(2)}) collective-permute-start(f32[5,1024]{1,0:T(8,128)S(1)} %select_maximum_fusion), channel_id=1, source_target_pairs={{0,4},{4,0},{8,12},{12,8},{16,20},{20,16},{24,28},{28,24},{1,5},{5... | collective-permute-start | bytes 61448 | tf_op jit(solution)/shard_map/ppermute | solution.py:77
  322.8 17.6 %collective-permute-start.69 = (bf16[320,1024]{1,0:T(8,128)(2,1)}, bf16[320,1024]{1,0:T(8,128)(2,1)S(1)}, u32[]{:S(2)}, u32[]{:S(2)}) collective-permute-start(bf16[320,1024]{1,0:T(8,128)(2,1)} %fusion.4), channel_id=1, source_target_pairs={{0,4},{4,0},{8,12},{12,8},{16,20},{20,16},{24,28},{28,24},{1,5},{5... | collective-permute-start | bytes 1966088 | tf_op jit(solution)/shard_map/ppermute | solution.py:77
  325.8 19.9 %collective-permute-start.70 = (bf16[256,1024]{1,0:T(8,128)(2,1)S(1)}, bf16[256,1024]{1,0:T(8,128)(2,1)S(1)}, u32[]{:S(2)}, u32[]{:S(2)}) collective-permute-start(bf16[256,1024]{1,0:T(8,128)(2,1)S(1)} %pad_maximum_fusion.9), channel_id=1, source_target_pairs={{0,8},{4,12},{8,0},{12,4},{16,24},{20,28},{24,16},{28,20},{1,9},{5... | collective-permute-start | bytes 1572872 | tf_op jit(solution)/shard_map/ppermute | solution.py:77
  327.9 17.8 %collective-permute-start.71 = (bf16[128,1024]{1,0:T(8,128)(2,1)S(1)}, bf16[128,1024]{1,0:T(8,128)(2,1)S(1)}, u32[]{:S(2)}, u32[]{:S(2)}) collective-permute-start(bf16[128,1024]{1,0:T(8,128)(2,1)S(1)} %add_convert_fusion.17), channel_id=1, source_target_pairs={{0,16},{4,20},{8,24},{12,28},{16,0},{20,4},{24,8},{28,12},{1,17},{... | collective-permute-start | bytes 786440 | tf_op jit(solution)/shard_map/ppermute | solution.py:77
  349.1 28.7 %collective-permute-start.77 = (bf16[512,1024]{1,0:T(8,128)(2,1)S(1)}, bf16[512,1024]{1,0:T(8,128)(2,1)S(1)}, u32[]{:S(2)}, u32[]{:S(2)}) collective-permute-start(bf16[512,1024]{1,0:T(8,128)(2,1)S(1)} %pad_maximum_fusion.5.own_ref), channel_id=1, source_target_pairs={{0,4},{4,0},{8,12},{12,8},{16,20},{20,16},{24,28},{28,24},{1,5},{5... | collective-permute-start | bytes 3145736 | tf_op jit(solution)/shard_map/ppermute | solution.py:77
  350.3 27.4 %collective-permute-start.78 = (bf16[256,1024]{1,0:T(8,128)(2,1)}, bf16[256,1024]{1,0:T(8,128)(2,1)}, u32[]{:S(2)}, u32[]{:S(2)}) collective-permute-start(bf16[256,1024]{1,0:T(8,128)(2,1)} %pad_maximum_fusion.10), channel_id=1, source_target_pairs={{0,8},{4,12},{8,0},{12,4},{16,24},{20,28},{24,16},{28,20},{1,9},{5... | collective-permute-start | bytes 1572872 | tf_op jit(solution)/shard_map/ppermute | solution.py:77
  352.2 22.5 %collective-permute-start.74 = (bf16[128,1024]{1,0:T(8,128)(2,1)}, bf16[128,1024]{1,0:T(8,128)(2,1)}, u32[]{:S(2)}, u32[]{:S(2)}) collective-permute-start(bf16[128,1024]{1,0:T(8,128)(2,1)} %get-tuple-element.712), channel_id=1, source_target_pairs={{0,8},{4,12},{8,0},{12,4},{16,24},{20,28},{24,16},{28,20},{1,9},{5... | collective-permute-start | bytes 786440 | tf_op jit(solution)/shard_map/ppermute | solution.py:77
  352.4 25.4 %collective-permute-start.75 = (bf16[128,1024]{1,0:T(8,128)(2,1)}, bf16[128,1024]{1,0:T(8,128)(2,1)}, u32[]{:S(2)}, u32[]{:S(2)}) collective-permute-start(bf16[128,1024]{1,0:T(8,128)(2,1)} %get-tuple-element.713), channel_id=1, source_target_pairs={{0,16},{4,20},{8,24},{12,28},{16,0},{20,4},{24,8},{28,12},{1,17},{... | collective-permute-start | bytes 786440 | tf_op jit(solution)/shard_map/ppermute | solution.py:77
  354.1 23.7 %collective-permute-start.76 = (bf16[128,1024]{1,0:T(8,128)(2,1)}, bf16[128,1024]{1,0:T(8,128)(2,1)}, u32[]{:S(2)}, u32[]{:S(2)}) collective-permute-start(bf16[128,1024]{1,0:T(8,128)(2,1)} %get-tuple-element.711), channel_id=1, source_target_pairs={{0,24},{4,28},{8,16},{12,20},{16,8},{20,12},{24,0},{28,4},{1,25},{... | collective-permute-start | bytes 786440 | tf_op jit(solution)/shard_map/ppermute | solution.py:77
  380.8 30.1 %collective-permute-start.82 = (bf16[512,1024]{1,0:T(8,128)(2,1)S(1)}, bf16[512,1024]{1,0:T(8,128)(2,1)S(1)}, u32[]{:S(2)}, u32[]{:S(2)}) collective-permute-start(bf16[512,1024]{1,0:T(8,128)(2,1)S(1)} %pad_maximum_fusion.6.own_ref), channel_id=1, source_target_pairs={{0,4},{4,0},{8,12},{12,8},{16,20},{20,16},{24,28},{28,24},{1,5},{5... | collective-permute-start | bytes 3145736 | tf_op jit(solution)/shard_map/ppermute | solution.py:77
  382.9 9.4 %collective-permute-start.83 = (bf16[1024,256]{1,0:T(8,128)(2,1)S(1)}, bf16[1024,256]{1,0:T(8,128)(2,1)S(1)}, u32[]{:S(2)}, u32[]{:S(2)}) collective-permute-start(bf16[1024,256]{1,0:T(8,128)(2,1)S(1)} %fusion.2), channel_id=1, source_target_pairs={{0,2},{1,3},{2,0},{3,1},{4,6},{5,7},{6,4},{7,5},{8,10},{9,11},{10,... | collective-permute-start | bytes 1572872 | tf_op jit(solution)/shard_map/ppermute | solution.py:77
  383.6 13.6 %collective-permute-start.79 = (bf16[128,1024]{1,0:T(8,128)(2,1)S(1)}, bf16[128,1024]{1,0:T(8,128)(2,1)S(1)}, u32[]{:S(2)}, u32[]{:S(2)}) collective-permute-start(bf16[128,1024]{1,0:T(8,128)(2,1)S(1)} %add_convert_fusion.16), channel_id=1, source_target_pairs={{0,8},{4,12},{8,0},{12,4},{16,24},{20,28},{24,16},{28,20},{1,9},{5... | collective-permute-start | bytes 786440 | tf_op jit(solution)/shard_map/ppermute | solution.py:77
  388.6 17.9 %collective-permute-start.80 = (bf16[128,1024]{1,0:T(8,128)(2,1)S(1)}, bf16[128,1024]{1,0:T(8,128)(2,1)S(1)}, u32[]{:S(2)}, u32[]{:S(2)}) collective-permute-start(bf16[128,1024]{1,0:T(8,128)(2,1)S(1)} %add_convert_fusion.16), channel_id=1, source_target_pairs={{0,16},{4,20},{8,24},{12,28},{16,0},{20,4},{24,8},{28,12},{1,17},{... | collective-permute-start | bytes 786440 | tf_op jit(solution)/shard_map/ppermute | solution.py:77
  389.3 21.5 %collective-permute-start.81 = (bf16[128,1024]{1,0:T(8,128)(2,1)S(1)}, bf16[128,1024]{1,0:T(8,128)(2,1)S(1)}, u32[]{:S(2)}, u32[]{:S(2)}) collective-permute-start(bf16[128,1024]{1,0:T(8,128)(2,1)S(1)} %add_convert_fusion.16), channel_id=1, source_target_pairs={{0,24},{4,28},{8,16},{12,20},{16,8},{20,12},{24,0},{28,4},{1,25},{... | collective-permute-start | bytes 786440 | tf_op jit(solution)/shard_map/ppermute | solution.py:77
  412.8 13.5 %collective-permute-start.84 = (bf16[2,1024,256]{2,1,0:T(8,128)(2,1)}, bf16[2,1024,256]{2,1,0:T(8,128)(2,1)}, u32[]{:S(2)}, u32[]{:S(2)}) collective-permute-start(bf16[2,1024,256]{2,1,0:T(8,128)(2,1)} %get-tuple-element.687), channel_id=1, source_target_pairs={{0,1},{1,0},{2,3},{3,2},{4,5},{5,4},{6,7},{7,6},{8,9},{9,8},{10,11... | collective-permute-start | bytes 3145736 | tf_op jit(solution)/shard_map/ppermute | solution.py:77
  414.1 25.4 %collective-permute-start.86 = (bf16[512,1024]{1,0:T(8,128)(2,1)}, bf16[512,1024]{1,0:T(8,128)(2,1)}, u32[]{:S(2)}, u32[]{:S(2)}) collective-permute-start(bf16[512,1024]{1,0:T(8,128)(2,1)} %pad_maximum_fusion.7.own_ref), channel_id=1, source_target_pairs={{0,4},{4,0},{8,12},{12,8},{16,20},{20,16},{24,28},{28,24},{1,5},{5... | collective-permute-start | bytes 3145736 | tf_op jit(solution)/shard_map/ppermute | solution.py:77
  415.8 8.5 %collective-permute-start.87 = (f32[5,1024]{1,0:T(8,128)S(1)}, f32[5,1024]{1,0:T(8,128)S(1)}, u32[]{:S(2)}, u32[]{:S(2)}) collective-permute-start(f32[5,1024]{1,0:T(8,128)S(1)} %fusion.21), channel_id=1, source_target_pairs={{0,8},{4,12},{8,0},{12,4},{16,24},{20,28},{24,16},{28,20},{1,9},{5... | collective-permute-start | bytes 61448 | tf_op jit(solution)/shard_map/ppermute | solution.py:77
  424.3 7.1 %collective-permute-start.88 = (f32[5,1024]{1,0:T(8,128)S(1)}, f32[5,1024]{1,0:T(8,128)S(1)}, u32[]{:S(2)}, u32[]{:S(2)}) collective-permute-start(f32[5,1024]{1,0:T(8,128)S(1)} %add.262), channel_id=1, source_target_pairs={{0,16},{4,20},{8,24},{12,28},{16,0},{20,4},{24,8},{28,12},{1,17},{... | collective-permute-start | bytes 61448 | tf_op jit(solution)/shard_map/ppermute | solution.py:77
  427.6 16.7 %collective-permute-start.85 = (bf16[1024,256]{1,0:T(8,128)(2,1)S(1)}, bf16[1024,256]{1,0:T(8,128)(2,1)S(1)}, u32[]{:S(2)}, u32[]{:S(2)}) collective-permute-start(bf16[1024,256]{1,0:T(8,128)(2,1)S(1)} %fusion), channel_id=1, source_target_pairs={{0,2},{1,3},{2,0},{3,1},{4,6},{5,7},{6,4},{7,5},{8,10},{9,11},{10,... | collective-permute-start | bytes 1572872 | tf_op jit(solution)/shard_map/ppermute | solution.py:77
  (123 other events, 975.1 us)
